TPU v7x, 768 devices: a whole 4x8x12 slice. The times are simulated.
768 devices in a mesh: blk: 96 (over x, z, core), rep: 8 (over y).
Axes of the slice: x: 4, y: 8, z: 12, core: 2. Of those that a mesh axis runs over, the one named last changes fastest.
Arguments:
- grad_out: bfloat16 [12288, 1024], P('blk'), may hold values from -6 to 6
- agg_hidden: bfloat16 [12288, 1024], P('blk', 'rep'), may hold values from -6 to 6
- pre_hidden: bfloat16 [12288, 1024], P('blk', 'rep'), may hold values from -6 to 6
- agg_input: bfloat16 [12288, 512], P('blk'), may hold values from -6 to 6
- weight_in: bfloat16 [512, 1024], P(None, 'rep'), may hold values from -0.25 to 0.25
- weight_out: bfloat16 [1024, 1024], P('rep'), may hold values from -0.1875 to 0.1875
- edge_tiles: bfloat16 [96, 64, 128, 128], P('blk'), may hold values from -0.5 to 0.5
- tile_source: int32 [96, 64], P('blk'), may hold values from 0 to 95, as said below
- tile_count: int32 [96], P('blk'), may hold values from 1 to 64, as said below
- degree: int32 [12288], P('blk'), may hold values from 1 to 16
Outputs:
- grad_w_out: float32 [1024, 1024], P('rep')
- grad_w_in: float32 [512, 1024], P(None, 'rep')
- grad_input: float32 [12288, 512], P('blk')
Inputs may be any that keep to these rules, and one draw needn't show every extreme that they name: `tile_source`: within one row block's list the 64 entries are distinct; slots at or after tile_count are ignored. `tile_count`: some row block has all 64 slots live.
All inputs are finite; a program needn't handle non-finite values.
Results may differ from a plain program's by a relative error of at most 0.011.
Values may be sent and summed in bfloat16 or wider, within the bound.
No kernel may reach another device: no remote copies, remote signals or barrier semaphores. Data moves between devices by JAX's collectives and lax.ppermute only.
A program may use at most 32 MiB of HBM per device.

v0:
```python
import jax
import jax.numpy as jnp
from jax import lax
from jax.sharding import PartitionSpec as P


def apply_tiles(gathered, edge_tiles, tile_source, tile_count):
    tile_rows = edge_tiles.shape[2]
    capacity = edge_tiles.shape[1]
    blocks = gathered.reshape(-1, tile_rows, gathered.shape[1])
    active = jnp.arange(capacity, dtype=jnp.int32) < tile_count[0]
    masked = jnp.where(active[:, None, None], edge_tiles[0], jnp.zeros_like(edge_tiles[0]))
    picked = jnp.take(blocks, tile_source[0], axis=0)
    return jnp.einsum("tij,tjk->ik", masked, picked, preferred_element_type=jnp.float32)


def local(
    grad_out,
    agg_hidden,
    pre_hidden,
    agg_input,
    weight_in,
    weight_out,
    edge_tiles,
    tile_source,
    tile_count,
    degree,
):
    inv_root = (1.0 / jnp.sqrt(degree.astype(jnp.float32)))[:, None]
    partial_out = lax.dot_general(
        agg_hidden, grad_out, (((0,), (0,)), ((), ())), preferred_element_type=jnp.float32
    )
    delta_agg = lax.dot_general(
        grad_out, weight_out, (((1,), (1,)), ((), ())), preferred_element_type=jnp.float32
    )
    scaled_out = (inv_root * delta_agg).astype(jnp.bfloat16)
    gathered = lax.all_gather(scaled_out, "blk", axis=0, tiled=True)
    summed_out = apply_tiles(gathered, edge_tiles, tile_source, tile_count)
    grad_hidden = inv_root * summed_out
    grad_pre = jnp.where(pre_hidden > 0, grad_hidden, jnp.zeros((), jnp.float32)).astype(
        jnp.bfloat16
    )
    scaled_pre = (inv_root * grad_pre.astype(jnp.float32)).astype(jnp.bfloat16)
    partial_in = lax.dot_general(
        agg_input, grad_pre, (((0,), (0,)), ((), ())), preferred_element_type=jnp.float32
    )
    gathered_pre = lax.all_gather(scaled_pre, "blk", axis=0, tiled=True)
    summed_pre = apply_tiles(gathered_pre, edge_tiles, tile_source, tile_count)
    spread = (inv_root * summed_pre).astype(jnp.bfloat16)
    partial_input = lax.dot_general(
        spread, weight_in, (((1,), (1,)), ((), ())), preferred_element_type=jnp.float32
    )
    grad_input = lax.psum(partial_input, "rep")
    grad_w_out, grad_w_in = lax.psum((partial_out, partial_in), "blk")
    return (grad_w_out, grad_w_in, grad_input)


def solution(mesh):
    return jax.shard_map(
        local,
        mesh=mesh,
        in_specs=(
            P("blk", None),
            P("blk", "rep"),
            P("blk", "rep"),
            P("blk", None),
            P(None, "rep"),
            P("rep", None),
            P("blk", None, None, None),
            P("blk", None),
            P("blk"),
            P("blk"),
        ),
        out_specs=(P("rep", None), P(None, "rep"), P("blk", None)),
        check_vma=False,
    )
```

profile of v0, /device:TPU:1, one launch (start us, length us, event | category | flops | bytes accessed | tf_op | source)
XLA Modules:
  0.0 621.1 jit_solution(1272716070444200692)
XLA Ops:
  7.2 0.0 copy-start
  7.2 0.0 all-gather.3.cloned.1.call-start
  7.2 0.7 convert_rsqrt_fusion
  7.9 0.2 copy-done
  8.1 1.8 fusion.24
  9.9 0.0 all-gather.3.cloned.1.call-update
  9.9 0.0 all-gather.5.cloned.1.call-start
  10.6 0.7 compare_select_fusion
  11.3 0.7 compare_and_fusion
  12.0 125.1 %all-gather.3.cloned.1.call-done = bf16[12288,128]{1,0:T(8,128)(2,1)} async-done(((bf16[128,128]{1,0:T(8,128)(2,1)}), bf16[12288,128]{1,0:T(8,128)(2,1)}) %all-gather.3.cloned.1.call-update) | async-done | bytes 3145744 | tf_op jit(solution)/shard_map/all_gather | solution.py:37
  137.1 0.0 copy-start.4
  137.1 2.8 gather_fusion
  140.0 0.0 copy-done.4
  140.0 0.0 copy-start.2
  140.0 0.0 copy-start.1
  140.0 3.0 multiply_convert_fusion
  143.0 0.0 all-gather.5.cloned.1.call-update
  143.1 0.0 all-reduce.6.cloned.1.call-start
  143.1 0.0 copy-done.2
  143.1 1.0 fusion.41
  144.2 0.0 copy-done.1
  144.2 0.9 convolution_bitcast_fusion
  145.1 0.0 all-reduce.6.cloned.1.call-update
  145.1 0.0 all-reduce.4.cloned.1.call-start
  145.2 111.3 %all-gather.5.cloned.1.call-done = bf16[12288,128]{1,0:T(8,128)(2,1)} async-done(((bf16[128,128]{1,0:T(8,128)(2,1)}), bf16[12288,128]{1,0:T(8,128)(2,1)}) %all-gather.5.cloned.1.call-update) | async-done | bytes 3145744 | tf_op jit(solution)/shard_map/all_gather | solution.py:47
  256.5 0.0 copy-start.3
  256.5 2.9 gather_fusion.1
  259.4 0.0 copy-done.3
  259.4 3.2 fusion.22
  262.6 0.0 all-reduce.4.cloned.1.call-update
  262.6 268.0 %all-reduce.6.cloned.1.call-done = (f32[128,1024]{1,0:T(8,128)}, f32[512,128]{0,1:T(8,128)}) async-done(((f32[128,1024]{1,0:T(8,128)}, f32[512,128]{0,1:T(8,128)}), (f32[128,1024]{1,0:T(8,128)}, f32[512,128]{0,1:T(8,128)})) %all-reduce.6.cloned.1.call-update) | async-done | bytes 786448 | tf_op jit(solution)/shard_map/psum | solution.py:54
  530.6 1.8 copy.13
  532.4 78.6 %all-reduce.4.cloned.1.call-done = f32[128,512]{1,0:T(8,128)} async-done(((f32[128,512]{1,0:T(8,128)}), f32[128,512]{1,0:T(8,128)}) %all-reduce.4.cloned.1.call-update) | async-done | bytes 262160 | tf_op jit(solution)/shard_map/psum | solution.py:53
  611.0 1.9 copy.18
  612.9 1.7 copy.19
  (1 shorter events, 0.0 us)
Async XLA Ops:
  7.2 1.0 copy-start
  7.2 129.9 %all-gather.3.cloned.1.call-start = ((), (), s32[]{:S(2)}) async-start(), calls=%async_computation | async-start | bytes 3178496 | tf_op jit(solution)/shard_map/all_gather | solution.py:37
  9.9 246.5 %all-gather.5.cloned.1.call-start = ((), (), s32[]{:S(2)}) async-start(), calls=%async_computation.1 | async-start | bytes 3178496 | tf_op jit(solution)/shard_map/all_gather | solution.py:47
  137.1 2.9 copy-start.4
  140.0 3.1 copy-start.2
  140.0 4.2 copy-start.1
  143.1 387.6 %all-reduce.6.cloned.1.call-start = ((), (), s32[]{:S(2)}) async-start(), calls=%async_computation.3 | async-start | bytes 1572864 | tf_op jit(solution)/shard_map/psum | solution.py:54
  145.1 465.9 %all-reduce.4.cloned.1.call-start = ((), (), s32[]{:S(2)}) async-start(), calls=%async_computation.2 | async-start | bytes 524288 | tf_op jit(solution)/shard_map/psum | solution.py:53
  256.5 2.9 copy-start.3
Sparse Core Ops, SparseCore 0:
  12.3 124.8 all-gather.2
  143.2 113.2 all-gather.4
  260.7 269.9 all-reduce.5
  532.9 78.0 all-reduce.3
where the time goes:
time: 625 us; the launch traced here: 621 us
  waiting for transfers between devices  583 us (93%)
  between operations  14.5 us (2%)
  local copies, waits for them, and re-layouts  11.3 us (2%)
  matrix products  10 us (2%)
    psum x1, waiting for transfers between devices, local(): grad_w_out, grad_w_in = lax.psum((partial_out, partial_in), 'blk')  268 us
    all_gather x1, waiting for transfers between devices, local(): gathered = lax.all_gather(scaled_out, 'blk', axis=0, tiled=True)  125 us
    all_gather x1, waiting for transfers between devices, local(): gathered_pre = lax.all_gather(scaled_pre, 'blk', axis=0, tiled=True)  111 us
    psum x1, waiting for transfers between devices, local(): grad_input = lax.psum(partial_input, 'rep')  78.6 us
  transfers between devices with their start and end apart: 4, of which 4 were waited for; matrix products, arithmetic and copies ran while one was open for 2% of the time, Pallas kernels for 0%

commit v1 on v0

v1 whole, which is shorter than its diff:
```python
import jax
import jax.numpy as jnp
from jax import lax
from jax.experimental import pallas as pl
from jax.experimental.pallas import tpu as pltpu
from jax.sharding import PartitionSpec as P

TILE = 128
NX, NZ, NC = 4, 12, 2
NREP = 8
SLOTS = 64
STEP = 8
BF16 = jnp.bfloat16
F32 = jnp.float32
VMEM_LIMIT = 48 * 1024 * 1024


def blk_index(x, z, c):
    return (x * NZ + z) * NC + c


Z_GROUPS = [[blk_index(x, z, c) for z in range(NZ)] for x in range(NX) for c in range(NC)]
X_GROUPS = [[blk_index(x, z, c) for x in range(NX)] for z in range(NZ) for c in range(NC)]
CORE_SWAP = [(i, i ^ 1) for i in range(NX * NZ * NC)]


def vmem():
    return pl.BlockSpec(memory_space=pltpu.VMEM)


def smem():
    return pl.BlockSpec(memory_space=pltpu.SMEM)


def call(kernel, out_shape, in_specs, flops, moved):
    return pl.pallas_call(
        kernel,
        out_shape=out_shape,
        in_specs=in_specs,
        out_specs=jax.tree.map(lambda _: vmem(), out_shape),
        compiler_params=pltpu.CompilerParams(vmem_limit_bytes=VMEM_LIMIT),
        cost_estimate=pl.CostEstimate(flops=flops, bytes_accessed=moved, transcendentals=0),
    )


def column_scale(degree_ref):
    inv_root = 1.0 / jnp.sqrt(degree_ref[...].astype(F32))
    return jnp.broadcast_to(inv_root, (TILE, TILE)).T


def scale_out_kernel(degree_ref, grad_out_ref, weight_out_ref, out_ref):
    delta = lax.dot_general(
        grad_out_ref[...], weight_out_ref[...], (((1,), (1,)), ((), ())), preferred_element_type=F32
    )
    scaled = (column_scale(degree_ref) * delta).astype(BF16)
    for j in range(NZ):
        out_ref[j] = scaled


def sum_tiles(core_ref, source_ref, count_ref, mine_ref, theirs_ref, tiles_ref, extra):
    core, count = core_ref[0], count_ref[0]

    def step(s, total):
        left, right = [], []
        for k in range(STEP):
            slot = s * STEP + k
            source = source_ref[0, slot]
            chip = lax.shift_right_logical(source, 1)
            place = chip + extra * lax.div(chip, NZ)
            block = jnp.where((source & 1) == core, mine_ref[place], theirs_ref[place])
            right.append(jnp.where(slot < count, block, jnp.zeros_like(block)))
            left.append(tiles_ref[0, slot])
        return total + jnp.dot(
            jnp.concatenate(left, axis=1), jnp.concatenate(right, axis=0), preferred_element_type=F32
        )

    steps = lax.div(count + (STEP - 1), STEP)
    return lax.fori_loop(0, steps, step, jnp.zeros((TILE, TILE), F32))


def hidden_kernel(
    core_ref,
    source_ref,
    count_ref,
    degree_ref,
    mine_ref,
    theirs_ref,
    tiles_ref,
    pre_hidden_ref,
    agg_hidden_ref,
    grad_out_ref,
    agg_input_ref,
    out_ref,
):
    scale = column_scale(degree_ref)
    summed = sum_tiles(core_ref, source_ref, count_ref, mine_ref, theirs_ref, tiles_ref, 0)
    grad_pre = jnp.where(pre_hidden_ref[...].astype(F32) > 0, scale * summed, 0.0).astype(BF16)
    scaled_pre = (scale * grad_pre.astype(F32)).astype(BF16)
    for j in range(NZ):
        out_ref[j, :TILE] = scaled_pre
    across = (((0,), (0,)), ((), ()))
    w_out = lax.dot_general(agg_hidden_ref[...], grad_out_ref[...], across, preferred_element_type=F32)
    for j in range(8):
        out_ref[j, TILE:] = w_out[:, j * TILE : (j + 1) * TILE].astype(BF16)
    w_in = lax.dot_general(agg_input_ref[...], grad_pre, across, preferred_element_type=F32)
    for j in range(4):
        out_ref[8 + j, TILE:] = w_in[j * TILE : (j + 1) * TILE].astype(BF16)


def row_sum_kernel(got_ref, out_ref):
    total = got_ref[0, TILE:].astype(F32)
    for j in range(1, NZ):
        total = total + got_ref[j, TILE:].astype(F32)
    total = total.astype(BF16)
    for i in range(NX):
        for j in range(NZ):
            out_ref[i, j] = got_ref[j, :TILE]
        out_ref[i, NZ] = total


def spread_kernel(
    core_ref, source_ref, count_ref, degree_ref, mine_ref, theirs_ref, tiles_ref, spread_ref, weight_ref
):
    summed = sum_tiles(core_ref, source_ref, count_ref, mine_ref, theirs_ref, tiles_ref, 1)
    spread = (column_scale(degree_ref) * summed).astype(BF16)
    for j in range(NREP):
        spread_ref[j] = spread
    total = jnp.zeros((TILE, TILE), F32)
    for i in range(NX):
        at = i * (NZ + 1) + NZ
        total = total + (mine_ref[at].astype(F32) + theirs_ref[at].astype(F32))
    total = total.astype(BF16)
    for j in range(NZ):
        weight_ref[j] = total


def final_kernel(weights_ref, spread_ref, weight_in_ref, w_out_ref, w_in_ref, input_ref):
    for j in range(8):
        w_out_ref[:, j * TILE : (j + 1) * TILE] = weights_ref[j].astype(F32)
    for j in range(4):
        w_in_ref[j * TILE : (j + 1) * TILE] = weights_ref[8 + j].astype(F32)
    total = jnp.zeros((TILE, 512), F32)
    for k in range(NREP):
        total = total + lax.dot_general(
            spread_ref[k], weight_in_ref[k], (((1,), (1,)), ((), ())), preferred_element_type=F32
        )
    input_ref[...] = total


def local(
    grad_out,
    agg_hidden,
    pre_hidden,
    agg_input,
    weight_in,
    weight_out,
    edge_tiles,
    tile_source,
    tile_count,
    degree,
):
    shape = jax.ShapeDtypeStruct
    core = (lax.axis_index("blk") % 2).astype(jnp.int32).reshape(1)
    degree = degree.reshape(1, TILE)
    with jax.named_scope("weight_in_gather"):
        weights_in = lax.all_gather(weight_in, "rep", axis=0, tiled=False)

    with jax.named_scope("scale_out"):
        sent = call(
            scale_out_kernel, shape((NZ, TILE, TILE), BF16), [vmem()] * 3, 2 * 128 * 128 * 1024, 900000
        )(degree, grad_out, weight_out)
    with jax.named_scope("gather_out_z"):
        row = lax.all_to_all(sent, "blk", 0, 0, tiled=True, axis_index_groups=Z_GROUPS)
    with jax.named_scope("gather_out_x"):
        row = jnp.broadcast_to(row[None], (NX, NZ, TILE, TILE))
        mine = lax.all_to_all(row, "blk", 0, 0, tiled=True, axis_index_groups=X_GROUPS)
        mine = mine.reshape(NX * NZ, TILE, TILE)
    with jax.named_scope("gather_out_core"):
        theirs = lax.ppermute(mine, "blk", CORE_SWAP)
    theirs, weights_in = lax.optimization_barrier((theirs, weights_in))

    with jax.named_scope("hidden"):
        sent = call(
            hidden_kernel,
            shape((NZ, 2 * TILE, TILE), BF16),
            [smem()] * 3 + [vmem()] * 8,
            2 * 128 * 128 * 128 * 76,
            6000000,
        )(core, tile_source, tile_count, degree, mine, theirs, edge_tiles, pre_hidden, agg_hidden, grad_out, agg_input)
    with jax.named_scope("gather_pre_z"):
        row = lax.all_to_all(sent, "blk", 0, 0, tiled=True, axis_index_groups=Z_GROUPS)
    with jax.named_scope("row_sum"):
        row = call(row_sum_kernel, shape((NX, NZ + 1, TILE, TILE), BF16), [vmem()], 200000, 2500000)(row)
    with jax.named_scope("gather_pre_x"):
        mine = lax.all_to_all(row, "blk", 0, 0, tiled=True, axis_index_groups=X_GROUPS)
        mine = mine.reshape(NX * (NZ + 1), TILE, TILE)
    with jax.named_scope("gather_pre_core"):
        theirs = lax.ppermute(mine, "blk", CORE_SWAP)

    with jax.named_scope("spread"):
        spread, weights = call(
            spread_kernel,
            [shape((NREP, TILE, TILE), BF16), shape((NZ, TILE, TILE), BF16)],
            [smem()] * 3 + [vmem()] * 4,
            2 * 128 * 128 * 128 * 64,
            6000000,
        )(core, tile_source, tile_count, degree, mine, theirs, edge_tiles)
    with jax.named_scope("gather_spread"):
        spread = lax.all_to_all(spread, "rep", 0, 0, tiled=True)
    with jax.named_scope("gather_weights_z"):
        weights = lax.all_to_all(weights, "blk", 0, 0, tiled=True, axis_index_groups=Z_GROUPS)
    with jax.named_scope("final"):
        return tuple(
            call(
                final_kernel,
                [shape((128, 1024), F32), shape((512, 128), F32), shape((128, 512), F32)],
                [vmem()] * 3,
                2 * 128 * 1024 * 512,
                2500000,
            )(weights, spread, weights_in)
        )


def solution(mesh):
    return jax.shard_map(
        local,
        mesh=mesh,
        in_specs=(
            P("blk", None),
            P("blk", "rep"),
            P("blk", "rep"),
            P("blk", None),
            P(None, "rep"),
            P("rep", None),
            P("blk", None, None, None),
            P("blk", None),
            P("blk"),
            P("blk"),
        ),
        out_specs=(P("rep", None), P(None, "rep"), P("blk", None)),
        check_vma=False,
    )
```

time: 625 us -> 215 us (0.34)
  waiting for transfers between devices: 583 us -> 36.7 us
  blocking collectives: 0 us -> 133 us
  starting transfers between devices: 0.16 us -> 17.4 us
  matrix products: 10 us -> 0 us
    psum x2 -> x0, waiting for transfers between devices: 347 us -> none  [the longest x1 268 us: local(): grad_w_out, grad_w_in = lax.psum((partial_out, partial_in), 'blk')]
    all_gather x2 -> x1, waiting for transfers between devices: 236 us -> 15.1 us  [local(): weights_in = lax.all_gather(weight_in, 'rep', axis=0, tiled=False)]
    all_to_all x0 -> x5, blocking collectives: none -> 133 us  [the longest x2 69.7 us: local(): lax.all_to_all(sent, 'blk', 0, 0, tiled=True, axis_index_groups=Z_GROUPS)]
    all_to_all x0 -> x1, waiting for transfers between devices: none -> 17.7 us  [local(): lax.all_to_all(row, 'blk', 0, 0, tiled=True, axis_index_groups=X_GROUPS)]
    ppermute x0 -> x2, starting transfers between devices: none -> 13.3 us  [local(): theirs = lax.ppermute(mine, 'blk', CORE_SWAP)]
    dot_general x5 -> x0, matrix products: 10 us -> none  [the longest x1 3.22 us: local(): lax.dot_general(spread, weight_in, (((1,), (1,)), ((), ())), preferred_el...]
  transfers between devices with their start and end apart: 4 -> 4, of which waited for: 4 -> 3; matrix products, arithmetic and copies ran while one was open for 2% -> 0% of each run, Pallas kernels for 0% -> 0%
where the time goes in v1:
time: 215 us; the launch traced here: 213 us
  blocking collectives  133 us (62%)
  waiting for transfers between devices  36.7 us (17%)
  starting transfers between devices  17.4 us (8%)
  between operations  14.8 us (7%)
  Pallas kernels  5.91 us (3%)
  local copies, waits for them, and re-layouts  5.64 us (3%)
    all_to_all x2, blocking collectives, local(): lax.all_to_all(sent, 'blk', 0, 0, tiled=True, axis_index_groups=Z_GROUPS)  69.7 us
    all_to_all x1, blocking collectives, local(): lax.all_to_all(row, 'blk', 0, 0, tiled=True, axis_index_groups=X_GROUPS)  24.6 us
    all_to_all x1, blocking collectives, local(): lax.all_to_all(weights, 'blk', 0, 0, tiled=True, axis_index_groups=Z_GROUPS)  22.5 us
    all_to_all x1, waiting for transfers between devices, local(): lax.all_to_all(row, 'blk', 0, 0, tiled=True, axis_index_groups=X_GROUPS)  17.7 us
    all_to_all x1, blocking collectives, local(): spread = lax.all_to_all(spread, 'rep', 0, 0, tiled=True)  16.1 us
    all_gather x1, waiting for transfers between devices, local(): weights_in = lax.all_gather(weight_in, 'rep', axis=0, tiled=False)  15.1 us
    ppermute x2, starting transfers between devices, local(): theirs = lax.ppermute(mine, 'blk', CORE_SWAP)  13.3 us
  transfers between devices with their start and end apart: 4, of which 3 were waited for; matrix products, arithmetic and copies ran while one was open for 0% of the time, Pallas kernels for 0%

profile of v1, /device:TPU:1, one launch (start us, length us, event | category | flops | bytes accessed | tf_op | source)
XLA Modules:
  0.0 213.4 jit_solution(14927626521331177269)
XLA Ops:
  7.2 0.0 copy-start.1
  7.2 0.9 copy-done.1
  8.1 0.0 copy-start.4
  8.1 0.9 copy-done.4
  9.1 0.0 copy-start.8
  9.1 0.7 copy-done.8
  9.7 0.2 scale_out.1
  10.0 34.2 %all_to_all.30 = bf16[12,128,128]{2,1,0:T(8,128)(2,1)S(1)} all-to-all(bf16[12,128,128]{2,1,0:T(8,128)(2,1)S(1)} %scale_out.1), channel_id=1, replica_groups={{0,16,32,48,64,80,96,112,128,144,160,176},{8,24,40,56,72,88,104,120,136..., dimensions={0} | all-to-all | bytes 786432 | tf_op jit(solution)/shard_map/gather_out_z/all_to_all | solution.py:173
  44.2 1.6 broadcast_in_dim.2
  45.7 0.0 copy-start.2
  45.7 0.0 copy-start.5
  45.7 0.0 copy-start.9
  45.7 0.0 copy-start.10
  45.7 4.2 %all-to-all-start.1 = ((bf16[4,12,128,128]{3,2,1,0:T(8,128)(2,1)}), bf16[4,12,128,128]{3,2,1,0:T(8,128)(2,1)S(1)}, u32[]{:S(2)}, u32[]{:S(2)}) async-start(bf16[4,12,128,128]{3,2,1,0:T(8,128)(2,1)} %broadcast_in_dim.2), calls=%async_computation.1 | async-start | bytes 3145728 | tf_op jit(solution)/shard_map/gather_out_x/all_to_all | solution.py:176
  49.9 0.0 all-gather.3.cloned.1.call-start
  49.9 0.7 all-gather.3.cloned.1.call-update
  50.6 17.7 %all-to-all-done.1 = bf16[4,12,128,128]{3,2,1,0:T(8,128)(2,1)S(1)} async-done(((bf16[4,12,128,128]{3,2,1,0:T(8,128)(2,1)}), bf16[4,12,128,128]{3,2,1,0:T(8,128)(2,1)S(1)}, u32[]{:S(2)}, u32[]{:S(2)}) %all-to-all-start.1) | async-done | bytes 1572896 | tf_op jit(solution)/shard_map/gather_out_x/all_to_all | solution.py:176
  68.3 5.1 %collective-permute-start = (bf16[48,128,128]{2,1,0:T(8,128)(2,1)S(1)}, bf16[48,128,128]{2,1,0:T(8,128)(2,1)S(1)}, u32[]{:S(2)}, u32[]{:S(2)}) collective-permute-start(bf16[48,128,128]{2,1,0:T(8,128)(2,1)S(1)} %bitcast.7), channel_id=1, source_target_pairs={{0,8},{8,0},{16,24},{24,16},{32,40},{40,32},{48,56},{56,48},{64,72... | collective-permute-start | bytes 4718600 | tf_op jit(solution)/shard_map/gather_out_core/ppermute | solution.py:179
  74.1 15.1 %all-gather.3.cloned.1.call-done = bf16[4096,128]{1,0:T(8,128)(2,1)} async-done(((bf16[512,128]{1,0:T(8,128)(2,1)}), bf16[4096,128]{1,0:T(8,128)(2,1)}) %all-gather.3.cloned.1.call-update) | async-done | bytes 1048592 | tf_op jit(solution)/shard_map/weight_in_gather/all_gather | solution.py:166
  89.2 0.0 collective-permute-done.theirs_ref
  89.2 0.0 copy-done.2
  89.2 0.0 copy-done.5
  89.2 0.0 copy-done.9
  89.2 0.0 copy-done.10
  89.2 0.0 copy-start.6
  89.2 0.7 copy-done.6
  90.0 0.0 copy-start.7
  90.0 0.8 copy-done.7
  90.8 2.8 %hidden.1 = bf16[12,256,128]{2,1,0:T(8,128)(2,1)S(1)} custom-call(s32[1]{0:T(128)} %bitcast.core_ref, s32[1,64]{1,0:T(1,128)S(1)} %copy-done.10, s32[1]{0:T(128)S(6)} %copy.13.count_ref, s32[1,128]{1,0:T(1,128)S(1)} %bitcast.11, bf16[48,128,128]{2,1,0:T(8,128)(2,1)S(1)} %bitcast.8, bf16[48,128,128]{2,1,0:T(8,128)(2,1)S(1)} %collective-permute-done.theirs_ref, ...), custom_call_target="tpu_custom_call" | custom-call | flops 318767104 | bytes 6000000 | tf_op jit(solution)/shard_map/hidden/pallas_call | solution.py:183
  93.5 35.5 %all_to_all.31.got_ref = bf16[12,256,128]{2,1,0:T(8,128)(2,1)S(1)} all-to-all(bf16[12,256,128]{2,1,0:T(8,128)(2,1)S(1)} %hidden.1), channel_id=1, replica_groups={{0,16,32,48,64,80,96,112,128,144,160,176},{8,24,40,56,72,88,104,120,136..., dimensions={0} | all-to-all | bytes 1572864 | tf_op jit(solution)/shard_map/gather_pre_z/all_to_all | solution.py:191
  129.0 0.2 row_sum.1
  129.2 0.0 copy-start
  129.2 24.6 %all_to_all.32 = bf16[4,13,128,128]{3,2,1,0:T(8,128)(2,1)S(1)} all-to-all(bf16[4,13,128,128]{3,2,1,0:T(8,128)(2,1)S(1)} %row_sum.1), channel_id=1, replica_groups={{0,192,384,576},{8,200,392,584},{16,208,400,592},{24,216,408,600},{32,2..., dimensions={0} | all-to-all | bytes 3407872 | tf_op jit(solution)/shard_map/gather_pre_x/all_to_all | solution.py:195
  153.8 8.1 %collective-permute-start.1 = (bf16[52,128,128]{2,1,0:T(8,128)(2,1)S(1)}, bf16[52,128,128]{2,1,0:T(8,128)(2,1)S(1)}, u32[]{:S(2)}, u32[]{:S(2)}) collective-permute-start(bf16[52,128,128]{2,1,0:T(8,128)(2,1)S(1)} %bitcast.5), channel_id=1, source_target_pairs={{0,8},{8,0},{16,24},{24,16},{32,40},{40,32},{48,56},{56,48},{64,72... | collective-permute-start | bytes 5111816 | tf_op jit(solution)/shard_map/gather_pre_core/ppermute | solution.py:198
  162.0 3.2 %collective-permute-done.1.theirs_ref = bf16[52,128,128]{2,1,0:T(8,128)(2,1)S(1)} collective-permute-done((bf16[52,128,128]{2,1,0:T(8,128)(2,1)S(1)}, bf16[52,128,128]{2,1,0:T(8,128)(2,1)S(1)}, u32[]{:S(2)}, u32[]{:S(2)}) %collective-permute-start.1) | collective-permute-done | bytes 1703968 | tf_op jit(solution)/shard_map/gather_pre_core/ppermute | solution.py:198
  165.2 0.0 copy-done
  165.2 1.4 spread.1
  166.6 0.0 copy-start.3
  166.6 16.1 %all_to_all.33.spread_ref = bf16[8,128,128]{2,1,0:T(8,128)(2,1)S(1)} all-to-all(bf16[8,128,128]{2,1,0:T(8,128)(2,1)S(1)} %get-tuple-element.9), channel_id=1, replica_groups=mesh['blk'=96,'rep'=8] {'rep'}, dimensions={0} | all-to-all | bytes 524288 | tf_op jit(solution)/shard_map/gather_spread/all_to_all | solution.py:209
  182.7 22.5 %all_to_all.34.weights_ref = bf16[12,128,128]{2,1,0:T(8,128)(2,1)S(1)} all-to-all(bf16[12,128,128]{2,1,0:T(8,128)(2,1)S(1)} %get-tuple-element.8), channel_id=1, replica_groups={{0,16,32,48,64,80,96,112,128,144,160,176},{8,24,40,56,72,88,104,120,136..., dimensions={0} | all-to-all | bytes 786432 | tf_op jit(solution)/shard_map/gather_weights_z/all_to_all | solution.py:211
  205.2 0.0 copy-done.3
  205.2 1.3 final.1
Async XLA Ops:
  7.2 1.0 copy-start.1
  8.1 0.9 copy-start.4
  9.1 0.7 copy-start.8
  45.7 43.5 %copy-start.2 = (bf16[128,1024]{1,0:T(8,128)(2,1)S(1)}, bf16[128,1024]{1,0:T(8,128)(2,1)}, u32[]{:S(2)}) copy-start(bf16[128,1024]{1,0:T(8,128)(2,1)} %grad_out_ref.3) | copy-start | bytes 786436
  45.7 43.5 %copy-start.5 = (bf16[128,512]{1,0:T(8,128)(2,1)S(1)}, bf16[128,512]{1,0:T(8,128)(2,1)}, u32[]{:S(2)}) copy-start(bf16[128,512]{1,0:T(8,128)(2,1)} %agg_input_ref.1) | copy-start | bytes 393220
  45.7 43.5 %copy-start.9 = (s32[128]{0:T(128)S(1)}, s32[128]{0:T(128)}, u32[]{:S(2)}) copy-start(s32[128]{0:T(128)} %param.19) | copy-start | bytes 1540
  45.7 43.5 %copy-start.10 = (s32[1,64]{1,0:T(1,128)S(1)}, s32[1,64]{1,0:T(1,128)}, u32[]{:S(2)}) copy-start(s32[1,64]{1,0:T(1,128)} %source_ref.3) | copy-start | bytes 772
  45.7 22.6 %all-to-all-start.1 = ((bf16[4,12,128,128]{3,2,1,0:T(8,128)(2,1)}), bf16[4,12,128,128]{3,2,1,0:T(8,128)(2,1)S(1)}, u32[]{:S(2)}, u32[]{:S(2)}) async-start(bf16[4,12,128,128]{3,2,1,0:T(8,128)(2,1)} %broadcast_in_dim.2), calls=%async_computation.1 | async-start | bytes 3145728 | tf_op jit(solution)/shard_map/gather_out_x/all_to_all | solution.py:176
  49.9 39.3 %all-gather.3.cloned.1.call-start = ((), (), s32[]{:S(2)}) async-start(), calls=%async_computation.6 | async-start | bytes 1179648 | tf_op jit(solution)/shard_map/weight_in_gather/all_gather | solution.py:166
  68.3 20.9 %collective-permute-start = (bf16[48,128,128]{2,1,0:T(8,128)(2,1)S(1)}, bf16[48,128,128]{2,1,0:T(8,128)(2,1)S(1)}, u32[]{:S(2)}, u32[]{:S(2)}) collective-permute-start(bf16[48,128,128]{2,1,0:T(8,128)(2,1)S(1)} %bitcast.7), channel_id=1, source_target_pairs={{0,8},{8,0},{16,24},{24,16},{32,40},{40,32},{48,56},{56,48},{64,72... | collective-permute-start | bytes 4718600 | tf_op jit(solution)/shard_map/gather_out_core/ppermute | solution.py:179
  89.2 0.8 copy-start.6
  90.0 0.8 copy-start.7
  129.2 35.9 %copy-start = (bf16[1,64,128,128]{3,2,1,0:T(8,128)(2,1)S(1)}, bf16[1,64,128,128]{3,2,1,0:T(8,128)(2,1)}, u32[]{:S(2)}) copy-start(bf16[1,64,128,128]{3,2,1,0:T(8,128)(2,1)} %tiles_ref.3) | copy-start | bytes 6291460
  153.8 11.3 %collective-permute-start.1 = (bf16[52,128,128]{2,1,0:T(8,128)(2,1)S(1)}, bf16[52,128,128]{2,1,0:T(8,128)(2,1)S(1)}, u32[]{:S(2)}, u32[]{:S(2)}) collective-permute-start(bf16[52,128,128]{2,1,0:T(8,128)(2,1)S(1)} %bitcast.5), channel_id=1, source_target_pairs={{0,8},{8,0},{16,24},{24,16},{32,40},{40,32},{48,56},{56,48},{64,72... | collective-permute-start | bytes 5111816 | tf_op jit(solution)/shard_map/gather_pre_core/ppermute | solution.py:198
  166.6 38.6 %copy-start.3 = (bf16[4096,128]{1,0:T(8,128)(2,1)S(1)}, bf16[4096,128]{1,0:T(8,128)(2,1)}, u32[]{:S(2)}) copy-start(bf16[4096,128]{1,0:T(8,128)(2,1)} %all-gather.3.cloned.1.call-done) | copy-start | bytes 3145732
Sparse Core Ops, SparseCore 0:
  53.1 36.0 all-gather.2

commit v2 on v0

v2 whole, which is shorter than its diff:
```python
import jax
import jax.numpy as jnp
from jax import lax
from jax.experimental import pallas as pl
from jax.experimental.pallas import tpu as pltpu
from jax.sharding import PartitionSpec as P

TILE = 128
NX, NZ, NC = 4, 12, 2
NREP = 8
LINE = NZ * NC
WIDE = LINE * TILE
BF16 = jnp.bfloat16
F32 = jnp.float32
VMEM_LIMIT = 40 * 1024 * 1024
ACROSS = (((0,), (0,)), ((), ()))
BY_ROWS = (((1,), (1,)), ((), ()))


def blk_index(x, z, c):
    return (x * NZ + z) * NC + c


Z_GROUPS = [[blk_index(x, z, c) for z in range(NZ)] for x in range(NX) for c in range(NC)]
X_GROUPS = [[blk_index(x, z, c) for x in range(NX)] for z in range(NZ) for c in range(NC)]
LINE_GROUPS = [[x * LINE + p for p in range(LINE)] for x in range(NX)]


def along_x(k):
    return [(x * LINE + p, (x + k) % NX * LINE + p) for x in range(NX) for p in range(LINE)]


def vmem():
    return pl.BlockSpec(memory_space=pltpu.VMEM)


def smem():
    return pl.BlockSpec(memory_space=pltpu.SMEM)


def call(kernel, out_shape, in_specs, flops, moved):
    return pl.pallas_call(
        kernel,
        out_shape=out_shape,
        in_specs=in_specs,
        out_specs=jax.tree.map(lambda _: vmem(), out_shape),
        compiler_params=pltpu.CompilerParams(vmem_limit_bytes=VMEM_LIMIT),
        cost_estimate=pl.CostEstimate(flops=flops, bytes_accessed=moved, transcendentals=0),
    )


def column_scale(degree_ref):
    inv_root = 1.0 / jnp.sqrt(degree_ref[...].astype(F32))
    return jnp.broadcast_to(inv_root, (TILE, TILE)).T


def scale_out_kernel(degree_ref, grad_out_ref, weight_out_ref, out_ref):
    delta = lax.dot_general(grad_out_ref[...], weight_out_ref[...], BY_ROWS, preferred_element_type=F32)
    out_ref[...] = (column_scale(degree_ref) * delta).astype(BF16)


def spread_tiles_kernel(x_ref, source_ref, count_ref, tiles_ref, *out_refs):
    for out_ref in out_refs:
        out_ref[...] = jnp.zeros_like(out_ref)

    def step(slot, carry):
        source = source_ref[0, slot]
        line = lax.div(source, LINE)
        columns = pl.ds(pl.multiple_of((source - line * LINE) * TILE, TILE), TILE)
        away = (line - x_ref[0] + NX) & (NX - 1)
        for k, out_ref in enumerate(out_refs):

            @pl.when(away == k)
            def _():
                out_ref[:, columns] = tiles_ref[0, slot]

        return carry

    lax.fori_loop(0, count_ref[0], step, 0)


def out_parts_kernel(x_ref, t0_ref, t1_ref, t2_ref, t3_ref, blocks_ref, out_ref):
    for k, tiles_ref in enumerate((t0_ref, t1_ref, t2_ref, t3_ref)):
        part = jnp.dot(tiles_ref[...], blocks_ref[...], preferred_element_type=F32)
        out_ref[(x_ref[0] - k + NX) & (NX - 1)] = part.astype(BF16)


def hidden_kernel(
    degree_ref, got_ref, pre_hidden_ref, agg_hidden_ref, grad_out_ref, agg_input_ref, scaled_ref, weight_ref
):
    scale = column_scale(degree_ref)
    summed = (got_ref[0].astype(F32) + got_ref[1].astype(F32)) + (got_ref[2].astype(F32) + got_ref[3].astype(F32))
    grad_pre = jnp.where(pre_hidden_ref[...].astype(F32) > 0, scale * summed, 0.0).astype(BF16)
    scaled_ref[...] = (scale * grad_pre.astype(F32)).astype(BF16)
    w_out = lax.dot_general(agg_hidden_ref[...], grad_out_ref[...], ACROSS, preferred_element_type=F32)
    for j in range(8):
        weight_ref[j] = w_out[:, j * TILE : (j + 1) * TILE].astype(BF16)
    w_in = lax.dot_general(agg_input_ref[...], grad_pre, ACROSS, preferred_element_type=F32)
    for j in range(4):
        weight_ref[8 + j] = w_in[j * TILE : (j + 1) * TILE].astype(BF16)


def pre_parts_kernel(x_ref, t0_ref, t1_ref, t2_ref, t3_ref, blocks_ref, weight_ref, out_ref):
    total = weight_ref[0].astype(F32)
    for j in range(1, NZ):
        total = total + weight_ref[j].astype(F32)
    total = total.astype(BF16)
    for k, tiles_ref in enumerate((t0_ref, t1_ref, t2_ref, t3_ref)):
        part = jnp.dot(tiles_ref[...], blocks_ref[...], preferred_element_type=F32)
        out_ref[(x_ref[0] - k + NX) & (NX - 1), :TILE] = part.astype(BF16)
        out_ref[k, TILE:] = total


def spread_kernel(degree_ref, got_ref, spread_ref, weight_ref):
    total = (got_ref[0].astype(F32) + got_ref[1].astype(F32)) + (got_ref[2].astype(F32) + got_ref[3].astype(F32))
    spread = (column_scale(degree_ref) * total[:TILE]).astype(BF16)
    for j in range(NREP):
        spread_ref[j] = spread
    weight_ref[...] = total[TILE:].astype(BF16)


def final_kernel(weights_ref, spread_ref, weight_in_ref, w_out_ref, w_in_ref, input_ref):
    for j in range(8):
        w_out_ref[:, j * TILE : (j + 1) * TILE] = weights_ref[2 * j].astype(F32) + weights_ref[2 * j + 1].astype(F32)
    for j in range(4):
        w_in_ref[j * TILE : (j + 1) * TILE] = weights_ref[16 + 2 * j].astype(F32) + weights_ref[17 + 2 * j].astype(F32)
    total = jnp.zeros((TILE, 512), F32)
    for k in range(NREP):
        total = total + lax.dot_general(spread_ref[k], weight_in_ref[k], BY_ROWS, preferred_element_type=F32)
    input_ref[...] = total


def local(
    grad_out,
    agg_hidden,
    pre_hidden,
    agg_input,
    weight_in,
    weight_out,
    edge_tiles,
    tile_source,
    tile_count,
    degree,
):
    shape = jax.ShapeDtypeStruct
    block = shape((TILE, TILE), BF16)
    x = (lax.axis_index("blk") // LINE).astype(jnp.int32).reshape(1)
    degree = degree.reshape(1, TILE)

    with jax.named_scope("spread_tiles"):
        tiles = call(
            spread_tiles_kernel, [shape((TILE, WIDE), BF16)] * NX, [smem()] * 3 + [vmem()], 1000000, 5000000
        )(x, tile_source, tile_count, edge_tiles)
    with jax.named_scope("exchange_tiles"):
        tiles = [tiles[0]] + [lax.ppermute(tiles[k], "blk", along_x(k)) for k in range(1, NX)]
    with jax.named_scope("weight_in_gather"):
        weights_in = jnp.broadcast_to(weight_in[None], (NREP, 512, TILE))
        weights_in = lax.all_to_all(weights_in, "rep", 0, 0, tiled=True)
    with jax.named_scope("scale_out"):
        scaled = call(scale_out_kernel, block, [vmem()] * 3, 2 * 128 * 128 * 1024, 600000)(
            degree, grad_out, weight_out
        )
    with jax.named_scope("gather_out"):
        blocks = lax.all_gather(scaled, "blk", axis=0, tiled=True, axis_index_groups=LINE_GROUPS)
    blocks, weights_in = lax.optimization_barrier((blocks, weights_in))
    with jax.named_scope("out_parts"):
        parts = call(
            out_parts_kernel, shape((NX, TILE, TILE), BF16), [smem()] + [vmem()] * 5, 2 * 512 * 3072 * 128, 4000000
        )(x, *tiles, blocks)
    with jax.named_scope("sum_out_x"):
        parts = lax.all_to_all(parts, "blk", 0, 0, tiled=True, axis_index_groups=X_GROUPS)
    with jax.named_scope("hidden"):
        scaled, weights = call(
            hidden_kernel, [block, shape((NZ, TILE, TILE), BF16)], [vmem()] * 6, 2 * 128 * 128 * 1536, 1200000
        )(degree, parts, pre_hidden, agg_hidden, grad_out, agg_input)
    with jax.named_scope("sum_weights_z"):
        weights = lax.all_to_all(weights, "blk", 0, 0, tiled=True, axis_index_groups=Z_GROUPS)
    with jax.named_scope("gather_pre"):
        blocks = lax.all_gather(scaled, "blk", axis=0, tiled=True, axis_index_groups=LINE_GROUPS)
    with jax.named_scope("pre_parts"):
        parts = call(
            pre_parts_kernel,
            shape((NX, 2 * TILE, TILE), BF16),
            [smem()] + [vmem()] * 6,
            2 * 512 * 3072 * 128,
            4500000,
        )(x, *tiles, blocks, weights)
    with jax.named_scope("sum_pre_x"):
        parts = lax.all_to_all(parts, "blk", 0, 0, tiled=True, axis_index_groups=X_GROUPS)
    with jax.named_scope("spread"):
        spread, weights = call(
            spread_kernel, [shape((NREP, TILE, TILE), BF16), block], [vmem()] * 2, 500000, 600000
        )(degree, parts)
    with jax.named_scope("gather_spread"):
        spread = lax.all_to_all(spread, "rep", 0, 0, tiled=True)
    with jax.named_scope("gather_weights"):
        weights = lax.all_gather(weights, "blk", axis=0, tiled=False, axis_index_groups=LINE_GROUPS)
    with jax.named_scope("final"):
        return tuple(
            call(
                final_kernel,
                [shape((128, 1024), F32), shape((512, 128), F32), shape((128, 512), F32)],
                [vmem()] * 3,
                2 * 128 * 1024 * 512,
                2500000,
            )(weights, spread, weights_in)
        )


def solution(mesh):
    return jax.shard_map(
        local,
        mesh=mesh,
        in_specs=(
            P("blk", None),
            P("blk", "rep"),
            P("blk", "rep"),
            P("blk", None),
            P(None, "rep"),
            P("rep", None),
            P("blk", None, None, None),
            P("blk", None),
            P("blk"),
            P("blk"),
        ),
        out_specs=(P("rep", None), P(None, "rep"), P("blk", None)),
        check_vma=False,
    )
```

time: 625 us -> 171 us (0.27)
  waiting for transfers between devices: 583 us -> 0.02 us
  blocking collectives: 0 us -> 120 us
  starting transfers between devices: 0.16 us -> 31.1 us
  between operations: 14.5 us -> 1.44 us
  matrix products: 10 us -> 0 us
  Pallas kernels: 0 us -> 9.41 us
    psum x2 -> x0, waiting for transfers between devices: 347 us -> none  [the longest x1 268 us: local(): grad_w_out, grad_w_in = lax.psum((partial_out, partial_in), 'blk')]
    all_gather x2 -> x0, waiting for transfers between devices: 236 us -> none  [the longest x1 125 us: local(): gathered = lax.all_gather(scaled_out, 'blk', axis=0, tiled=True)]
    all_gather x0 -> x3, blocking collectives: none -> 103 us  [the longest x2 78.1 us: local(): lax.all_gather(scaled, 'blk', axis=0, tiled=True, axis_index_groups=LINE_...]
    all_to_all x0 -> x3, starting transfers between devices: none -> 20.4 us  [the longest x1 7.78 us: local(): weights_in = lax.all_to_all(weights_in, 'rep', 0, 0, tiled=True)]
    all_to_all x0 -> x2, blocking collectives: none -> 16.1 us  [local(): lax.all_to_all(parts, 'blk', 0, 0, tiled=True, axis_index_groups=X_GROUPS)]
    ppermute x0 -> x3, starting transfers between devices: none -> 10.6 us  [local(): lax.ppermute(tiles[k], 'blk', along_x(k))]
    dot_general x5 -> x0, matrix products: 10 us -> none  [the longest x1 3.22 us: local(): lax.dot_general(spread, weight_in, (((1,), (1,)), ((), ())), preferred_el...]
    pallas_call x0 -> x7, Pallas kernels: none -> 9.41 us  [the longest x1 2.31 us: local(): call(spread_tiles_kernel, [shape((TILE, WIDE), BF16)] * NX, [smem()] * 3...]
  transfers between devices with their start and end apart: 4 -> 6, of which waited for: 4 -> 0; matrix products, arithmetic and copies ran while one was open for 2% -> 0% of each run, Pallas kernels for 0% -> 1%
where the time goes in v2:
time: 171 us; the launch traced here: 170 us
  blocking collectives  120 us (70%)
  starting transfers between devices  31.1 us (18%)
  Pallas kernels  9.41 us (6%)
  local copies, waits for them, and re-layouts  8.55 us (5%)
    all_gather x2, blocking collectives, local(): lax.all_gather(scaled, 'blk', axis=0, tiled=True, axis_index_groups=LINE_...  78.1 us
    all_gather x1, blocking collectives, local(): lax.all_gather(weights, 'blk', axis=0, tiled=False, axis_index_groups=LIN...  25.4 us
    all_to_all x2, blocking collectives, local(): lax.all_to_all(parts, 'blk', 0, 0, tiled=True, axis_index_groups=X_GROUPS)  16.1 us
    ppermute x3, starting transfers between devices, local(): lax.ppermute(tiles[k], 'blk', along_x(k))  10.6 us
    all_to_all x1, starting transfers between devices, local(): weights_in = lax.all_to_all(weights_in, 'rep', 0, 0, tiled=True)  7.78 us
    all_to_all x1, starting transfers between devices, local(): spread = lax.all_to_all(spread, 'rep', 0, 0, tiled=True)  6.64 us
    unnamed x24, local copies, waits for them, and re-layouts  6.51 us
    all_to_all x1, starting transfers between devices, local(): lax.all_to_all(weights, 'blk', 0, 0, tiled=True, axis_index_groups=Z_GROUPS)  6 us
  transfers between devices with their start and end apart: 6, of which 0 were waited for; matrix products, arithmetic and copies ran while one was open for 0% of the time, Pallas kernels for 1%

profile of v2, /device:TPU:1, one launch (start us, length us, event | category | flops | bytes accessed | tf_op | source)
XLA Modules:
  0.0 170.0 jit_solution(7535235492084264884)
XLA Ops:
  0.6 0.0 copy-start.11
  0.6 2.0 %broadcast_in_dim.2 = bf16[8,512,128]{2,1,0:T(8,128)(2,1)} broadcast(bf16[512,128]{1,0:T(8,128)(2,1)} %param.14), dimensions={1,2} | broadcast | bytes 1179648 | tf_op jit(solution)/shard_map/weight_in_gather/broadcast_in_dim | solution.py:157
  2.7 0.0 copy-start.10
  2.7 7.8 %all-to-all-start = ((bf16[8,512,128]{2,1,0:T(8,128)(2,1)}), bf16[8,512,128]{2,1,0:T(8,128)(2,1)S(1)}, u32[]{:S(2)}, u32[]{:S(2)}) async-start(bf16[8,512,128]{2,1,0:T(8,128)(2,1)} %broadcast_in_dim.2), calls=%async_computation | async-start | bytes 2097152 | tf_op jit(solution)/shard_map/weight_in_gather/all_to_all | solution.py:158
  11.1 0.0 copy-done.11
  11.1 0.0 copy-start.2
  11.1 1.6 copy-done.2
  12.7 2.3 %spread_tiles.1 = (bf16[128,3072]{1,0:T(8,128)(2,1)S(1)}, bf16[128,3072]{1,0:T(8,128)(2,1)}, bf16[128,3072]{1,0:T(8,128)(2,1)}, bf16[128,3072]{1,0:T(8,128)(2,1)}) custom-call(s32[1]{0:T(128)} %bitcast.1.x_ref, s32[1,64]{1,0:T(1,128)S(1)} %copy-done.11, s32[1]{0:T(128)S(6)} %copy.13.count_ref, bf16[1,64,128,128]{3,2,1,0:T(8,128)(2,1)S(1)} %copy-done.2), custom_call_target="tpu_custom_call" | custom-call | flops 1000000 | bytes 5000000 | tf_op jit(solution)/shard_map/spread_tiles/pallas_call | solution.py:151
  15.0 3.7 %collective-permute-start = (bf16[128,3072]{1,0:T(8,128)(2,1)}, bf16[128,3072]{1,0:T(8,128)(2,1)S(1)}, u32[]{:S(2)}, u32[]{:S(2)}) collective-permute-start(bf16[128,3072]{1,0:T(8,128)(2,1)} %get-tuple-element.14), channel_id=1, source_target_pairs={{0,192},{8,200},{16,208},{24,216},{32,224},{40,232},{48,240},{56,2... | collective-permute-start | bytes 2359304 | tf_op jit(solution)/shard_map/exchange_tiles/ppermute | solution.py:155
  18.8 4.6 %collective-permute-start.1 = (bf16[128,3072]{1,0:T(8,128)(2,1)}, bf16[128,3072]{1,0:T(8,128)(2,1)S(1)}, u32[]{:S(2)}, u32[]{:S(2)}) collective-permute-start(bf16[128,3072]{1,0:T(8,128)(2,1)} %get-tuple-element.15), channel_id=1, source_target_pairs={{0,384},{8,392},{16,400},{24,408},{32,416},{40,424},{48,432},{56,4... | collective-permute-start | bytes 2359304 | tf_op jit(solution)/shard_map/exchange_tiles/ppermute | solution.py:155
  23.4 2.3 %collective-permute-start.2 = (bf16[128,3072]{1,0:T(8,128)(2,1)}, bf16[128,3072]{1,0:T(8,128)(2,1)}, u32[]{:S(2)}, u32[]{:S(2)}) collective-permute-start(bf16[128,3072]{1,0:T(8,128)(2,1)} %get-tuple-element.16), channel_id=1, source_target_pairs={{0,576},{8,584},{16,592},{24,600},{32,608},{40,616},{48,624},{56,6... | collective-permute-start | bytes 2359304 | tf_op jit(solution)/shard_map/exchange_tiles/ppermute | solution.py:155
  25.7 0.0 copy-done.10
  25.7 0.0 copy-start.3
  25.7 0.9 copy-done.3
  26.7 0.0 copy-start.6
  26.7 0.9 copy-done.6
  27.6 0.2 scale_out.1
  27.9 40.2 %all_gather.12.blocks_ref = bf16[3072,128]{1,0:T(8,128)(2,1)} all-gather(bf16[128,128]{1,0:T(8,128)(2,1)S(1)} %scale_out.1), channel_id=1, replica_groups={{0,8,16,24,32,40,48,56,64,72,80,88,96,104,112,120,128,136,144,152,160,1..., dimensions={0}, use_global_device_ids=true | all-gather | bytes 819200 | tf_op jit(solution)/shard_map/gather_out/all_gather | solution.py:164
  68.0 0.0 all-to-all-done.weight_in_ref
  68.0 0.0 collective-permute-done.t1_ref
  68.0 0.0 collective-permute-done.1.t2_ref
  68.0 0.0 collective-permute-done.2.t3_ref
  68.1 0.0 copy-start
  68.1 1.1 copy-done
  69.2 0.0 copy-start.4
  69.2 0.0 copy-start.8
  69.2 0.0 copy-start.9
  69.2 2.2 %out_parts.1 = bf16[4,128,128]{2,1,0:T(8,128)(2,1)S(1)} custom-call(s32[1]{0:T(128)} %bitcast.1.x_ref, bf16[128,3072]{1,0:T(8,128)(2,1)S(1)} %get-tuple-element.13.t0_ref, bf16[128,3072]{1,0:T(8,128)(2,1)S(1)} %collective-permute-done.t1_ref, bf16[128,3072]{1,0:T(8,128)(2,1)S(1)} %collective-permute-done.1.t2_ref, ...), custom_call_target="tpu_custom_call" | custom-call | flops 402653184 | bytes 4000000 | tf_op jit(solution)/shard_map/out_parts/pallas_call | solution.py:167
  71.4 7.3 %all_to_all.25.got_ref = bf16[4,128,128]{2,1,0:T(8,128)(2,1)S(1)} all-to-all(bf16[4,128,128]{2,1,0:T(8,128)(2,1)S(1)} %out_parts.1), channel_id=1, replica_groups={{0,192,384,576},{8,200,392,584},{16,208,400,592},{24,216,408,600},{32,2..., dimensions={0} | all-to-all | bytes 262144 | tf_op jit(solution)/shard_map/sum_out_x/all_to_all | solution.py:171
  78.7 0.0 copy-done.4
  78.7 0.0 copy-done.7
  78.7 0.0 copy-done.8
  78.7 0.0 copy-done.9
  78.7 0.3 hidden.1
  79.1 0.0 copy-start.5
  79.1 0.7 copy-done.5
  79.8 6.0 %all-to-all-start.2 = ((bf16[12,128,128]{2,1,0:T(8,128)(2,1)}), bf16[12,128,128]{2,1,0:T(8,128)(2,1)}, u32[]{:S(2)}, u32[]{:S(2)}) async-start(bf16[12,128,128]{2,1,0:T(8,128)(2,1)} %copy-done.5), calls=%async_computation.2 | async-start | bytes 786432 | tf_op jit(solution)/shard_map/sum_weights_z/all_to_all | solution.py:177
  85.8 37.9 %all_gather.13.blocks_ref = bf16[3072,128]{1,0:T(8,128)(2,1)} all-gather(bf16[128,128]{1,0:T(8,128)(2,1)S(1)} %get-tuple-element.18), channel_id=1, replica_groups={{0,8,16,24,32,40,48,56,64,72,80,88,96,104,112,120,128,136,144,152,160,1..., dimensions={0}, use_global_device_ids=true | all-gather | bytes 819200 | tf_op jit(solution)/shard_map/gather_pre/all_gather | solution.py:179
  123.7 0.0 all-to-all-done.2.weight_ref
  123.7 0.0 copy-start.1
  123.7 1.1 copy-done.1
  124.9 2.2 %pre_parts.1 = bf16[4,256,128]{2,1,0:T(8,128)(2,1)S(1)} custom-call(s32[1]{0:T(128)} %bitcast.1.x_ref, bf16[128,3072]{1,0:T(8,128)(2,1)S(1)} %get-tuple-element.13.t0_ref, bf16[128,3072]{1,0:T(8,128)(2,1)S(1)} %collective-permute-done.t1_ref, bf16[128,3072]{1,0:T(8,128)(2,1)S(1)} %collective-permute-done.1.t2_ref, ...), custom_call_target="tpu_custom_call" | custom-call | flops 402653184 | bytes 4500000 | tf_op jit(solution)/shard_map/pre_parts/pallas_call | solution.py:181
  127.1 8.8 %all_to_all.26.got_ref = bf16[4,256,128]{2,1,0:T(8,128)(2,1)S(1)} all-to-all(bf16[4,256,128]{2,1,0:T(8,128)(2,1)S(1)} %pre_parts.1), channel_id=1, replica_groups={{0,192,384,576},{8,200,392,584},{16,208,400,592},{24,216,408,600},{32,2..., dimensions={0} | all-to-all | bytes 524288 | tf_op jit(solution)/shard_map/sum_pre_x/all_to_all | solution.py:189
  135.9 0.8 spread.1
  136.7 6.6 %all-to-all-start.4 = ((bf16[8,128,128]{2,1,0:T(8,128)(2,1)}), bf16[8,128,128]{2,1,0:T(8,128)(2,1)S(1)}, u32[]{:S(2)}, u32[]{:S(2)}) async-start(bf16[8,128,128]{2,1,0:T(8,128)(2,1)} %get-tuple-element.21), calls=%async_computation.4 | async-start | bytes 524288 | tf_op jit(solution)/shard_map/gather_spread/all_to_all | solution.py:195
  143.3 25.4 %all-gather = bf16[3072,128]{1,0:T(8,128)(2,1)S(1)} all-gather(bf16[128,128]{1,0:T(8,128)(2,1)S(1)} %get-tuple-element.20), channel_id=2, replica_groups={{0,8,16,24,32,40,48,56,64,72,80,88,96,104,112,120,128,136,144,152,160,1..., dimensions={0}, use_global_device_ids=true | all-gather | bytes 819200 | tf_op jit(solution)/shard_map/gather_weights/all_gather | solution.py:197
  168.7 0.0 all-to-all-done.4.spread_ref
  168.7 1.3 final.1
  (1 shorter events, 0.0 us)
Async XLA Ops:
  0.6 10.5 %copy-start.11 = (s32[1,64]{1,0:T(1,128)S(1)}, s32[1,64]{1,0:T(1,128)}, u32[]{:S(2)}) copy-start(s32[1,64]{1,0:T(1,128)} %source_ref.1) | copy-start | bytes 772
  2.7 23.0 %copy-start.10 = (s32[128]{0:T(128)S(1)}, s32[128]{0:T(128)}, u32[]{:S(2)}) copy-start(s32[128]{0:T(128)} %param.19) | copy-start | bytes 1540
  2.7 65.3 %all-to-all-start = ((bf16[8,512,128]{2,1,0:T(8,128)(2,1)}), bf16[8,512,128]{2,1,0:T(8,128)(2,1)S(1)}, u32[]{:S(2)}, u32[]{:S(2)}) async-start(bf16[8,512,128]{2,1,0:T(8,128)(2,1)} %broadcast_in_dim.2), calls=%async_computation | async-start | bytes 2097152 | tf_op jit(solution)/shard_map/weight_in_gather/all_to_all | solution.py:158
  11.1 1.6 copy-start.2
  15.0 53.0 %collective-permute-start = (bf16[128,3072]{1,0:T(8,128)(2,1)}, bf16[128,3072]{1,0:T(8,128)(2,1)S(1)}, u32[]{:S(2)}, u32[]{:S(2)}) collective-permute-start(bf16[128,3072]{1,0:T(8,128)(2,1)} %get-tuple-element.14), channel_id=1, source_target_pairs={{0,192},{8,200},{16,208},{24,216},{32,224},{40,232},{48,240},{56,2... | collective-permute-start | bytes 2359304 | tf_op jit(solution)/shard_map/exchange_tiles/ppermute | solution.py:155
  18.8 49.3 %collective-permute-start.1 = (bf16[128,3072]{1,0:T(8,128)(2,1)}, bf16[128,3072]{1,0:T(8,128)(2,1)S(1)}, u32[]{:S(2)}, u32[]{:S(2)}) collective-permute-start(bf16[128,3072]{1,0:T(8,128)(2,1)} %get-tuple-element.15), channel_id=1, source_target_pairs={{0,384},{8,392},{16,400},{24,408},{32,416},{40,424},{48,432},{56,4... | collective-permute-start | bytes 2359304 | tf_op jit(solution)/shard_map/exchange_tiles/ppermute | solution.py:155
  23.4 44.7 %collective-permute-start.2 = (bf16[128,3072]{1,0:T(8,128)(2,1)}, bf16[128,3072]{1,0:T(8,128)(2,1)}, u32[]{:S(2)}, u32[]{:S(2)}) collective-permute-start(bf16[128,3072]{1,0:T(8,128)(2,1)} %get-tuple-element.16), channel_id=1, source_target_pairs={{0,576},{8,584},{16,592},{24,600},{32,608},{40,616},{48,624},{56,6... | collective-permute-start | bytes 2359304 | tf_op jit(solution)/shard_map/exchange_tiles/ppermute | solution.py:155
  25.7 1.0 copy-start.3
  26.7 0.9 copy-start.6
  68.1 1.1 copy-start
  69.2 9.5 %copy-start.4 = (bf16[128,1024]{1,0:T(8,128)(2,1)S(1)}, bf16[128,1024]{1,0:T(8,128)(2,1)}, u32[]{:S(2)}) copy-start(bf16[128,1024]{1,0:T(8,128)(2,1)} %grad_out_ref.3) | copy-start | bytes 786436
  69.2 9.5 %copy-start.7 = (bf16[128,512]{1,0:T(8,128)(2,1)S(1)}, bf16[128,512]{1,0:T(8,128)(2,1)}, u32[]{:S(2)}) copy-start(bf16[128,512]{1,0:T(8,128)(2,1)} %agg_input_ref.1) | copy-start | bytes 393220
  69.2 9.5 %copy-start.8 = (bf16[128,128]{1,0:T(8,128)(2,1)S(1)}, bf16[128,128]{1,0:T(8,128)(2,1)}, u32[]{:S(2)}) copy-start(bf16[128,128]{1,0:T(8,128)(2,1)} %pre_hidden_ref.1) | copy-start | bytes 98308
  69.2 9.5 %copy-start.9 = (bf16[128,128]{1,0:T(8,128)(2,1)S(1)}, bf16[128,128]{1,0:T(8,128)(2,1)}, u32[]{:S(2)}) copy-start(bf16[128,128]{1,0:T(8,128)(2,1)} %agg_hidden_ref.1) | copy-start | bytes 98308
  79.1 0.7 copy-start.5
  79.8 43.9 %all-to-all-start.2 = ((bf16[12,128,128]{2,1,0:T(8,128)(2,1)}), bf16[12,128,128]{2,1,0:T(8,128)(2,1)}, u32[]{:S(2)}, u32[]{:S(2)}) async-start(bf16[12,128,128]{2,1,0:T(8,128)(2,1)} %copy-done.5), calls=%async_computation.2 | async-start | bytes 786432 | tf_op jit(solution)/shard_map/sum_weights_z/all_to_all | solution.py:177
  123.7 1.1 copy-start.1
  136.7 32.0 %all-to-all-start.4 = ((bf16[8,128,128]{2,1,0:T(8,128)(2,1)}), bf16[8,128,128]{2,1,0:T(8,128)(2,1)S(1)}, u32[]{:S(2)}, u32[]{:S(2)}) async-start(bf16[8,128,128]{2,1,0:T(8,128)(2,1)} %get-tuple-element.21), calls=%async_computation.4 | async-start | bytes 524288 | tf_op jit(solution)/shard_map/gather_spread/all_to_all | solution.py:195

commit v3 on v2

v3 whole, which is shorter than its diff:
```python
import jax
import jax.numpy as jnp
from jax import lax
from jax.experimental import pallas as pl
from jax.experimental.pallas import tpu as pltpu
from jax.sharding import PartitionSpec as P

TILE = 128
NX, NZ, NC = 4, 12, 2
NREP = 8
LINE = NZ * NC
WIDE = LINE * TILE
PIECE = 24
CHUNK = NX * PIECE
ROOM = 32
BF16 = jnp.bfloat16
F32 = jnp.float32
VMEM_LIMIT = 14 * 1024 * 1024
ACROSS = (((0,), (0,)), ((), ()))
BY_ROWS = (((1,), (1,)), ((), ()))


def blk_index(x, z, c):
    return (x * NZ + z) * NC + c


Z_GROUPS = [[blk_index(x, z, c) for z in range(NZ)] for x in range(NX) for c in range(NC)]
X_GROUPS = [[blk_index(x, z, c) for x in range(NX)] for z in range(NZ) for c in range(NC)]
LINE_GROUPS = [[x * LINE + p for p in range(LINE)] for x in range(NX)]


def along_x(k):
    return [(x * LINE + p, (x + k) % NX * LINE + p) for x in range(NX) for p in range(LINE)]


def vmem():
    return pl.BlockSpec(memory_space=pltpu.VMEM)


def smem():
    return pl.BlockSpec(memory_space=pltpu.SMEM)


def call(kernel, out_shape, in_specs, flops, moved):
    return pl.pallas_call(
        kernel,
        out_shape=out_shape,
        in_specs=in_specs,
        out_specs=jax.tree.map(lambda _: vmem(), out_shape),
        compiler_params=pltpu.CompilerParams(vmem_limit_bytes=VMEM_LIMIT),
        cost_estimate=pl.CostEstimate(flops=flops, bytes_accessed=moved, transcendentals=0),
    )


def column_scale(degree_ref):
    inv_root = 1.0 / jnp.sqrt(degree_ref[...].astype(F32))
    return jnp.broadcast_to(inv_root, (TILE, TILE)).T


def scale_out_kernel(degree_ref, grad_out_ref, weight_out_ref, agg_hidden_ref, scaled_ref, weight_ref):
    delta = lax.dot_general(grad_out_ref[...], weight_out_ref[...], BY_ROWS, preferred_element_type=F32)
    scaled_ref[...] = (column_scale(degree_ref) * delta).astype(BF16)
    w_out = lax.dot_general(agg_hidden_ref[...], grad_out_ref[...], ACROSS, preferred_element_type=F32)
    for j in range(8):
        weight_ref[j * TILE : (j + 1) * TILE] = w_out[:, j * TILE : (j + 1) * TILE].astype(BF16)
    weight_ref[8 * TILE :] = jnp.zeros((NZ * CHUNK - 8 * TILE, TILE), BF16)


def turn_input_kernel(degree_ref, agg_input_ref, out_ref):
    root = jnp.sqrt(degree_ref[...].astype(F32))
    for j in range(4):
        rows = slice(j * TILE, (j + 1) * TILE)
        out_ref[rows] = (agg_input_ref[:, rows].astype(F32).T * root).astype(BF16)


def spread_tiles_kernel(x_ref, source_ref, count_ref, tiles_ref, *out_refs):
    for out_ref in out_refs:
        out_ref[...] = jnp.zeros_like(out_ref)

    def step(slot, carry):
        source = source_ref[0, slot]
        line = lax.div(source, LINE)
        columns = pl.ds(pl.multiple_of((source - line * LINE) * TILE, TILE), TILE)
        away = (line - x_ref[0] + NX) & (NX - 1)
        for k, out_ref in enumerate(out_refs):

            @pl.when(away == k)
            def _():
                out_ref[:, columns] = tiles_ref[0, slot]

        return carry

    lax.fori_loop(0, count_ref[0], step, 0)


def multiply(tiles_refs, blocks):
    return [jnp.dot(tiles_ref[...], blocks, preferred_element_type=F32).astype(BF16) for tiles_ref in tiles_refs]


def out_parts_kernel(x_ref, t0_ref, t1_ref, t2_ref, t3_ref, blocks_ref, weight_ref, out_ref):
    parts = multiply((t0_ref, t1_ref, t2_ref, t3_ref), blocks_ref[...])
    total = weight_ref[0].astype(F32)
    for j in range(1, NZ):
        total = total + weight_ref[j].astype(F32)
    for k in range(NX):
        out_ref[(x_ref[0] - k + NX) & (NX - 1), :TILE] = parts[k]
        piece = total[k * PIECE : (k + 1) * PIECE]
        piece = jnp.concatenate([piece, jnp.zeros((ROOM - PIECE, TILE), F32)], axis=0)
        out_ref[k, TILE:] = piece.astype(BF16)


def sum_lines(got_ref):
    return (got_ref[0].astype(F32) + got_ref[1].astype(F32)) + (got_ref[2].astype(F32) + got_ref[3].astype(F32))


def hidden_kernel(degree_ref, got_ref, pre_hidden_ref, out_ref):
    scale = column_scale(degree_ref)
    total = sum_lines(got_ref)
    grad_pre = jnp.where(pre_hidden_ref[...].astype(F32) > 0, scale * total[:TILE], 0.0).astype(BF16)
    out_ref[:TILE] = (scale * grad_pre.astype(F32)).astype(BF16)
    out_ref[TILE:] = total[TILE:].astype(BF16)


def pre_parts_kernel(x_ref, t0_ref, t1_ref, t2_ref, t3_ref, blocks_ref, turned_ref, out_ref, weight_ref):
    blocks = blocks_ref[:, :TILE].reshape(WIDE, TILE)
    parts = multiply((t0_ref, t1_ref, t2_ref, t3_ref), blocks)
    w_in = jnp.zeros((4 * TILE, TILE), F32)
    for p in range(0, LINE, 2):
        turned = jnp.concatenate([turned_ref[p], turned_ref[p + 1]], axis=1)
        w_in = w_in + jnp.dot(turned, blocks[p * TILE : (p + 2) * TILE], preferred_element_type=F32)
    for k in range(NX):
        out_ref[(x_ref[0] - k + NX) & (NX - 1), :TILE] = parts[k]
        out_ref[k, TILE:] = w_in[k * TILE : (k + 1) * TILE].astype(BF16)
    pieces = []
    for z in range(NZ):
        both = blocks_ref[2 * z, TILE:].astype(F32) + blocks_ref[2 * z + 1, TILE:].astype(F32)
        pieces.append(both[:PIECE])
    weight_ref[...] = jnp.concatenate(pieces, axis=0).astype(BF16)


def spread_kernel(degree_ref, got_ref, w_out_ref, spread_ref, weight_ref):
    total = sum_lines(got_ref)
    spread = (column_scale(degree_ref) * total[:TILE]).astype(BF16)
    for j in range(NREP):
        spread_ref[j] = spread
    weight_ref[: NZ * PIECE] = w_out_ref[...]
    weight_ref[NZ * PIECE :] = total[TILE:].astype(BF16)


def final_kernel(weights_ref, spread_ref, weight_in_ref, w_out_ref, w_in_ref, input_ref):
    for x in range(NX):
        weights = weights_ref[x].astype(F32)
        for z in range(NZ):
            row = z * CHUNK + x * PIECE
            at, left = z * PIECE, min(PIECE, 8 * TILE - row)
            while left > 0:
                j, r = row // TILE, row % TILE
                n = min(left, TILE - r)
                w_out_ref[r : r + n, j * TILE : (j + 1) * TILE] = weights[at : at + n]
                row, at, left = row + n, at + n, left - n
        w_in_ref[x * TILE : (x + 1) * TILE] = weights[NZ * PIECE :]
    total = jnp.zeros((TILE, 512), F32)
    for k in range(NREP):
        total = total + lax.dot_general(spread_ref[k], weight_in_ref[k], BY_ROWS, preferred_element_type=F32)
    input_ref[...] = total


def local(
    grad_out,
    agg_hidden,
    pre_hidden,
    agg_input,
    weight_in,
    weight_out,
    edge_tiles,
    tile_source,
    tile_count,
    degree,
):
    shape = jax.ShapeDtypeStruct
    block = shape((TILE, TILE), BF16)
    x = (lax.axis_index("blk") // LINE).astype(jnp.int32).reshape(1)
    degree = degree.reshape(1, TILE)

    with jax.named_scope("turn_input"):
        turned = call(turn_input_kernel, shape((4 * TILE, TILE), BF16), [vmem()] * 2, 300000, 300000)(degree, agg_input)
    with jax.named_scope("gather_input"):
        turned = lax.all_gather(turned, "blk", axis=0, tiled=False, axis_index_groups=LINE_GROUPS)
    with jax.named_scope("gather_weight_in"):
        weights_in = lax.all_gather(weight_in, "rep", axis=0, tiled=False)
    with jax.named_scope("spread_tiles"):
        tiles = call(
            spread_tiles_kernel, [shape((TILE, WIDE), BF16)] * NX, [smem()] * 3 + [vmem()], 1000000, 5000000
        )(x, tile_source, tile_count, edge_tiles)
    with jax.named_scope("exchange_tiles"):
        tiles = [tiles[0]] + [lax.ppermute(tiles[k], "blk", along_x(k)) for k in range(1, NX)]
    with jax.named_scope("scale_out"):
        scaled, weights = call(
            scale_out_kernel, [block, shape((NZ * CHUNK, TILE), BF16)], [vmem()] * 4, 4 * 128 * 128 * 1024, 900000
        )(degree, grad_out, weight_out, agg_hidden)
    with jax.named_scope("sum_weights_z"):
        weights = weights.reshape(NZ, CHUNK, TILE)
        weights = lax.all_to_all(weights, "blk", 0, 0, tiled=True, axis_index_groups=Z_GROUPS)
    with jax.named_scope("gather_out"):
        blocks = lax.all_gather(scaled, "blk", axis=0, tiled=True, axis_index_groups=LINE_GROUPS)
    with jax.named_scope("out_parts"):
        parts = call(
            out_parts_kernel,
            shape((NX, TILE + ROOM, TILE), BF16),
            [smem()] + [vmem()] * 6,
            2 * 512 * 3072 * 128,
            4000000,
        )(x, *tiles, blocks, weights)
    with jax.named_scope("sum_out_x"):
        parts = lax.all_to_all(parts, "blk", 0, 0, tiled=True, axis_index_groups=X_GROUPS)
    with jax.named_scope("hidden"):
        scaled = call(hidden_kernel, shape((TILE + ROOM, TILE), BF16), [vmem()] * 3, 1000000, 600000)(
            degree, parts, pre_hidden
        )
    with jax.named_scope("gather_pre"):
        blocks = lax.all_gather(scaled, "blk", axis=0, tiled=False, axis_index_groups=LINE_GROUPS)
    with jax.named_scope("pre_parts"):
        parts, w_out = call(
            pre_parts_kernel,
            [shape((NX, 2 * TILE, TILE), BF16), shape((NZ * PIECE, TILE), BF16)],
            [smem()] + [vmem()] * 6,
            4 * 512 * 3072 * 128,
            8000000,
        )(x, *tiles, blocks, turned)
    with jax.named_scope("sum_pre_x"):
        parts = lax.all_to_all(parts, "blk", 0, 0, tiled=True, axis_index_groups=X_GROUPS)
    parts, weights_in = lax.optimization_barrier((parts, weights_in))
    with jax.named_scope("spread"):
        spread, weights = call(
            spread_kernel,
            [shape((NREP, TILE, TILE), BF16), shape((NZ * PIECE + TILE, TILE), BF16)],
            [vmem()] * 3,
            500000,
            800000,
        )(degree, parts, w_out)
    with jax.named_scope("gather_spread"):
        spread = lax.all_to_all(spread, "rep", 0, 0, tiled=True)
    with jax.named_scope("gather_weights"):
        weights = lax.all_gather(weights, "blk", axis=0, tiled=False, axis_index_groups=X_GROUPS)
    with jax.named_scope("final"):
        return tuple(
            call(
                final_kernel,
                [shape((128, 1024), F32), shape((512, 128), F32), shape((128, 512), F32)],
                [vmem()] * 3,
                2 * 128 * 1024 * 512,
                2500000,
            )(weights, spread, weights_in)
        )


def solution(mesh):
    return jax.shard_map(
        local,
        mesh=mesh,
        in_specs=(
            P("blk", None),
            P("blk", "rep"),
            P("blk", "rep"),
            P("blk", None),
            P(None, "rep"),
            P("rep", None),
            P("blk", None, None, None),
            P("blk", None),
            P("blk"),
            P("blk"),
        ),
        out_specs=(P("rep", None), P(None, "rep"), P("blk", None)),
        check_vma=False,
    )
```

time: 171 us -> 165 us (0.965)
  the two profiles are of different devices: /device:TPU:1 before, /device:TPU:8 now
where the time goes in v3:
time: 165 us; the launch traced here: 164 us
  blocking collectives  80.8 us (49%)
  starting transfers between devices  36.8 us (22%)
  between operations  14.9 us (9%)
  local copies, waits for them, and re-layouts  13.5 us (8%)
  Pallas kernels  9.61 us (6%)
  waiting for transfers between devices  8.6 us (5%)
    all_gather x1, blocking collectives, local(): lax.all_gather(scaled, 'blk', axis=0, tiled=True, axis_index_groups=LINE_...  30.7 us
    all_gather x1, blocking collectives, local(): lax.all_gather(scaled, 'blk', axis=0, tiled=False, axis_index_groups=LINE...  27.1 us
    all_to_all x1, starting transfers between devices, local(): lax.all_to_all(weights, 'blk', 0, 0, tiled=True, axis_index_groups=Z_GROUPS)  15.2 us
    unnamed x32, local copies, waits for them, and re-layouts  13.5 us
    all_gather x1, blocking collectives, local(): lax.all_gather(weights, 'blk', axis=0, tiled=False, axis_index_groups=X_G...  13.1 us
    ppermute x3, starting transfers between devices, local(): lax.ppermute(tiles[k], 'blk', along_x(k))  10.6 us
    all_to_all x1, blocking collectives, local(): lax.all_to_all(parts, 'blk', 0, 0, tiled=True, axis_index_groups=X_GROUPS)  9.86 us
    all_to_all x1, starting transfers between devices, local(): spread = lax.all_to_all(spread, 'rep', 0, 0, tiled=True)  7.54 us
  transfers between devices with their start and end apart: 8, of which 2 were waited for; matrix products, arithmetic and copies ran while one was open for 0% of the time, Pallas kernels for 4%

profile of v3, /device:TPU:8, one launch (start us, length us, event | category | flops | bytes accessed | tf_op | source)
XLA Modules:
  0.0 164.2 jit_solution(17144966457340730836)
XLA Ops:
  7.2 0.0 all-gather.7.cloned.1.call-start
  7.2 0.9 copy-done.9
  8.1 0.7 copy-done.12
  8.8 0.8 turn_input.1
  9.5 0.0 all-gather.7.cloned.1.call-update
  9.6 0.0 all-gather.9.cloned.1.call-start
  9.6 0.7 all-gather.9.cloned.1.call-update
  10.3 0.0 copy-start.6
  10.3 0.9 copy-done.6
  11.3 0.9 copy-done.7
  12.2 0.8 copy-done.10
  13.0 0.7 copy-done.13
  13.6 1.0 scale_out.1
  14.7 15.2 %all-to-all-start = ((bf16[12,96,128]{2,1,0:T(8,128)(2,1)}), bf16[12,96,128]{2,1,0:T(8,128)(2,1)}, u32[]{:S(2)}, u32[]{:S(2)}) async-start(bf16[12,96,128]{2,1,0:T(8,128)(2,1)} %bitcast.2), calls=%async_computation | async-start | bytes 589824 | tf_op jit(solution)/shard_map/sum_weights_z/all_to_all | solution.py:203
  30.5 0.0 copy-start.4
  30.5 1.6 copy-done.4
  32.1 0.7 copy-done.15
  32.8 1.9 %spread_tiles.1 = (bf16[128,3072]{1,0:T(8,128)(2,1)S(1)}, bf16[128,3072]{1,0:T(8,128)(2,1)S(1)}, bf16[128,3072]{1,0:T(8,128)(2,1)S(1)}, bf16[128,3072]{1,0:T(8,128)(2,1)S(1)}) custom-call(s32[1]{0:T(128)} %bitcast.1.x_ref, s32[1,64]{1,0:T(1,128)S(1)} %copy-done.15, s32[1]{0:T(128)S(6)} %copy.13.count_ref, bf16[1,64,128,128]{3,2,1,0:T(8,128)(2,1)S(1)} %copy-done.4), custom_call_target="tpu_custom_call" | custom-call | flops 1000000 | bytes 5000000 | tf_op jit(solution)/shard_map/spread_tiles/pallas_call | solution.py:192
  34.6 0.0 copy-start.11
  34.7 0.0 copy-start.14
  34.7 3.1 %collective-permute-start = (bf16[128,3072]{1,0:T(8,128)(2,1)S(1)}, bf16[128,3072]{1,0:T(8,128)(2,1)S(1)}, u32[]{:S(2)}, u32[]{:S(2)}) collective-permute-start(bf16[128,3072]{1,0:T(8,128)(2,1)S(1)} %get-tuple-element.16), channel_id=1, source_target_pairs={{0,192},{8,200},{16,208},{24,216},{32,224},{40,232},{48,240},{56,2... | collective-permute-start | bytes 2359304 | tf_op jit(solution)/shard_map/exchange_tiles/ppermute | solution.py:196
  37.8 5.6 %collective-permute-start.1 = (bf16[128,3072]{1,0:T(8,128)(2,1)S(1)}, bf16[128,3072]{1,0:T(8,128)(2,1)S(1)}, u32[]{:S(2)}, u32[]{:S(2)}) collective-permute-start(bf16[128,3072]{1,0:T(8,128)(2,1)S(1)} %get-tuple-element.17), channel_id=1, source_target_pairs={{0,384},{8,392},{16,400},{24,408},{32,416},{40,424},{48,432},{56,4... | collective-permute-start | bytes 2359304 | tf_op jit(solution)/shard_map/exchange_tiles/ppermute | solution.py:196
  43.4 1.9 %collective-permute-start.2 = (bf16[128,3072]{1,0:T(8,128)(2,1)S(1)}, bf16[128,3072]{1,0:T(8,128)(2,1)S(1)}, u32[]{:S(2)}, u32[]{:S(2)}) collective-permute-start(bf16[128,3072]{1,0:T(8,128)(2,1)S(1)} %get-tuple-element.18), channel_id=1, source_target_pairs={{0,576},{8,584},{16,592},{24,600},{32,608},{40,616},{48,624},{56,6... | collective-permute-start | bytes 2359304 | tf_op jit(solution)/shard_map/exchange_tiles/ppermute | solution.py:196
  45.3 30.7 %all_gather.27.blocks_ref = bf16[3072,128]{1,0:T(8,128)(2,1)} all-gather(bf16[128,128]{1,0:T(8,128)(2,1)S(1)} %get-tuple-element.19), channel_id=1, replica_groups={{0,8,16,24,32,40,48,56,64,72,80,88,96,104,112,120,128,136,144,152,160,1..., dimensions={0}, use_global_device_ids=true | all-gather | bytes 819200 | tf_op jit(solution)/shard_map/gather_out/all_gather | solution.py:205
  76.0 0.0 collective-permute-done.t1_ref
  76.0 0.0 collective-permute-done.1.t2_ref
  76.0 0.5 collective-permute-done.2.t3_ref
  76.5 0.0 all-to-all-done.weight_ref
  76.5 1.4 copy-done.3
  77.9 2.0 %out_parts.1 = bf16[4,160,128]{2,1,0:T(8,128)(2,1)S(1)} custom-call(s32[1]{0:T(128)} %bitcast.1.x_ref, bf16[128,3072]{1,0:T(8,128)(2,1)S(1)} %get-tuple-element.15.t0_ref, bf16[128,3072]{1,0:T(8,128)(2,1)S(1)} %collective-permute-done.t1_ref, bf16[128,3072]{1,0:T(8,128)(2,1)S(1)} %collective-permute-done.1.t2_ref, ...), custom_call_target="tpu_custom_call" | custom-call | flops 402653184 | bytes 4000000 | tf_op jit(solution)/shard_map/out_parts/pallas_call | solution.py:207
  79.9 9.9 %all_to_all.20.got_ref = bf16[4,160,128]{2,1,0:T(8,128)(2,1)S(1)} all-to-all(bf16[4,160,128]{2,1,0:T(8,128)(2,1)S(1)} %out_parts.1), channel_id=1, replica_groups={{0,192,384,576},{8,200,392,584},{16,208,400,592},{24,216,408,600},{32,2..., dimensions={0} | all-to-all | bytes 327680 | tf_op jit(solution)/shard_map/sum_out_x/all_to_all | solution.py:215
  89.7 0.0 copy-done.11
  89.7 0.1 hidden.1
  89.9 27.1 %all-gather = bf16[3840,128]{1,0:T(8,128)(2,1)S(1)} all-gather(bf16[160,128]{1,0:T(8,128)(2,1)S(1)} %hidden.1), channel_id=2, replica_groups={{0,8,16,24,32,40,48,56,64,72,80,88,96,104,112,120,128,136,144,152,160,1..., dimensions={0}, use_global_device_ids=true | all-gather | bytes 1024000 | tf_op jit(solution)/shard_map/gather_pre/all_gather | solution.py:221
  117.0 1.9 %copy-done = bf16[12288,128]{1,0:T(8,128)(2,1)S(1)} copy-done((bf16[12288,128]{1,0:T(8,128)(2,1)S(1)}, bf16[12288,128]{1,0:T(8,128)(2,1)}, u32[]{:S(2)}) %copy-start) | copy-done | bytes 3145752
  118.9 1.1 copy-done.2
  120.0 1.8 %pre_parts.1 = (bf16[4,256,128]{2,1,0:T(8,128)(2,1)S(1)}, bf16[288,128]{1,0:T(8,128)(2,1)S(1)}) custom-call(s32[1]{0:T(128)} %bitcast.1.x_ref, bf16[128,3072]{1,0:T(8,128)(2,1)S(1)} %get-tuple-element.15.t0_ref, bf16[128,3072]{1,0:T(8,128)(2,1)S(1)} %collective-permute-done.t1_ref, bf16[128,3072]{1,0:T(8,128)(2,1)S(1)} %collective-permute-done.1.t2_ref, ...), custom_call_target="tpu_custom_call" | custom-call | flops 805306368 | bytes 8000000 | tf_op jit(solution)/shard_map/pre_parts/pallas_call | solution.py:223
  121.8 0.0 copy-start.8
  121.8 0.7 copy-done.8
  122.5 3.4 %all-to-all-start.2 = ((bf16[4,256,128]{2,1,0:T(8,128)(2,1)}), bf16[4,256,128]{2,1,0:T(8,128)(2,1)S(1)}, u32[]{:S(2)}, u32[]{:S(2)}) async-start(bf16[4,256,128]{2,1,0:T(8,128)(2,1)} %copy-done.8), calls=%async_computation.2 | async-start | bytes 524288 | tf_op jit(solution)/shard_map/sum_pre_x/all_to_all | solution.py:231
  125.9 0.0 all-gather.9.cloned.1.call-done
  126.0 7.4 %all-to-all-done.2.got_ref = bf16[4,256,128]{2,1,0:T(8,128)(2,1)S(1)} async-done(((bf16[4,256,128]{2,1,0:T(8,128)(2,1)}), bf16[4,256,128]{2,1,0:T(8,128)(2,1)S(1)}, u32[]{:S(2)}, u32[]{:S(2)}) %all-to-all-start.2) | async-done | bytes 262176 | tf_op jit(solution)/shard_map/sum_pre_x/all_to_all | solution.py:231
  133.3 0.8 spread.1
  134.2 7.5 %all-to-all-start.3 = ((bf16[8,128,128]{2,1,0:T(8,128)(2,1)}), bf16[8,128,128]{2,1,0:T(8,128)(2,1)S(1)}, u32[]{:S(2)}, u32[]{:S(2)}) async-start(bf16[8,128,128]{2,1,0:T(8,128)(2,1)} %get-tuple-element.25), calls=%async_computation.3 | async-start | bytes 524288 | tf_op jit(solution)/shard_map/gather_spread/all_to_all | solution.py:242
  141.7 13.1 %all-gather.3 = bf16[1664,128]{1,0:T(8,128)(2,1)S(1)} all-gather(bf16[416,128]{1,0:T(8,128)(2,1)S(1)} %get-tuple-element.24), channel_id=5, replica_groups={{0,192,384,576},{8,200,392,584},{16,208,400,592},{24,216,408,600},{32,2..., dimensions={0}, use_global_device_ids=true | all-gather | bytes 532480 | tf_op jit(solution)/shard_map/gather_weights/all_gather | solution.py:244
  154.8 0.0 all-to-all-done.3.spread_ref
  154.8 1.2 copy-done.5
  156.1 1.3 final.1
  (14 shorter events, 0.0 us)
Async XLA Ops:
  7.2 109.8 %all-gather.7.cloned.1.call-start = ((), (), s32[]{:S(2)}) async-start(), calls=%async_computation.4 | async-start | bytes 3276800 | tf_op jit(solution)/shard_map/gather_input/all_gather | solution.py:188
  7.2 0.9 copy-start.9
  8.1 0.7 copy-start.12
  9.6 116.4 %all-gather.9.cloned.1.call-start = ((), (), s32[]{:S(2)}) async-start(), calls=%async_computation.5 | async-start | bytes 1179648 | tf_op jit(solution)/shard_map/gather_weight_in/all_gather | solution.py:190
  10.3 1.0 copy-start.6
  11.3 0.9 copy-start.7
  12.2 0.8 copy-start.10
  13.0 0.7 copy-start.13
  14.7 61.8 %all-to-all-start = ((bf16[12,96,128]{2,1,0:T(8,128)(2,1)}), bf16[12,96,128]{2,1,0:T(8,128)(2,1)}, u32[]{:S(2)}, u32[]{:S(2)}) async-start(bf16[12,96,128]{2,1,0:T(8,128)(2,1)} %bitcast.2), calls=%async_computation | async-start | bytes 589824 | tf_op jit(solution)/shard_map/sum_weights_z/all_to_all | solution.py:203
  30.5 1.6 copy-start.4
  32.1 0.7 copy-start.15
  34.6 55.1 %copy-start.11 = (bf16[128,128]{1,0:T(8,128)(2,1)S(1)}, bf16[128,128]{1,0:T(8,128)(2,1)}, u32[]{:S(2)}) copy-start(bf16[128,128]{1,0:T(8,128)(2,1)} %pre_hidden_ref.1) | copy-start | bytes 98308
  34.7 55.1 %copy-start.14 = (s32[128]{0:T(128)S(1)}, s32[128]{0:T(128)}, u32[]{:S(2)}) copy-start(s32[128]{0:T(128)} %param.19) | copy-start | bytes 1540
  34.7 41.3 %collective-permute-start = (bf16[128,3072]{1,0:T(8,128)(2,1)S(1)}, bf16[128,3072]{1,0:T(8,128)(2,1)S(1)}, u32[]{:S(2)}, u32[]{:S(2)}) collective-permute-start(bf16[128,3072]{1,0:T(8,128)(2,1)S(1)} %get-tuple-element.16), channel_id=1, source_target_pairs={{0,192},{8,200},{16,208},{24,216},{32,224},{40,232},{48,240},{56,2... | collective-permute-start | bytes 2359304 | tf_op jit(solution)/shard_map/exchange_tiles/ppermute | solution.py:196
  37.8 38.2 %collective-permute-start.1 = (bf16[128,3072]{1,0:T(8,128)(2,1)S(1)}, bf16[128,3072]{1,0:T(8,128)(2,1)S(1)}, u32[]{:S(2)}, u32[]{:S(2)}) collective-permute-start(bf16[128,3072]{1,0:T(8,128)(2,1)S(1)} %get-tuple-element.17), channel_id=1, source_target_pairs={{0,384},{8,392},{16,400},{24,408},{32,416},{40,424},{48,432},{56,4... | collective-permute-start | bytes 2359304 | tf_op jit(solution)/shard_map/exchange_tiles/ppermute | solution.py:196
  43.4 33.1 %collective-permute-start.2 = (bf16[128,3072]{1,0:T(8,128)(2,1)S(1)}, bf16[128,3072]{1,0:T(8,128)(2,1)S(1)}, u32[]{:S(2)}, u32[]{:S(2)}) collective-permute-start(bf16[128,3072]{1,0:T(8,128)(2,1)S(1)} %get-tuple-element.18), channel_id=1, source_target_pairs={{0,576},{8,584},{16,592},{24,600},{32,608},{40,616},{48,624},{56,6... | collective-permute-start | bytes 2359304 | tf_op jit(solution)/shard_map/exchange_tiles/ppermute | solution.py:196
  76.5 13.2 %copy-start.1 = (bf16[128,3072]{1,0:T(8,128)(2,1)}, bf16[128,3072]{1,0:T(8,128)(2,1)S(1)}, u32[]{:S(2)}) copy-start(bf16[128,3072]{1,0:T(8,128)(2,1)S(1)} %collective-permute-done.2.t3_ref) | copy-start | bytes 2359300
  76.5 1.4 copy-start.3
  117.0 1.9 %copy-start = (bf16[12288,128]{1,0:T(8,128)(2,1)S(1)}, bf16[12288,128]{1,0:T(8,128)(2,1)}, u32[]{:S(2)}) copy-start(bf16[12288,128]{1,0:T(8,128)(2,1)} %all-gather.7.cloned.1.call-done) | copy-start | bytes 9437188
  118.9 1.1 copy-start.2
  121.8 0.7 copy-start.8
  122.5 10.8 %all-to-all-start.2 = ((bf16[4,256,128]{2,1,0:T(8,128)(2,1)}), bf16[4,256,128]{2,1,0:T(8,128)(2,1)S(1)}, u32[]{:S(2)}, u32[]{:S(2)}) async-start(bf16[4,256,128]{2,1,0:T(8,128)(2,1)} %copy-done.8), calls=%async_computation.2 | async-start | bytes 524288 | tf_op jit(solution)/shard_map/sum_pre_x/all_to_all | solution.py:231
  134.2 20.7 %all-to-all-start.3 = ((bf16[8,128,128]{2,1,0:T(8,128)(2,1)}), bf16[8,128,128]{2,1,0:T(8,128)(2,1)S(1)}, u32[]{:S(2)}, u32[]{:S(2)}) async-start(bf16[8,128,128]{2,1,0:T(8,128)(2,1)} %get-tuple-element.25), calls=%async_computation.3 | async-start | bytes 524288 | tf_op jit(solution)/shard_map/gather_spread/all_to_all | solution.py:242
  154.8 1.2 copy-start.5
Sparse Core Ops, SparseCore 0:
  11.0 69.9 all-gather.6
  83.4 41.2 all-gather.8

commit v4 on v3

--- a/solution.py
+++ b/solution.py
@@ -15,7 +15,7 @@
 ROOM = 32
 BF16 = jnp.bfloat16
 F32 = jnp.float32
-VMEM_LIMIT = 14 * 1024 * 1024
+MIB = 1024 * 1024
 ACROSS = (((0,), (0,)), ((), ()))
 BY_ROWS = (((1,), (1,)), ((), ()))
 
@@ -41,13 +41,18 @@
     return pl.BlockSpec(memory_space=pltpu.SMEM)
 
 
-def call(kernel, out_shape, in_specs, flops, moved):
+def hbm():
+    return pl.BlockSpec(memory_space=pltpu.HBM)
+
+
+def call(kernel, out_shape, in_specs, flops, moved, scratch=(), limit=14):
     return pl.pallas_call(
         kernel,
         out_shape=out_shape,
         in_specs=in_specs,
         out_specs=jax.tree.map(lambda _: vmem(), out_shape),
-        compiler_params=pltpu.CompilerParams(vmem_limit_bytes=VMEM_LIMIT),
+        scratch_shapes=scratch,
+        compiler_params=pltpu.CompilerParams(vmem_limit_bytes=limit * MIB),
         cost_estimate=pl.CostEstimate(flops=flops, bytes_accessed=moved, transcendentals=0),
     )
 
@@ -57,25 +62,55 @@
     return jnp.broadcast_to(inv_root, (TILE, TILE)).T
 
 
-def scale_out_kernel(degree_ref, grad_out_ref, weight_out_ref, agg_hidden_ref, scaled_ref, weight_ref):
-    delta = lax.dot_general(grad_out_ref[...], weight_out_ref[...], BY_ROWS, preferred_element_type=F32)
-    scaled_ref[...] = (column_scale(degree_ref) * delta).astype(BF16)
-    w_out = lax.dot_general(agg_hidden_ref[...], grad_out_ref[...], ACROSS, preferred_element_type=F32)
-    for j in range(8):
-        weight_ref[j * TILE : (j + 1) * TILE] = w_out[:, j * TILE : (j + 1) * TILE].astype(BF16)
+def start_kernel(
+    x_ref,
+    count_ref,
+    source_hbm,
+    degree_hbm,
+    grad_out_hbm,
+    weight_out_hbm,
+    agg_hidden_hbm,
+    agg_input_hbm,
+    tiles_hbm,
+    t0_ref,
+    t1_ref,
+    t2_ref,
+    t3_ref,
+    scaled_ref,
+    weight_ref,
+    turned_ref,
+    source_ref,
+    degree_ref,
+    grad_out_ref,
+    weight_out_ref,
+    agg_hidden_ref,
+    agg_input_ref,
+    tiles_ref,
+    sems,
+):
+    pairs = (
+        (source_hbm, source_ref),
+        (tiles_hbm, tiles_ref),
+        (degree_hbm, degree_ref),
+        (agg_input_hbm, agg_input_ref),
+        (grad_out_hbm, grad_out_ref),
+        (weight_out_hbm, weight_out_ref),
+        (agg_hidden_hbm, agg_hidden_ref),
+    )
+    copies = [pltpu.make_async_copy(there, here, sems.at[i]) for i, (there, here) in enumerate(pairs)]
+    for copy in copies:
+        copy.start()
+    out_refs = (t0_ref, t1_ref, t2_ref, t3_ref)
+    for out_ref in out_refs:
+        out_ref[...] = jnp.zeros_like(out_ref)
     weight_ref[8 * TILE :] = jnp.zeros((NZ * CHUNK - 8 * TILE, TILE), BF16)
-
-
-def turn_input_kernel(degree_ref, agg_input_ref, out_ref):
+    for copy in copies:
+        copy.wait()
+
     root = jnp.sqrt(degree_ref[...].astype(F32))
     for j in range(4):
         rows = slice(j * TILE, (j + 1) * TILE)
-        out_ref[rows] = (agg_input_ref[:, rows].astype(F32).T * root).astype(BF16)
-
-
-def spread_tiles_kernel(x_ref, source_ref, count_ref, tiles_ref, *out_refs):
-    for out_ref in out_refs:
-        out_ref[...] = jnp.zeros_like(out_ref)
+        turned_ref[rows] = (agg_input_ref[:, rows].astype(F32).T * root).astype(BF16)
 
     def step(slot, carry):
         source = source_ref[0, slot]
@@ -91,6 +126,11 @@
         return carry
 
     lax.fori_loop(0, count_ref[0], step, 0)
+    delta = lax.dot_general(grad_out_ref[...], weight_out_ref[...], BY_ROWS, preferred_element_type=F32)
+    scaled_ref[...] = (column_scale(degree_ref) * delta).astype(BF16)
+    w_out = lax.dot_general(agg_hidden_ref[...], grad_out_ref[...], ACROSS, preferred_element_type=F32)
+    for j in range(8):
+        weight_ref[j * TILE : (j + 1) * TILE] = w_out[:, j * TILE : (j + 1) * TILE].astype(BF16)
 
 
 def multiply(tiles_refs, blocks):
@@ -121,21 +161,27 @@
     out_ref[TILE:] = total[TILE:].astype(BF16)
 
 
-def pre_parts_kernel(x_ref, t0_ref, t1_ref, t2_ref, t3_ref, blocks_ref, turned_ref, out_ref, weight_ref):
+def pre_parts_kernel(
+    x_ref, t0_ref, t1_ref, t2_ref, t3_ref, blocks_ref, turned_hbm, out_ref, weight_ref, turned_ref, sem
+):
+    copy = pltpu.make_async_copy(turned_hbm, turned_ref, sem)
+    copy.start()
     blocks = blocks_ref[:, :TILE].reshape(WIDE, TILE)
     parts = multiply((t0_ref, t1_ref, t2_ref, t3_ref), blocks)
+    for k in range(NX):
+        out_ref[(x_ref[0] - k + NX) & (NX - 1), :TILE] = parts[k]
+    pieces = []
+    for z in range(NZ):
+        both = blocks_ref[2 * z, TILE:].astype(F32) + blocks_ref[2 * z + 1, TILE:].astype(F32)
+        pieces.append(both[:PIECE])
+    weight_ref[...] = jnp.concatenate(pieces, axis=0).astype(BF16)
+    copy.wait()
     w_in = jnp.zeros((4 * TILE, TILE), F32)
     for p in range(0, LINE, 2):
         turned = jnp.concatenate([turned_ref[p], turned_ref[p + 1]], axis=1)
         w_in = w_in + jnp.dot(turned, blocks[p * TILE : (p + 2) * TILE], preferred_element_type=F32)
     for k in range(NX):
-        out_ref[(x_ref[0] - k + NX) & (NX - 1), :TILE] = parts[k]
         out_ref[k, TILE:] = w_in[k * TILE : (k + 1) * TILE].astype(BF16)
-    pieces = []
-    for z in range(NZ):
-        both = blocks_ref[2 * z, TILE:].astype(F32) + blocks_ref[2 * z + 1, TILE:].astype(F32)
-        pieces.append(both[:PIECE])
-    weight_ref[...] = jnp.concatenate(pieces, axis=0).astype(BF16)
 
 
 def spread_kernel(degree_ref, got_ref, w_out_ref, spread_ref, weight_ref):
@@ -147,7 +193,9 @@
     weight_ref[NZ * PIECE :] = total[TILE:].astype(BF16)
 
 
-def final_kernel(weights_ref, spread_ref, weight_in_ref, w_out_ref, w_in_ref, input_ref):
+def final_kernel(weights_ref, spread_ref, weight_in_hbm, w_out_ref, w_in_ref, input_ref, weight_in_ref, sem):
+    copy = pltpu.make_async_copy(weight_in_hbm, weight_in_ref, sem)
+    copy.start()
     for x in range(NX):
         weights = weights_ref[x].astype(F32)
         for z in range(NZ):
@@ -159,6 +207,7 @@
                 w_out_ref[r : r + n, j * TILE : (j + 1) * TILE] = weights[at : at + n]
                 row, at, left = row + n, at + n, left - n
         w_in_ref[x * TILE : (x + 1) * TILE] = weights[NZ * PIECE :]
+    copy.wait()
     total = jnp.zeros((TILE, 512), F32)
     for k in range(NREP):
         total = total + lax.dot_general(spread_ref[k], weight_in_ref[k], BY_ROWS, preferred_element_type=F32)
@@ -182,22 +231,25 @@
     x = (lax.axis_index("blk") // LINE).astype(jnp.int32).reshape(1)
     degree = degree.reshape(1, TILE)
 
-    with jax.named_scope("turn_input"):
-        turned = call(turn_input_kernel, shape((4 * TILE, TILE), BF16), [vmem()] * 2, 300000, 300000)(degree, agg_input)
+    copied = [tile_source, degree, grad_out, weight_out, agg_hidden, agg_input, edge_tiles]
+    homes = [pltpu.SMEM] + [pltpu.VMEM] * 6
+    with jax.named_scope("start"):
+        *tiles, scaled, weights, turned = call(
+            start_kernel,
+            [shape((TILE, WIDE), BF16)] * NX
+            + [block, shape((NZ * CHUNK, TILE), BF16), shape((4 * TILE, TILE), BF16)],
+            [smem()] * 2 + [hbm()] * 7,
+            4 * 128 * 128 * 1024,
+            6000000,
+            [home(a.shape, a.dtype) for home, a in zip(homes, copied)] + [pltpu.SemaphoreType.DMA((7,))],
+            limit=56,
+        )(x, tile_count, *copied)
     with jax.named_scope("gather_input"):
         turned = lax.all_gather(turned, "blk", axis=0, tiled=False, axis_index_groups=LINE_GROUPS)
     with jax.named_scope("gather_weight_in"):
         weights_in = lax.all_gather(weight_in, "rep", axis=0, tiled=False)
-    with jax.named_scope("spread_tiles"):
-        tiles = call(
-            spread_tiles_kernel, [shape((TILE, WIDE), BF16)] * NX, [smem()] * 3 + [vmem()], 1000000, 5000000
-        )(x, tile_source, tile_count, edge_tiles)
     with jax.named_scope("exchange_tiles"):
         tiles = [tiles[0]] + [lax.ppermute(tiles[k], "blk", along_x(k)) for k in range(1, NX)]
-    with jax.named_scope("scale_out"):
-        scaled, weights = call(
-            scale_out_kernel, [block, shape((NZ * CHUNK, TILE), BF16)], [vmem()] * 4, 4 * 128 * 128 * 1024, 900000
-        )(degree, grad_out, weight_out, agg_hidden)
     with jax.named_scope("sum_weights_z"):
         weights = weights.reshape(NZ, CHUNK, TILE)
         weights = lax.all_to_all(weights, "blk", 0, 0, tiled=True, axis_index_groups=Z_GROUPS)
@@ -210,6 +262,7 @@
             [smem()] + [vmem()] * 6,
             2 * 512 * 3072 * 128,
             4000000,
+            limit=50,
         )(x, *tiles, blocks, weights)
     with jax.named_scope("sum_out_x"):
         parts = lax.all_to_all(parts, "blk", 0, 0, tiled=True, axis_index_groups=X_GROUPS)
@@ -223,13 +276,14 @@
         parts, w_out = call(
             pre_parts_kernel,
             [shape((NX, 2 * TILE, TILE), BF16), shape((NZ * PIECE, TILE), BF16)],
-            [smem()] + [vmem()] * 6,
+            [smem()] + [vmem()] * 5 + [hbm()],
             4 * 512 * 3072 * 128,
             8000000,
+            [pltpu.VMEM((LINE, 4 * TILE, TILE), BF16), pltpu.SemaphoreType.DMA],
+            limit=50,
         )(x, *tiles, blocks, turned)
     with jax.named_scope("sum_pre_x"):
         parts = lax.all_to_all(parts, "blk", 0, 0, tiled=True, axis_index_groups=X_GROUPS)
-    parts, weights_in = lax.optimization_barrier((parts, weights_in))
     with jax.named_scope("spread"):
         spread, weights = call(
             spread_kernel,
@@ -247,9 +301,11 @@
             call(
                 final_kernel,
                 [shape((128, 1024), F32), shape((512, 128), F32), shape((128, 512), F32)],
-                [vmem()] * 3,
+                [vmem()] * 2 + [hbm()],
                 2 * 128 * 1024 * 512,
                 2500000,
+                [pltpu.VMEM((NREP, 4 * TILE, TILE), BF16), pltpu.SemaphoreType.DMA],
+                limit=56,
             )(weights, spread, weights_in)
         )
 

time: 165 us -> 161 us (0.976)
  local copies, waits for them, and re-layouts: 13.5 us -> 1.86 us
  blocking collectives: 80.8 us -> 91.4 us
  waiting for transfers between devices: 8.6 us -> 1.42 us
  Pallas kernels: 9.61 us -> 16.1 us
  starting transfers between devices: 36.8 us -> 34.4 us
    unnamed x32 -> x10, local copies, waits for them, and re-layouts: 13.5 us -> 1.86 us
    all_to_all x1 -> x2, blocking collectives: 9.86 us -> 19.7 us  [local(): lax.all_to_all(parts, 'blk', 0, 0, tiled=True, axis_index_groups=X_GROUPS)]
    all_to_all x1 -> x0, waiting for transfers between devices: 7.38 us -> none  [local(): lax.all_to_all(parts, 'blk', 0, 0, tiled=True, axis_index_groups=X_GROUPS)]
    all_to_all x1 -> x0, starting transfers between devices: 3.41 us -> none  [local(): lax.all_to_all(parts, 'blk', 0, 0, tiled=True, axis_index_groups=X_GROUPS)]
    pallas_call x1, Pallas kernels: 1.78 us -> 4.96 us  [local(): call(pre_parts_kernel, [shape((NX, 2 * TILE, TILE), BF16), shape((NZ * PI...]
    pallas_call x1, Pallas kernels: 1.28 us -> 3.45 us  [local(): call(final_kernel, [shape((128, 1024), F32), shape((512, 128), F32), shap...]
    pallas_call x3 -> x1, Pallas kernels: 3.66 us -> 4.59 us  [local(): call(start_kernel, [shape((TILE, WIDE), BF16)] * NX + [block, shape((NZ *...]
  transfers between devices with their start and end apart: 8 -> 7, of which waited for: 2 -> 1; matrix products, arithmetic and copies ran while one was open for 0% -> 0% of each run, Pallas kernels for 4% -> 5%
where the time goes in v4:
time: 161 us; the launch traced here: 160 us
  blocking collectives  91.4 us (57%)
  starting transfers between devices  34.4 us (21%)
  Pallas kernels  16.1 us (10%)
  between operations  14.8 us (9%)
  local copies, waits for them, and re-layouts  1.86 us (1%)
    all_gather x1, blocking collectives, local(): lax.all_gather(scaled, 'blk', axis=0, tiled=True, axis_index_groups=LINE_...  29.2 us
    all_gather x1, blocking collectives, local(): lax.all_gather(scaled, 'blk', axis=0, tiled=False, axis_index_groups=LINE...  28.6 us
    all_to_all x2, blocking collectives, local(): lax.all_to_all(parts, 'blk', 0, 0, tiled=True, axis_index_groups=X_GROUPS)  19.7 us
    all_to_all x1, starting transfers between devices, local(): lax.all_to_all(weights, 'blk', 0, 0, tiled=True, axis_index_groups=Z_GROUPS)  15.7 us
    all_gather x1, blocking collectives, local(): lax.all_gather(weights, 'blk', axis=0, tiled=False, axis_index_groups=X_G...  13.8 us
    ppermute x3, starting transfers between devices, local(): lax.ppermute(tiles[k], 'blk', along_x(k))  11.1 us
    all_to_all x1, starting transfers between devices, local(): spread = lax.all_to_all(spread, 'rep', 0, 0, tiled=True)  7.55 us
    pallas_call x1, Pallas kernels, local(): call(pre_parts_kernel, [shape((NX, 2 * TILE, TILE), BF16), shape((NZ * PI...  4.96 us
  transfers between devices with their start and end apart: 7, of which 1 were waited for; matrix products, arithmetic and copies ran while one was open for 0% of the time, Pallas kernels for 5%

profile of v4, /device:TPU:8, one launch (start us, length us, event | category | flops | bytes accessed | tf_op | source)
XLA Modules:
  0.0 160.0 jit_solution(5001294438962936082)
XLA Ops:
  7.2 0.0 all-gather.7.cloned.1.call-start
  7.9 4.6 %start.1 = (bf16[128,3072]{1,0:T(8,128)(2,1)}, bf16[128,3072]{1,0:T(8,128)(2,1)}, bf16[128,3072]{1,0:T(8,128)(2,1)}, bf16[128,3072]{1,0:T(8,128)(2,1)}, bf16[128...) custom-call(s32[1]{0:T(128)} %bitcast.1.x_ref, s32[1]{0:T(128)S(6)} %copy.13.count_ref, ...), custom_call_target="tpu_custom_call" | custom-call | flops 67108864 | bytes 6000000 | tf_op jit(solution)/shard_map/start/pallas_call | solution.py:237
  12.5 0.0 all-gather.7.cloned.1.call-update
  12.5 0.0 copy-start.2
  12.5 0.0 copy-start.3
  12.5 15.7 %all-to-all-start = ((bf16[12,96,128]{2,1,0:T(8,128)(2,1)}), bf16[12,96,128]{2,1,0:T(8,128)(2,1)S(1)}, u32[]{:S(2)}, u32[]{:S(2)}) async-start(bf16[12,96,128]{2,1,0:T(8,128)(2,1)} %bitcast.14), calls=%async_computation | async-start | bytes 589824 | tf_op jit(solution)/shard_map/sum_weights_z/all_to_all | solution.py:255
  28.2 0.0 all-gather.9.cloned.1.call-start
  28.3 2.0 %collective-permute-start = (bf16[128,3072]{1,0:T(8,128)(2,1)}, bf16[128,3072]{1,0:T(8,128)(2,1)S(1)}, u32[]{:S(2)}, u32[]{:S(2)}) collective-permute-start(bf16[128,3072]{1,0:T(8,128)(2,1)} %get-tuple-element.15), channel_id=1, source_target_pairs={{0,192},{8,200},{16,208},{24,216},{32,224},{40,232},{48,240},{56,2... | collective-permute-start | bytes 2359304 | tf_op jit(solution)/shard_map/exchange_tiles/ppermute | solution.py:252
  30.3 5.5 %collective-permute-start.1 = (bf16[128,3072]{1,0:T(8,128)(2,1)}, bf16[128,3072]{1,0:T(8,128)(2,1)S(1)}, u32[]{:S(2)}, u32[]{:S(2)}) collective-permute-start(bf16[128,3072]{1,0:T(8,128)(2,1)} %get-tuple-element.16), channel_id=1, source_target_pairs={{0,384},{8,392},{16,400},{24,408},{32,416},{40,424},{48,432},{56,4... | collective-permute-start | bytes 2359304 | tf_op jit(solution)/shard_map/exchange_tiles/ppermute | solution.py:252
  35.8 3.6 %collective-permute-start.2 = (bf16[128,3072]{1,0:T(8,128)(2,1)}, bf16[128,3072]{1,0:T(8,128)(2,1)S(1)}, u32[]{:S(2)}, u32[]{:S(2)}) collective-permute-start(bf16[128,3072]{1,0:T(8,128)(2,1)} %get-tuple-element.17), channel_id=1, source_target_pairs={{0,576},{8,584},{16,592},{24,600},{32,608},{40,616},{48,624},{56,6... | collective-permute-start | bytes 2359304 | tf_op jit(solution)/shard_map/exchange_tiles/ppermute | solution.py:252
  39.4 0.0 all-gather.9.cloned.1.call-update
  39.4 0.0 copy-start.1
  39.5 29.2 %all_gather.27.blocks_ref = bf16[3072,128]{1,0:T(8,128)(2,1)} all-gather(bf16[128,128]{1,0:T(8,128)(2,1)} %get-tuple-element.18), channel_id=1, replica_groups={{0,8,16,24,32,40,48,56,64,72,80,88,96,104,112,120,128,136,144,152,160,1..., dimensions={0}, use_global_device_ids=true | all-gather | bytes 819200 | tf_op jit(solution)/shard_map/gather_out/all_gather | solution.py:257
  68.7 0.0 collective-permute-done.t1_ref
  68.7 0.0 collective-permute-done.1.t2_ref
  68.7 1.4 collective-permute-done.2.t3_ref
  70.1 0.0 all-to-all-done.weight_ref
  70.1 0.0 copy-start
  70.1 1.1 copy-done
  71.2 2.2 %out_parts.1 = bf16[4,160,128]{2,1,0:T(8,128)(2,1)S(1)} custom-call(s32[1]{0:T(128)} %bitcast.1.x_ref, bf16[128,3072]{1,0:T(8,128)(2,1)S(1)} %copy-done, bf16[128,3072]{1,0:T(8,128)(2,1)S(1)} %collective-permute-done.t1_ref, bf16[128,3072]{1,0:T(8,128)(2,1)S(1)} %collective-permute-done.1.t2_ref, bf16[128,3072]{1,0:T(8,128)(2,1)S(1)} %collective-permute-done.2.t3_ref, ...), custom_call_target="tpu_custom_call" | custom-call | flops 402653184 | bytes 4000000 | tf_op jit(solution)/shard_map/out_parts/pallas_call | solution.py:259
  73.4 9.9 %all_to_all.20.got_ref = bf16[4,160,128]{2,1,0:T(8,128)(2,1)S(1)} all-to-all(bf16[4,160,128]{2,1,0:T(8,128)(2,1)S(1)} %out_parts.1), channel_id=1, replica_groups={{0,192,384,576},{8,200,392,584},{16,208,400,592},{24,216,408,600},{32,2..., dimensions={0} | all-to-all | bytes 327680 | tf_op jit(solution)/shard_map/sum_out_x/all_to_all | solution.py:268
  83.2 0.0 copy-done.2
  83.2 0.0 copy-done.3
  83.2 0.1 hidden.1
  83.4 28.6 %all-gather = bf16[3840,128]{1,0:T(8,128)(2,1)} all-gather(bf16[160,128]{1,0:T(8,128)(2,1)S(1)} %hidden.1), channel_id=2, replica_groups={{0,8,16,24,32,40,48,56,64,72,80,88,96,104,112,120,128,136,144,152,160,1..., dimensions={0}, use_global_device_ids=true | all-gather | bytes 1024000 | tf_op jit(solution)/shard_map/gather_pre/all_gather | solution.py:274
  112.0 0.0 all-gather.7.cloned.1.call-done
  112.0 0.0 copy-done.1
  112.0 5.0 %pre_parts.1 = (bf16[4,256,128]{2,1,0:T(8,128)(2,1)S(1)}, bf16[288,128]{1,0:T(8,128)(2,1)S(1)}) custom-call(s32[1]{0:T(128)} %bitcast.1.x_ref, bf16[128,3072]{1,0:T(8,128)(2,1)S(1)} %copy-done.1, bf16[128,3072]{1,0:T(8,128)(2,1)S(1)} %collective-permute-done.t1_ref, bf16[128,3072]{1,0:T(8,128)(2,1)S(1)} %collective-permute-done.1.t2_ref, ...), custom_call_target="tpu_custom_call" | custom-call | flops 805306368 | bytes 8000000 | tf_op jit(solution)/shard_map/pre_parts/pallas_call | solution.py:276
  116.9 9.9 %all_to_all.21.got_ref = bf16[4,256,128]{2,1,0:T(8,128)(2,1)S(1)} all-to-all(bf16[4,256,128]{2,1,0:T(8,128)(2,1)S(1)} %get-tuple-element.21), channel_id=1, replica_groups={{0,192,384,576},{8,200,392,584},{16,208,400,592},{24,216,408,600},{32,2..., dimensions={0} | all-to-all | bytes 524288 | tf_op jit(solution)/shard_map/sum_pre_x/all_to_all | solution.py:286
  126.8 0.8 spread.1
  127.6 7.6 %all-to-all-start.3 = ((bf16[8,128,128]{2,1,0:T(8,128)(2,1)}), bf16[8,128,128]{2,1,0:T(8,128)(2,1)S(1)}, u32[]{:S(2)}, u32[]{:S(2)}) async-start(bf16[8,128,128]{2,1,0:T(8,128)(2,1)} %get-tuple-element.24), calls=%async_computation.3 | async-start | bytes 524288 | tf_op jit(solution)/shard_map/gather_spread/all_to_all | solution.py:296
  135.2 13.8 %all-gather.2 = bf16[1664,128]{1,0:T(8,128)(2,1)} all-gather(bf16[416,128]{1,0:T(8,128)(2,1)S(1)} %get-tuple-element.23), channel_id=4, replica_groups={{0,192,384,576},{8,200,392,584},{16,208,400,592},{24,216,408,600},{32,2..., dimensions={0}, use_global_device_ids=true | all-gather | bytes 532480 | tf_op jit(solution)/shard_map/gather_weights/all_gather | solution.py:298
  149.0 0.0 all-gather.9.cloned.1.call-done
  149.0 0.0 all-to-all-done.3.spread_ref
  149.0 0.0 copy-start.4
  149.0 0.7 copy-done.4
  149.7 3.4 %final.1 = (f32[128,1024]{1,0:T(8,128)}, f32[512,128]{1,0:T(8,128)}, f32[128,512]{1,0:T(8,128)}) custom-call(bf16[4,416,128]{2,1,0:T(8,128)(2,1)} %bitcast.12, bf16[8,128,128]{2,1,0:T(8,128)(2,1)} %copy-done.4, bf16[8,512,128]{2,1,0:T(8,128)(2,1)} %bitcast.13), custom_call_target="tpu_custom_call" | custom-call | flops 134217728 | bytes 2500000 | tf_op jit(solution)/shard_map/final/pallas_call | solution.py:301
Async XLA Ops:
  7.2 104.8 %all-gather.7.cloned.1.call-start = ((), (), s32[]{:S(2)}) async-start(), calls=%async_computation.4 | async-start | bytes 3276800 | tf_op jit(solution)/shard_map/gather_input/all_gather | solution.py:248
  12.5 70.7 %copy-start.2 = (bf16[128,128]{1,0:T(8,128)(2,1)S(1)}, bf16[128,128]{1,0:T(8,128)(2,1)}, u32[]{:S(2)}) copy-start(bf16[128,128]{1,0:T(8,128)(2,1)} %pre_hidden_ref.1) | copy-start | bytes 98308
  12.5 70.7 %copy-start.3 = (s32[128]{0:T(128)S(1)}, s32[128]{0:T(128)}, u32[]{:S(2)}) copy-start(s32[128]{0:T(128)} %param.19) | copy-start | bytes 1540
  12.5 57.5 %all-to-all-start = ((bf16[12,96,128]{2,1,0:T(8,128)(2,1)}), bf16[12,96,128]{2,1,0:T(8,128)(2,1)S(1)}, u32[]{:S(2)}, u32[]{:S(2)}) async-start(bf16[12,96,128]{2,1,0:T(8,128)(2,1)} %bitcast.14), calls=%async_computation | async-start | bytes 589824 | tf_op jit(solution)/shard_map/sum_weights_z/all_to_all | solution.py:255
  28.2 120.8 %all-gather.9.cloned.1.call-start = ((), (), s32[]{:S(2)}) async-start(), calls=%async_computation.5 | async-start | bytes 1179648 | tf_op jit(solution)/shard_map/gather_weight_in/all_gather | solution.py:250
  28.3 40.4 %collective-permute-start = (bf16[128,3072]{1,0:T(8,128)(2,1)}, bf16[128,3072]{1,0:T(8,128)(2,1)S(1)}, u32[]{:S(2)}, u32[]{:S(2)}) collective-permute-start(bf16[128,3072]{1,0:T(8,128)(2,1)} %get-tuple-element.15), channel_id=1, source_target_pairs={{0,192},{8,200},{16,208},{24,216},{32,224},{40,232},{48,240},{56,2... | collective-permute-start | bytes 2359304 | tf_op jit(solution)/shard_map/exchange_tiles/ppermute | solution.py:252
  30.3 38.4 %collective-permute-start.1 = (bf16[128,3072]{1,0:T(8,128)(2,1)}, bf16[128,3072]{1,0:T(8,128)(2,1)S(1)}, u32[]{:S(2)}, u32[]{:S(2)}) collective-permute-start(bf16[128,3072]{1,0:T(8,128)(2,1)} %get-tuple-element.16), channel_id=1, source_target_pairs={{0,384},{8,392},{16,400},{24,408},{32,416},{40,424},{48,432},{56,4... | collective-permute-start | bytes 2359304 | tf_op jit(solution)/shard_map/exchange_tiles/ppermute | solution.py:252
  35.8 34.3 %collective-permute-start.2 = (bf16[128,3072]{1,0:T(8,128)(2,1)}, bf16[128,3072]{1,0:T(8,128)(2,1)S(1)}, u32[]{:S(2)}, u32[]{:S(2)}) collective-permute-start(bf16[128,3072]{1,0:T(8,128)(2,1)} %get-tuple-element.17), channel_id=1, source_target_pairs={{0,576},{8,584},{16,592},{24,600},{32,608},{40,616},{48,624},{56,6... | collective-permute-start | bytes 2359304 | tf_op jit(solution)/shard_map/exchange_tiles/ppermute | solution.py:252
  39.4 72.5 %copy-start.1 = (bf16[128,3072]{1,0:T(8,128)(2,1)S(1)}, bf16[128,3072]{1,0:T(8,128)(2,1)}, u32[]{:S(2)}) copy-start(bf16[128,3072]{1,0:T(8,128)(2,1)} %get-tuple-element.14.t0_ref) | copy-start | bytes 2359300
  70.1 1.1 copy-start
  127.6 21.4 %all-to-all-start.3 = ((bf16[8,128,128]{2,1,0:T(8,128)(2,1)}), bf16[8,128,128]{2,1,0:T(8,128)(2,1)S(1)}, u32[]{:S(2)}, u32[]{:S(2)}) async-start(bf16[8,128,128]{2,1,0:T(8,128)(2,1)} %get-tuple-element.24), calls=%async_computation.3 | async-start | bytes 524288 | tf_op jit(solution)/shard_map/gather_spread/all_to_all | solution.py:296
  149.0 0.7 copy-start.4
Sparse Core Ops, SparseCore 0:
  12.6 68.0 all-gather.6
  83.1 41.3 all-gather.8

commit v5 on v4

--- a/solution.py
+++ b/solution.py
@@ -133,20 +133,40 @@
         weight_ref[j * TILE : (j + 1) * TILE] = w_out[:, j * TILE : (j + 1) * TILE].astype(BF16)
 
 
+def copy_in(pairs, parts, sems):
+    started, at = [], 0
+    for there, here in pairs:
+        n = here.shape[0] // parts
+        copies = []
+        for i in range(parts):
+            rows = pl.ds(i * n, n)
+            copies.append(pltpu.make_async_copy(there.at[rows], here.at[rows], sems.at[at]))
+            copies[-1].start()
+            at += 1
+        started.append(copies)
+    return started
+
+
 def multiply(tiles_refs, blocks):
     return [jnp.dot(tiles_ref[...], blocks, preferred_element_type=F32).astype(BF16) for tiles_ref in tiles_refs]
 
 
-def out_parts_kernel(x_ref, t0_ref, t1_ref, t2_ref, t3_ref, blocks_ref, weight_ref, out_ref):
-    parts = multiply((t0_ref, t1_ref, t2_ref, t3_ref), blocks_ref[...])
+def out_parts_kernel(
+    x_ref, t0_hbm, t1_ref, t2_ref, t3_ref, blocks_hbm, weight_ref, out_ref, blocks_ref, t0_ref, sems
+):
+    got, first = copy_in(((blocks_hbm, blocks_ref), (t0_hbm, t0_ref)), 4, sems)
     total = weight_ref[0].astype(F32)
     for j in range(1, NZ):
         total = total + weight_ref[j].astype(F32)
     for k in range(NX):
-        out_ref[(x_ref[0] - k + NX) & (NX - 1), :TILE] = parts[k]
         piece = total[k * PIECE : (k + 1) * PIECE]
         piece = jnp.concatenate([piece, jnp.zeros((ROOM - PIECE, TILE), F32)], axis=0)
         out_ref[k, TILE:] = piece.astype(BF16)
+    for copy in got + first:
+        copy.wait()
+    parts = multiply((t0_ref, t1_ref, t2_ref, t3_ref), blocks_ref[...])
+    for k in range(NX):
+        out_ref[(x_ref[0] - k + NX) & (NX - 1), :TILE] = parts[k]
 
 
 def sum_lines(got_ref):
@@ -162,10 +182,22 @@
 
 
 def pre_parts_kernel(
-    x_ref, t0_ref, t1_ref, t2_ref, t3_ref, blocks_ref, turned_hbm, out_ref, weight_ref, turned_ref, sem
+    x_ref,
+    t0_ref,
+    t1_ref,
+    t2_ref,
+    t3_ref,
+    blocks_hbm,
+    turned_hbm,
+    out_ref,
+    weight_ref,
+    blocks_ref,
+    turned_ref,
+    sems,
 ):
-    copy = pltpu.make_async_copy(turned_hbm, turned_ref, sem)
-    copy.start()
+    got, turned_parts = copy_in(((blocks_hbm, blocks_ref), (turned_hbm, turned_ref)), 6, sems)
+    for copy in got:
+        copy.wait()
     blocks = blocks_ref[:, :TILE].reshape(WIDE, TILE)
     parts = multiply((t0_ref, t1_ref, t2_ref, t3_ref), blocks)
     for k in range(NX):
@@ -175,11 +207,11 @@
         both = blocks_ref[2 * z, TILE:].astype(F32) + blocks_ref[2 * z + 1, TILE:].astype(F32)
         pieces.append(both[:PIECE])
     weight_ref[...] = jnp.concatenate(pieces, axis=0).astype(BF16)
-    copy.wait()
     w_in = jnp.zeros((4 * TILE, TILE), F32)
-    for p in range(0, LINE, 2):
-        turned = jnp.concatenate([turned_ref[p], turned_ref[p + 1]], axis=1)
-        w_in = w_in + jnp.dot(turned, blocks[p * TILE : (p + 2) * TILE], preferred_element_type=F32)
+    for p in range(0, LINE, 4):
+        turned_parts[p // 4].wait()
+        turned = jnp.concatenate([turned_ref[p + i] for i in range(4)], axis=1)
+        w_in = w_in + jnp.dot(turned, blocks[p * TILE : (p + 4) * TILE], preferred_element_type=F32)
     for k in range(NX):
         out_ref[k, TILE:] = w_in[k * TILE : (k + 1) * TILE].astype(BF16)
 
@@ -193,9 +225,8 @@
     weight_ref[NZ * PIECE :] = total[TILE:].astype(BF16)
 
 
-def final_kernel(weights_ref, spread_ref, weight_in_hbm, w_out_ref, w_in_ref, input_ref, weight_in_ref, sem):
-    copy = pltpu.make_async_copy(weight_in_hbm, weight_in_ref, sem)
-    copy.start()
+def final_kernel(weights_ref, spread_ref, weight_in_hbm, w_out_ref, w_in_ref, input_ref, weight_in_ref, sems):
+    (parts,) = copy_in(((weight_in_hbm, weight_in_ref),), NREP, sems)
     for x in range(NX):
         weights = weights_ref[x].astype(F32)
         for z in range(NZ):
@@ -207,9 +238,9 @@
                 w_out_ref[r : r + n, j * TILE : (j + 1) * TILE] = weights[at : at + n]
                 row, at, left = row + n, at + n, left - n
         w_in_ref[x * TILE : (x + 1) * TILE] = weights[NZ * PIECE :]
-    copy.wait()
     total = jnp.zeros((TILE, 512), F32)
     for k in range(NREP):
+        parts[k].wait()
         total = total + lax.dot_general(spread_ref[k], weight_in_ref[k], BY_ROWS, preferred_element_type=F32)
     input_ref[...] = total
 
@@ -259,9 +290,10 @@
         parts = call(
             out_parts_kernel,
             shape((NX, TILE + ROOM, TILE), BF16),
-            [smem()] + [vmem()] * 6,
+            [smem(), hbm()] + [vmem()] * 3 + [hbm(), vmem()],
             2 * 512 * 3072 * 128,
             4000000,
+            [pltpu.VMEM((WIDE, TILE), BF16), pltpu.VMEM((TILE, WIDE), BF16), pltpu.SemaphoreType.DMA((8,))],
             limit=50,
         )(x, *tiles, blocks, weights)
     with jax.named_scope("sum_out_x"):
@@ -276,10 +308,14 @@
         parts, w_out = call(
             pre_parts_kernel,
             [shape((NX, 2 * TILE, TILE), BF16), shape((NZ * PIECE, TILE), BF16)],
-            [smem()] + [vmem()] * 5 + [hbm()],
+            [smem()] + [vmem()] * 4 + [hbm()] * 2,
             4 * 512 * 3072 * 128,
             8000000,
-            [pltpu.VMEM((LINE, 4 * TILE, TILE), BF16), pltpu.SemaphoreType.DMA],
+            [
+                pltpu.VMEM((LINE, TILE + ROOM, TILE), BF16),
+                pltpu.VMEM((LINE, 4 * TILE, TILE), BF16),
+                pltpu.SemaphoreType.DMA((12,)),
+            ],
             limit=50,
         )(x, *tiles, blocks, turned)
     with jax.named_scope("sum_pre_x"):
@@ -304,7 +340,7 @@
                 [vmem()] * 2 + [hbm()],
                 2 * 128 * 1024 * 512,
                 2500000,
-                [pltpu.VMEM((NREP, 4 * TILE, TILE), BF16), pltpu.SemaphoreType.DMA],
+                [pltpu.VMEM((NREP, 4 * TILE, TILE), BF16), pltpu.SemaphoreType.DMA((NREP,))],
                 limit=56,
             )(weights, spread, weights_in)
         )

time: 161 us -> 160 us (level)
  no operation moved by 1% of the time
where the time goes in v5:
time: 160 us; the launch traced here: 159 us
  blocking collectives  92 us (58%)
  starting transfers between devices  34.1 us (21%)
  Pallas kernels  16.4 us (10%)
  between operations  14.8 us (9%)
  local copies, waits for them, and re-layouts  1.87 us (1%)
    all_gather x1, blocking collectives, local(): lax.all_gather(scaled, 'blk', axis=0, tiled=True, axis_index_groups=LINE_...  29.8 us
    all_gather x1, blocking collectives, local(): lax.all_gather(scaled, 'blk', axis=0, tiled=False, axis_index_groups=LINE...  28.6 us
    all_to_all x2, blocking collectives, local(): lax.all_to_all(parts, 'blk', 0, 0, tiled=True, axis_index_groups=X_GROUPS)  19.7 us
    all_to_all x1, starting transfers between devices, local(): lax.all_to_all(weights, 'blk', 0, 0, tiled=True, axis_index_groups=Z_GROUPS)  15 us
    all_gather x1, blocking collectives, local(): lax.all_gather(weights, 'blk', axis=0, tiled=False, axis_index_groups=X_G...  13.9 us
    ppermute x3, starting transfers between devices, local(): lax.ppermute(tiles[k], 'blk', along_x(k))  11.5 us
    all_to_all x1, starting transfers between devices, local(): spread = lax.all_to_all(spread, 'rep', 0, 0, tiled=True)  7.55 us
    pallas_call x1, Pallas kernels, local(): call(start_kernel, [shape((TILE, WIDE), BF16)] * NX + [block, shape((NZ *...  5.08 us
  transfers between devices with their start and end apart: 7, of which 1 were waited for; matrix products, arithmetic and copies ran while one was open for 0% of the time, Pallas kernels for 5%

profile of v5, /device:TPU:8, one launch (start us, length us, event | category | flops | bytes accessed | tf_op | source)
XLA Modules:
  0.0 159.4 jit_solution(203748544594513399)
XLA Ops:
  7.2 0.0 all-gather.7.cloned.1.call-start
  7.9 5.1 %start.1 = (bf16[128,3072]{1,0:T(8,128)(2,1)}, bf16[128,3072]{1,0:T(8,128)(2,1)}, bf16[128,3072]{1,0:T(8,128)(2,1)}, bf16[128,3072]{1,0:T(8,128)(2,1)}, bf16[128...) custom-call(s32[1]{0:T(128)} %bitcast.1.x_ref, s32[1]{0:T(128)S(6)} %copy.13.count_ref, ...), custom_call_target="tpu_custom_call" | custom-call | flops 67108864 | bytes 6000000 | tf_op jit(solution)/shard_map/start/pallas_call | solution.py:268
  13.0 0.0 all-gather.7.cloned.1.call-update
  13.0 0.0 copy-start.2
  13.0 0.0 copy-start.3
  13.0 15.0 %all-to-all-start = ((bf16[12,96,128]{2,1,0:T(8,128)(2,1)}), bf16[12,96,128]{2,1,0:T(8,128)(2,1)S(1)}, u32[]{:S(2)}, u32[]{:S(2)}) async-start(bf16[12,96,128]{2,1,0:T(8,128)(2,1)} %bitcast.14), calls=%async_computation | async-start | bytes 589824 | tf_op jit(solution)/shard_map/sum_weights_z/all_to_all | solution.py:286
  28.0 0.0 all-gather.9.cloned.1.call-start
  28.1 3.5 %collective-permute-start = (bf16[128,3072]{1,0:T(8,128)(2,1)}, bf16[128,3072]{1,0:T(8,128)(2,1)S(1)}, u32[]{:S(2)}, u32[]{:S(2)}) collective-permute-start(bf16[128,3072]{1,0:T(8,128)(2,1)} %get-tuple-element.15), channel_id=1, source_target_pairs={{0,192},{8,200},{16,208},{24,216},{32,224},{40,232},{48,240},{56,2... | collective-permute-start | bytes 2359304 | tf_op jit(solution)/shard_map/exchange_tiles/ppermute | solution.py:283
  31.6 3.5 %collective-permute-start.1 = (bf16[128,3072]{1,0:T(8,128)(2,1)}, bf16[128,3072]{1,0:T(8,128)(2,1)S(1)}, u32[]{:S(2)}, u32[]{:S(2)}) collective-permute-start(bf16[128,3072]{1,0:T(8,128)(2,1)} %get-tuple-element.16), channel_id=1, source_target_pairs={{0,384},{8,392},{16,400},{24,408},{32,416},{40,424},{48,432},{56,4... | collective-permute-start | bytes 2359304 | tf_op jit(solution)/shard_map/exchange_tiles/ppermute | solution.py:283
  35.1 4.5 %collective-permute-start.2 = (bf16[128,3072]{1,0:T(8,128)(2,1)}, bf16[128,3072]{1,0:T(8,128)(2,1)S(1)}, u32[]{:S(2)}, u32[]{:S(2)}) collective-permute-start(bf16[128,3072]{1,0:T(8,128)(2,1)} %get-tuple-element.17), channel_id=1, source_target_pairs={{0,576},{8,584},{16,592},{24,600},{32,608},{40,616},{48,624},{56,6... | collective-permute-start | bytes 2359304 | tf_op jit(solution)/shard_map/exchange_tiles/ppermute | solution.py:283
  39.6 0.0 all-gather.9.cloned.1.call-update
  39.6 0.0 copy-start.1
  39.6 29.8 %all_gather.27.blocks_hbm = bf16[3072,128]{1,0:T(8,128)(2,1)} all-gather(bf16[128,128]{1,0:T(8,128)(2,1)} %get-tuple-element.18), channel_id=1, replica_groups={{0,8,16,24,32,40,48,56,64,72,80,88,96,104,112,120,128,136,144,152,160,1..., dimensions={0}, use_global_device_ids=true | all-gather | bytes 819200 | tf_op jit(solution)/shard_map/gather_out/all_gather | solution.py:288
  69.4 0.0 collective-permute-done.t1_ref
  69.5 0.0 collective-permute-done.1.t2_ref
  69.5 0.2 collective-permute-done.2.t3_ref
  69.7 0.0 all-to-all-done.weight_ref
  69.7 0.0 copy-start
  69.7 1.1 copy-done
  70.8 2.3 %out_parts.1 = bf16[4,160,128]{2,1,0:T(8,128)(2,1)S(1)} custom-call(s32[1]{0:T(128)} %bitcast.1.x_ref, bf16[128,3072]{1,0:T(8,128)(2,1)S(1)} %copy-done, bf16[128,3072]{1,0:T(8,128)(2,1)S(1)} %collective-permute-done.t1_ref, bf16[128,3072]{1,0:T(8,128)(2,1)S(1)} %collective-permute-done.1.t2_ref, bf16[128,3072]{1,0:T(8,128)(2,1)S(1)} %collective-permute-done.2.t3_ref, ...), custom_call_target="tpu_custom_call" | custom-call | flops 402653184 | bytes 4000000 | tf_op jit(solution)/shard_map/out_parts/pallas_call | solution.py:290
  73.1 9.8 %all_to_all.20.got_ref = bf16[4,160,128]{2,1,0:T(8,128)(2,1)S(1)} all-to-all(bf16[4,160,128]{2,1,0:T(8,128)(2,1)S(1)} %out_parts.1), channel_id=1, replica_groups={{0,192,384,576},{8,200,392,584},{16,208,400,592},{24,216,408,600},{32,2..., dimensions={0} | all-to-all | bytes 327680 | tf_op jit(solution)/shard_map/sum_out_x/all_to_all | solution.py:300
  82.9 0.0 copy-done.2
  82.9 0.0 copy-done.3
  83.0 0.1 hidden.1
  83.1 28.6 %all-gather = bf16[3840,128]{1,0:T(8,128)(2,1)} all-gather(bf16[160,128]{1,0:T(8,128)(2,1)S(1)} %hidden.1), channel_id=2, replica_groups={{0,8,16,24,32,40,48,56,64,72,80,88,96,104,112,120,128,136,144,152,160,1..., dimensions={0}, use_global_device_ids=true | all-gather | bytes 1024000 | tf_op jit(solution)/shard_map/gather_pre/all_gather | solution.py:306
  111.7 0.0 all-gather.7.cloned.1.call-done
  111.7 0.0 copy-done.1
  111.7 4.5 %pre_parts.1 = (bf16[4,256,128]{2,1,0:T(8,128)(2,1)S(1)}, bf16[288,128]{1,0:T(8,128)(2,1)S(1)}) custom-call(s32[1]{0:T(128)} %bitcast.1.x_ref, bf16[128,3072]{1,0:T(8,128)(2,1)S(1)} %copy-done.1, bf16[128,3072]{1,0:T(8,128)(2,1)S(1)} %collective-permute-done.t1_ref, bf16[128,3072]{1,0:T(8,128)(2,1)S(1)} %collective-permute-done.1.t2_ref, ...), custom_call_target="tpu_custom_call" | custom-call | flops 805306368 | bytes 8000000 | tf_op jit(solution)/shard_map/pre_parts/pallas_call | solution.py:308
  116.2 9.8 %all_to_all.21.got_ref = bf16[4,256,128]{2,1,0:T(8,128)(2,1)S(1)} all-to-all(bf16[4,256,128]{2,1,0:T(8,128)(2,1)S(1)} %get-tuple-element.21), channel_id=1, replica_groups={{0,192,384,576},{8,200,392,584},{16,208,400,592},{24,216,408,600},{32,2..., dimensions={0} | all-to-all | bytes 524288 | tf_op jit(solution)/shard_map/sum_pre_x/all_to_all | solution.py:322
  126.0 0.8 spread.1
  126.8 7.5 %all-to-all-start.3 = ((bf16[8,128,128]{2,1,0:T(8,128)(2,1)}), bf16[8,128,128]{2,1,0:T(8,128)(2,1)S(1)}, u32[]{:S(2)}, u32[]{:S(2)}) async-start(bf16[8,128,128]{2,1,0:T(8,128)(2,1)} %get-tuple-element.24), calls=%async_computation.3 | async-start | bytes 524288 | tf_op jit(solution)/shard_map/gather_spread/all_to_all | solution.py:332
  134.4 13.9 %all-gather.2 = bf16[1664,128]{1,0:T(8,128)(2,1)} all-gather(bf16[416,128]{1,0:T(8,128)(2,1)S(1)} %get-tuple-element.23), channel_id=4, replica_groups={{0,192,384,576},{8,200,392,584},{16,208,400,592},{24,216,408,600},{32,2..., dimensions={0}, use_global_device_ids=true | all-gather | bytes 532480 | tf_op jit(solution)/shard_map/gather_weights/all_gather | solution.py:334
  148.2 0.0 all-gather.9.cloned.1.call-done
  148.2 0.0 all-to-all-done.3.spread_ref
  148.2 0.0 copy-start.4
  148.2 0.7 copy-done.4
  148.9 3.6 %final.1 = (f32[128,1024]{1,0:T(8,128)}, f32[512,128]{1,0:T(8,128)}, f32[128,512]{1,0:T(8,128)}) custom-call(bf16[4,416,128]{2,1,0:T(8,128)(2,1)} %bitcast.12, bf16[8,128,128]{2,1,0:T(8,128)(2,1)} %copy-done.4, bf16[8,512,128]{2,1,0:T(8,128)(2,1)} %bitcast.13), custom_call_target="tpu_custom_call" | custom-call | flops 134217728 | bytes 2500000 | tf_op jit(solution)/shard_map/final/pallas_call | solution.py:337
Async XLA Ops:
  7.2 104.5 %all-gather.7.cloned.1.call-start = ((), (), s32[]{:S(2)}) async-start(), calls=%async_computation.4 | async-start | bytes 3276800 | tf_op jit(solution)/shard_map/gather_input/all_gather | solution.py:279
  13.0 69.9 %copy-start.2 = (bf16[128,128]{1,0:T(8,128)(2,1)S(1)}, bf16[128,128]{1,0:T(8,128)(2,1)}, u32[]{:S(2)}) copy-start(bf16[128,128]{1,0:T(8,128)(2,1)} %pre_hidden_ref.1) | copy-start | bytes 98308
  13.0 69.9 %copy-start.3 = (s32[128]{0:T(128)S(1)}, s32[128]{0:T(128)}, u32[]{:S(2)}) copy-start(s32[128]{0:T(128)} %param.19) | copy-start | bytes 1540
  13.0 56.6 %all-to-all-start = ((bf16[12,96,128]{2,1,0:T(8,128)(2,1)}), bf16[12,96,128]{2,1,0:T(8,128)(2,1)S(1)}, u32[]{:S(2)}, u32[]{:S(2)}) async-start(bf16[12,96,128]{2,1,0:T(8,128)(2,1)} %bitcast.14), calls=%async_computation | async-start | bytes 589824 | tf_op jit(solution)/shard_map/sum_weights_z/all_to_all | solution.py:286
  28.0 120.2 %all-gather.9.cloned.1.call-start = ((), (), s32[]{:S(2)}) async-start(), calls=%async_computation.5 | async-start | bytes 1179648 | tf_op jit(solution)/shard_map/gather_weight_in/all_gather | solution.py:281
  28.1 41.4 %collective-permute-start = (bf16[128,3072]{1,0:T(8,128)(2,1)}, bf16[128,3072]{1,0:T(8,128)(2,1)S(1)}, u32[]{:S(2)}, u32[]{:S(2)}) collective-permute-start(bf16[128,3072]{1,0:T(8,128)(2,1)} %get-tuple-element.15), channel_id=1, source_target_pairs={{0,192},{8,200},{16,208},{24,216},{32,224},{40,232},{48,240},{56,2... | collective-permute-start | bytes 2359304 | tf_op jit(solution)/shard_map/exchange_tiles/ppermute | solution.py:283
  31.6 37.9 %collective-permute-start.1 = (bf16[128,3072]{1,0:T(8,128)(2,1)}, bf16[128,3072]{1,0:T(8,128)(2,1)S(1)}, u32[]{:S(2)}, u32[]{:S(2)}) collective-permute-start(bf16[128,3072]{1,0:T(8,128)(2,1)} %get-tuple-element.16), channel_id=1, source_target_pairs={{0,384},{8,392},{16,400},{24,408},{32,416},{40,424},{48,432},{56,4... | collective-permute-start | bytes 2359304 | tf_op jit(solution)/shard_map/exchange_tiles/ppermute | solution.py:283
  35.1 34.6 %collective-permute-start.2 = (bf16[128,3072]{1,0:T(8,128)(2,1)}, bf16[128,3072]{1,0:T(8,128)(2,1)S(1)}, u32[]{:S(2)}, u32[]{:S(2)}) collective-permute-start(bf16[128,3072]{1,0:T(8,128)(2,1)} %get-tuple-element.17), channel_id=1, source_target_pairs={{0,576},{8,584},{16,592},{24,600},{32,608},{40,616},{48,624},{56,6... | collective-permute-start | bytes 2359304 | tf_op jit(solution)/shard_map/exchange_tiles/ppermute | solution.py:283
  39.6 72.1 %copy-start.1 = (bf16[128,3072]{1,0:T(8,128)(2,1)S(1)}, bf16[128,3072]{1,0:T(8,128)(2,1)}, u32[]{:S(2)}) copy-start(bf16[128,3072]{1,0:T(8,128)(2,1)} %get-tuple-element.14.t0_hbm.t0_ref) | copy-start | bytes 2359300
  69.7 1.1 copy-start
  126.8 21.4 %all-to-all-start.3 = ((bf16[8,128,128]{2,1,0:T(8,128)(2,1)}), bf16[8,128,128]{2,1,0:T(8,128)(2,1)S(1)}, u32[]{:S(2)}, u32[]{:S(2)}) async-start(bf16[8,128,128]{2,1,0:T(8,128)(2,1)} %get-tuple-element.24), calls=%async_computation.3 | async-start | bytes 524288 | tf_op jit(solution)/shard_map/gather_spread/all_to_all | solution.py:332
  148.2 0.7 copy-start.4
Sparse Core Ops, SparseCore 0:
  13.1 68.0 all-gather.6
  83.6 41.0 all-gather.8

commit v6 on v4

--- a/solution.py
+++ b/solution.py
@@ -162,10 +162,13 @@
 
 
 def pre_parts_kernel(
-    x_ref, t0_ref, t1_ref, t2_ref, t3_ref, blocks_ref, turned_hbm, out_ref, weight_ref, turned_ref, sem
+    x_ref, t0_ref, t1_ref, t2_ref, t3_ref, blocks_ref, turned_hbm, out_ref, weight_ref, turned_ref, sems
 ):
-    copy = pltpu.make_async_copy(turned_hbm, turned_ref, sem)
-    copy.start()
+    copies = []
+    for i in range(6):
+        part = pl.ds(4 * i, 4)
+        copies.append(pltpu.make_async_copy(turned_hbm.at[part], turned_ref.at[part], sems.at[i]))
+        copies[-1].start()
     blocks = blocks_ref[:, :TILE].reshape(WIDE, TILE)
     parts = multiply((t0_ref, t1_ref, t2_ref, t3_ref), blocks)
     for k in range(NX):
@@ -175,11 +178,11 @@
         both = blocks_ref[2 * z, TILE:].astype(F32) + blocks_ref[2 * z + 1, TILE:].astype(F32)
         pieces.append(both[:PIECE])
     weight_ref[...] = jnp.concatenate(pieces, axis=0).astype(BF16)
-    copy.wait()
     w_in = jnp.zeros((4 * TILE, TILE), F32)
-    for p in range(0, LINE, 2):
-        turned = jnp.concatenate([turned_ref[p], turned_ref[p + 1]], axis=1)
-        w_in = w_in + jnp.dot(turned, blocks[p * TILE : (p + 2) * TILE], preferred_element_type=F32)
+    for p in range(0, LINE, 4):
+        copies[p // 4].wait()
+        turned = jnp.concatenate([turned_ref[p + i] for i in range(4)], axis=1)
+        w_in = w_in + jnp.dot(turned, blocks[p * TILE : (p + 4) * TILE], preferred_element_type=F32)
     for k in range(NX):
         out_ref[k, TILE:] = w_in[k * TILE : (k + 1) * TILE].astype(BF16)
 
@@ -193,9 +196,7 @@
     weight_ref[NZ * PIECE :] = total[TILE:].astype(BF16)
 
 
-def final_kernel(weights_ref, spread_ref, weight_in_hbm, w_out_ref, w_in_ref, input_ref, weight_in_ref, sem):
-    copy = pltpu.make_async_copy(weight_in_hbm, weight_in_ref, sem)
-    copy.start()
+def final_kernel(weights_ref, spread_ref, weight_in_ref, w_out_ref, w_in_ref, input_ref):
     for x in range(NX):
         weights = weights_ref[x].astype(F32)
         for z in range(NZ):
@@ -207,7 +208,6 @@
                 w_out_ref[r : r + n, j * TILE : (j + 1) * TILE] = weights[at : at + n]
                 row, at, left = row + n, at + n, left - n
         w_in_ref[x * TILE : (x + 1) * TILE] = weights[NZ * PIECE :]
-    copy.wait()
     total = jnp.zeros((TILE, 512), F32)
     for k in range(NREP):
         total = total + lax.dot_general(spread_ref[k], weight_in_ref[k], BY_ROWS, preferred_element_type=F32)
@@ -270,6 +270,7 @@
         scaled = call(hidden_kernel, shape((TILE + ROOM, TILE), BF16), [vmem()] * 3, 1000000, 600000)(
             degree, parts, pre_hidden
         )
+    scaled, turned = lax.optimization_barrier((scaled, turned))
     with jax.named_scope("gather_pre"):
         blocks = lax.all_gather(scaled, "blk", axis=0, tiled=False, axis_index_groups=LINE_GROUPS)
     with jax.named_scope("pre_parts"):
@@ -279,8 +280,8 @@
             [smem()] + [vmem()] * 5 + [hbm()],
             4 * 512 * 3072 * 128,
             8000000,
-            [pltpu.VMEM((LINE, 4 * TILE, TILE), BF16), pltpu.SemaphoreType.DMA],
-            limit=50,
+            [pltpu.VMEM((LINE, 4 * TILE, TILE), BF16), pltpu.SemaphoreType.DMA((6,))],
+            limit=48,
         )(x, *tiles, blocks, turned)
     with jax.named_scope("sum_pre_x"):
         parts = lax.all_to_all(parts, "blk", 0, 0, tiled=True, axis_index_groups=X_GROUPS)
@@ -301,11 +302,10 @@
             call(
                 final_kernel,
                 [shape((128, 1024), F32), shape((512, 128), F32), shape((128, 512), F32)],
-                [vmem()] * 2 + [hbm()],
+                [vmem()] * 3,
                 2 * 128 * 1024 * 512,
                 2500000,
-                [pltpu.VMEM((NREP, 4 * TILE, TILE), BF16), pltpu.SemaphoreType.DMA],
-                limit=56,
+                limit=14,
             )(weights, spread, weights_in)
         )
 

time: 161 us -> 155 us (0.963)
  Pallas kernels: 16.1 us -> 12.7 us
  blocking collectives: 91.4 us -> 88.7 us
    all_gather x1, blocking collectives: 28.6 us -> 25.9 us  [local(): lax.all_gather(scaled, 'blk', axis=0, tiled=False, axis_index_groups=LINE...]
    pallas_call x1, Pallas kernels: 3.45 us -> 1.28 us  [local(): call(final_kernel, [shape((128, 1024), F32), shape((512, 128), F32), shap...]
where the time goes in v6:
time: 155 us; the launch traced here: 154 us
  blocking collectives  88.7 us (57%)
  starting transfers between devices  34.6 us (22%)
  between operations  14.8 us (10%)
  Pallas kernels  12.7 us (8%)
  local copies, waits for them, and re-layouts  2.39 us (2%)
    all_gather x1, blocking collectives, local(): lax.all_gather(scaled, 'blk', axis=0, tiled=True, axis_index_groups=LINE_...  29.6 us
    all_gather x1, blocking collectives, local(): lax.all_gather(scaled, 'blk', axis=0, tiled=False, axis_index_groups=LINE...  25.9 us
    all_to_all x2, blocking collectives, local(): lax.all_to_all(parts, 'blk', 0, 0, tiled=True, axis_index_groups=X_GROUPS)  20.3 us
    all_to_all x1, starting transfers between devices, local(): lax.all_to_all(weights, 'blk', 0, 0, tiled=True, axis_index_groups=Z_GROUPS)  16 us
    all_gather x1, blocking collectives, local(): lax.all_gather(weights, 'blk', axis=0, tiled=False, axis_index_groups=X_G...  12.9 us
    ppermute x3, starting transfers between devices, local(): lax.ppermute(tiles[k], 'blk', along_x(k))  11 us
    all_to_all x1, starting transfers between devices, local(): spread = lax.all_to_all(spread, 'rep', 0, 0, tiled=True)  7.57 us
    pallas_call x1, Pallas kernels, local(): call(start_kernel, [shape((TILE, WIDE), BF16)] * NX + [block, shape((NZ *...  4.21 us
  transfers between devices with their start and end apart: 7, of which 1 were waited for; matrix products, arithmetic and copies ran while one was open for 0% of the time, Pallas kernels for 5%

profile of v6, /device:TPU:8, one launch (start us, length us, event | category | flops | bytes accessed | tf_op | source)
XLA Modules:
  0.0 154.3 jit_solution(11493689904325600681)
XLA Ops:
  7.2 0.0 all-gather.7.cloned.1.call-start
  7.9 4.2 %start.1 = (bf16[128,3072]{1,0:T(8,128)(2,1)}, bf16[128,3072]{1,0:T(8,128)(2,1)}, bf16[128,3072]{1,0:T(8,128)(2,1)}, bf16[128,3072]{1,0:T(8,128)(2,1)}, bf16[128...) custom-call(s32[1]{0:T(128)} %bitcast.1.x_ref, s32[1]{0:T(128)S(6)} %copy.13.count_ref, ...), custom_call_target="tpu_custom_call" | custom-call | flops 67108864 | bytes 6000000 | tf_op jit(solution)/shard_map/start/pallas_call | solution.py:237
  12.1 0.0 all-gather.7.cloned.1.call-update
  12.1 0.0 copy-start.3
  12.1 0.0 copy-start.4
  12.2 16.0 %all-to-all-start = ((bf16[12,96,128]{2,1,0:T(8,128)(2,1)}), bf16[12,96,128]{2,1,0:T(8,128)(2,1)S(1)}, u32[]{:S(2)}, u32[]{:S(2)}) async-start(bf16[12,96,128]{2,1,0:T(8,128)(2,1)} %bitcast.14), calls=%async_computation | async-start | bytes 589824 | tf_op jit(solution)/shard_map/sum_weights_z/all_to_all | solution.py:255
  28.2 0.0 all-gather.9.cloned.1.call-start
  28.2 2.8 %collective-permute-start = (bf16[128,3072]{1,0:T(8,128)(2,1)}, bf16[128,3072]{1,0:T(8,128)(2,1)S(1)}, u32[]{:S(2)}, u32[]{:S(2)}) collective-permute-start(bf16[128,3072]{1,0:T(8,128)(2,1)} %get-tuple-element.17), channel_id=1, source_target_pairs={{0,192},{8,200},{16,208},{24,216},{32,224},{40,232},{48,240},{56,2... | collective-permute-start | bytes 2359304 | tf_op jit(solution)/shard_map/exchange_tiles/ppermute | solution.py:252
  31.1 4.5 %collective-permute-start.1 = (bf16[128,3072]{1,0:T(8,128)(2,1)}, bf16[128,3072]{1,0:T(8,128)(2,1)S(1)}, u32[]{:S(2)}, u32[]{:S(2)}) collective-permute-start(bf16[128,3072]{1,0:T(8,128)(2,1)} %get-tuple-element.18), channel_id=1, source_target_pairs={{0,384},{8,392},{16,400},{24,408},{32,416},{40,424},{48,432},{56,4... | collective-permute-start | bytes 2359304 | tf_op jit(solution)/shard_map/exchange_tiles/ppermute | solution.py:252
  35.6 3.6 %collective-permute-start.2 = (bf16[128,3072]{1,0:T(8,128)(2,1)}, bf16[128,3072]{1,0:T(8,128)(2,1)S(1)}, u32[]{:S(2)}, u32[]{:S(2)}) collective-permute-start(bf16[128,3072]{1,0:T(8,128)(2,1)} %get-tuple-element.19), channel_id=1, source_target_pairs={{0,576},{8,584},{16,592},{24,600},{32,608},{40,616},{48,624},{56,6... | collective-permute-start | bytes 2359304 | tf_op jit(solution)/shard_map/exchange_tiles/ppermute | solution.py:252
  39.2 0.0 all-gather.9.cloned.1.call-update
  39.2 0.0 copy-start.1
  39.3 29.6 %all_gather.27.blocks_ref = bf16[3072,128]{1,0:T(8,128)(2,1)} all-gather(bf16[128,128]{1,0:T(8,128)(2,1)} %get-tuple-element.20), channel_id=1, replica_groups={{0,8,16,24,32,40,48,56,64,72,80,88,96,104,112,120,128,136,144,152,160,1..., dimensions={0}, use_global_device_ids=true | all-gather | bytes 819200 | tf_op jit(solution)/shard_map/gather_out/all_gather | solution.py:257
  68.8 0.0 collective-permute-done.t1_ref
  68.8 0.0 collective-permute-done.1.t2_ref
  68.8 1.0 collective-permute-done.2.t3_ref
  69.8 0.0 all-to-all-done.weight_ref
  69.8 0.0 copy-start
  69.8 1.1 copy-done
  70.9 2.2 %out_parts.1 = bf16[4,160,128]{2,1,0:T(8,128)(2,1)S(1)} custom-call(s32[1]{0:T(128)} %bitcast.1.x_ref, bf16[128,3072]{1,0:T(8,128)(2,1)S(1)} %copy-done, bf16[128,3072]{1,0:T(8,128)(2,1)S(1)} %collective-permute-done.t1_ref, bf16[128,3072]{1,0:T(8,128)(2,1)S(1)} %collective-permute-done.1.t2_ref, bf16[128,3072]{1,0:T(8,128)(2,1)S(1)} %collective-permute-done.2.t3_ref, ...), custom_call_target="tpu_custom_call" | custom-call | flops 402653184 | bytes 4000000 | tf_op jit(solution)/shard_map/out_parts/pallas_call | solution.py:259
  73.1 10.5 %all_to_all.20.got_ref = bf16[4,160,128]{2,1,0:T(8,128)(2,1)S(1)} all-to-all(bf16[4,160,128]{2,1,0:T(8,128)(2,1)S(1)} %out_parts.1), channel_id=1, replica_groups={{0,192,384,576},{8,200,392,584},{16,208,400,592},{24,216,408,600},{32,2..., dimensions={0} | all-to-all | bytes 327680 | tf_op jit(solution)/shard_map/sum_out_x/all_to_all | solution.py:268
  83.6 0.0 copy-done.3
  83.6 0.0 copy-done.4
  83.6 0.1 hidden.1
  83.7 0.0 all-gather.7.cloned.1.call-done
  83.7 25.9 %all-gather.1 = bf16[3840,128]{1,0:T(8,128)(2,1)S(1)} all-gather(bf16[160,128]{1,0:T(8,128)(2,1)S(1)} %hidden.1), channel_id=3, replica_groups={{0,8,16,24,32,40,48,56,64,72,80,88,96,104,112,120,128,136,144,152,160,1..., dimensions={0}, use_global_device_ids=true | all-gather | bytes 1024000 | tf_op jit(solution)/shard_map/gather_pre/all_gather | solution.py:275
  109.7 0.0 copy-done.1
  109.7 4.1 %pre_parts.1 = (bf16[4,256,128]{2,1,0:T(8,128)(2,1)S(1)}, bf16[288,128]{1,0:T(8,128)(2,1)S(1)}) custom-call(s32[1]{0:T(128)} %bitcast.1.x_ref, bf16[128,3072]{1,0:T(8,128)(2,1)S(1)} %copy-done.1, bf16[128,3072]{1,0:T(8,128)(2,1)S(1)} %collective-permute-done.t1_ref, bf16[128,3072]{1,0:T(8,128)(2,1)S(1)} %collective-permute-done.1.t2_ref, ...), custom_call_target="tpu_custom_call" | custom-call | flops 805306368 | bytes 8000000 | tf_op jit(solution)/shard_map/pre_parts/pallas_call | solution.py:277
  113.8 9.8 %all_to_all.21.got_ref = bf16[4,256,128]{2,1,0:T(8,128)(2,1)S(1)} all-to-all(bf16[4,256,128]{2,1,0:T(8,128)(2,1)S(1)} %get-tuple-element.25), channel_id=1, replica_groups={{0,192,384,576},{8,200,392,584},{16,208,400,592},{24,216,408,600},{32,2..., dimensions={0} | all-to-all | bytes 524288 | tf_op jit(solution)/shard_map/sum_pre_x/all_to_all | solution.py:287
  123.7 0.8 spread.1
  124.5 7.6 %all-to-all-start.3 = ((bf16[8,128,128]{2,1,0:T(8,128)(2,1)}), bf16[8,128,128]{2,1,0:T(8,128)(2,1)S(1)}, u32[]{:S(2)}, u32[]{:S(2)}) async-start(bf16[8,128,128]{2,1,0:T(8,128)(2,1)} %get-tuple-element.28), calls=%async_computation.3 | async-start | bytes 524288 | tf_op jit(solution)/shard_map/gather_spread/all_to_all | solution.py:297
  132.1 12.9 %all-gather.2 = bf16[1664,128]{1,0:T(8,128)(2,1)S(1)} all-gather(bf16[416,128]{1,0:T(8,128)(2,1)S(1)} %get-tuple-element.27), channel_id=4, replica_groups={{0,192,384,576},{8,200,392,584},{16,208,400,592},{24,216,408,600},{32,2..., dimensions={0}, use_global_device_ids=true | all-gather | bytes 532480 | tf_op jit(solution)/shard_map/gather_weights/all_gather | solution.py:299
  145.0 0.0 all-gather.9.cloned.1.call-done
  145.0 0.0 all-to-all-done.3.spread_ref
  145.0 0.0 copy-start.2
  145.0 1.2 copy-done.2
  146.2 1.3 final.1
Async XLA Ops:
  7.2 76.6 %all-gather.7.cloned.1.call-start = ((), (), s32[]{:S(2)}) async-start(), calls=%async_computation.4 | async-start | bytes 3276800 | tf_op jit(solution)/shard_map/gather_input/all_gather | solution.py:248
  12.1 71.5 %copy-start.3 = (bf16[128,128]{1,0:T(8,128)(2,1)S(1)}, bf16[128,128]{1,0:T(8,128)(2,1)}, u32[]{:S(2)}) copy-start(bf16[128,128]{1,0:T(8,128)(2,1)} %pre_hidden_ref.1) | copy-start | bytes 98308
  12.1 71.5 %copy-start.4 = (s32[128]{0:T(128)S(1)}, s32[128]{0:T(128)}, u32[]{:S(2)}) copy-start(s32[128]{0:T(128)} %param.19) | copy-start | bytes 1540
  12.2 57.6 %all-to-all-start = ((bf16[12,96,128]{2,1,0:T(8,128)(2,1)}), bf16[12,96,128]{2,1,0:T(8,128)(2,1)S(1)}, u32[]{:S(2)}, u32[]{:S(2)}) async-start(bf16[12,96,128]{2,1,0:T(8,128)(2,1)} %bitcast.14), calls=%async_computation | async-start | bytes 589824 | tf_op jit(solution)/shard_map/sum_weights_z/all_to_all | solution.py:255
  28.2 116.8 %all-gather.9.cloned.1.call-start = ((), (), s32[]{:S(2)}) async-start(), calls=%async_computation.5 | async-start | bytes 1179648 | tf_op jit(solution)/shard_map/gather_weight_in/all_gather | solution.py:250
  28.2 40.6 %collective-permute-start = (bf16[128,3072]{1,0:T(8,128)(2,1)}, bf16[128,3072]{1,0:T(8,128)(2,1)S(1)}, u32[]{:S(2)}, u32[]{:S(2)}) collective-permute-start(bf16[128,3072]{1,0:T(8,128)(2,1)} %get-tuple-element.17), channel_id=1, source_target_pairs={{0,192},{8,200},{16,208},{24,216},{32,224},{40,232},{48,240},{56,2... | collective-permute-start | bytes 2359304 | tf_op jit(solution)/shard_map/exchange_tiles/ppermute | solution.py:252
  31.1 37.8 %collective-permute-start.1 = (bf16[128,3072]{1,0:T(8,128)(2,1)}, bf16[128,3072]{1,0:T(8,128)(2,1)S(1)}, u32[]{:S(2)}, u32[]{:S(2)}) collective-permute-start(bf16[128,3072]{1,0:T(8,128)(2,1)} %get-tuple-element.18), channel_id=1, source_target_pairs={{0,384},{8,392},{16,400},{24,408},{32,416},{40,424},{48,432},{56,4... | collective-permute-start | bytes 2359304 | tf_op jit(solution)/shard_map/exchange_tiles/ppermute | solution.py:252
  35.6 34.2 %collective-permute-start.2 = (bf16[128,3072]{1,0:T(8,128)(2,1)}, bf16[128,3072]{1,0:T(8,128)(2,1)S(1)}, u32[]{:S(2)}, u32[]{:S(2)}) collective-permute-start(bf16[128,3072]{1,0:T(8,128)(2,1)} %get-tuple-element.19), channel_id=1, source_target_pairs={{0,576},{8,584},{16,592},{24,600},{32,608},{40,616},{48,624},{56,6... | collective-permute-start | bytes 2359304 | tf_op jit(solution)/shard_map/exchange_tiles/ppermute | solution.py:252
  39.2 70.4 %copy-start.1 = (bf16[128,3072]{1,0:T(8,128)(2,1)S(1)}, bf16[128,3072]{1,0:T(8,128)(2,1)}, u32[]{:S(2)}) copy-start(bf16[128,3072]{1,0:T(8,128)(2,1)} %get-tuple-element.16.t0_ref) | copy-start | bytes 2359300
  69.8 1.1 copy-start
  124.5 20.5 %all-to-all-start.3 = ((bf16[8,128,128]{2,1,0:T(8,128)(2,1)}), bf16[8,128,128]{2,1,0:T(8,128)(2,1)S(1)}, u32[]{:S(2)}, u32[]{:S(2)}) async-start(bf16[8,128,128]{2,1,0:T(8,128)(2,1)} %get-tuple-element.28), calls=%async_computation.3 | async-start | bytes 524288 | tf_op jit(solution)/shard_map/gather_spread/all_to_all | solution.py:297
  145.0 1.2 copy-start.2
Sparse Core Ops, SparseCore 0:
  12.2 68.3 all-gather.6
  83.0 40.9 all-gather.8

commit v7 on v6

--- a/solution.py
+++ b/solution.py
@@ -26,6 +26,7 @@
 
 Z_GROUPS = [[blk_index(x, z, c) for z in range(NZ)] for x in range(NX) for c in range(NC)]
 X_GROUPS = [[blk_index(x, z, c) for x in range(NX)] for z in range(NZ) for c in range(NC)]
+SIDE_GROUPS = [[blk_index(x, z, c) for x in range(NX) for c in range(NC)] for z in range(NZ)]
 LINE_GROUPS = [[x * LINE + p for p in range(LINE)] for x in range(NX)]
 
 
@@ -63,7 +64,7 @@
 
 
 def start_kernel(
-    x_ref,
+    me_ref,
     count_ref,
     source_hbm,
     degree_hbm,
@@ -112,11 +113,13 @@
         rows = slice(j * TILE, (j + 1) * TILE)
         turned_ref[rows] = (agg_input_ref[:, rows].astype(F32).T * root).astype(BF16)
 
+    x = lax.div(me_ref[0], LINE)
+
     def step(slot, carry):
         source = source_ref[0, slot]
         line = lax.div(source, LINE)
         columns = pl.ds(pl.multiple_of((source - line * LINE) * TILE, TILE), TILE)
-        away = (line - x_ref[0] + NX) & (NX - 1)
+        away = (line - x + NX) & (NX - 1)
         for k, out_ref in enumerate(out_refs):
 
             @pl.when(away == k)
@@ -137,13 +140,13 @@
     return [jnp.dot(tiles_ref[...], blocks, preferred_element_type=F32).astype(BF16) for tiles_ref in tiles_refs]
 
 
-def out_parts_kernel(x_ref, t0_ref, t1_ref, t2_ref, t3_ref, blocks_ref, weight_ref, out_ref):
+def out_parts_kernel(me_ref, t0_ref, t1_ref, t2_ref, t3_ref, blocks_ref, weight_ref, out_ref):
     parts = multiply((t0_ref, t1_ref, t2_ref, t3_ref), blocks_ref[...])
     total = weight_ref[0].astype(F32)
     for j in range(1, NZ):
         total = total + weight_ref[j].astype(F32)
     for k in range(NX):
-        out_ref[(x_ref[0] - k + NX) & (NX - 1), :TILE] = parts[k]
+        out_ref[(lax.div(me_ref[0], LINE) - k + NX) & (NX - 1), :TILE] = parts[k]
         piece = total[k * PIECE : (k + 1) * PIECE]
         piece = jnp.concatenate([piece, jnp.zeros((ROOM - PIECE, TILE), F32)], axis=0)
         out_ref[k, TILE:] = piece.astype(BF16)
@@ -161,28 +164,22 @@
     out_ref[TILE:] = total[TILE:].astype(BF16)
 
 
-def pre_parts_kernel(
-    x_ref, t0_ref, t1_ref, t2_ref, t3_ref, blocks_ref, turned_hbm, out_ref, weight_ref, turned_ref, sems
-):
-    copies = []
-    for i in range(6):
-        part = pl.ds(4 * i, 4)
-        copies.append(pltpu.make_async_copy(turned_hbm.at[part], turned_ref.at[part], sems.at[i]))
-        copies[-1].start()
+def pre_parts_kernel(me_ref, t0_ref, t1_ref, t2_ref, t3_ref, blocks_ref, turned_ref, out_ref, weight_ref):
     blocks = blocks_ref[:, :TILE].reshape(WIDE, TILE)
     parts = multiply((t0_ref, t1_ref, t2_ref, t3_ref), blocks)
     for k in range(NX):
-        out_ref[(x_ref[0] - k + NX) & (NX - 1), :TILE] = parts[k]
+        out_ref[(lax.div(me_ref[0], LINE) - k + NX) & (NX - 1), :TILE] = parts[k]
     pieces = []
     for z in range(NZ):
         both = blocks_ref[2 * z, TILE:].astype(F32) + blocks_ref[2 * z + 1, TILE:].astype(F32)
         pieces.append(both[:PIECE])
     weight_ref[...] = jnp.concatenate(pieces, axis=0).astype(BF16)
+    core = me_ref[0] & 1
     w_in = jnp.zeros((4 * TILE, TILE), F32)
-    for p in range(0, LINE, 4):
-        copies[p // 4].wait()
-        turned = jnp.concatenate([turned_ref[p + i] for i in range(4)], axis=1)
-        w_in = w_in + jnp.dot(turned, blocks[p * TILE : (p + 4) * TILE], preferred_element_type=F32)
+    for z in range(0, NZ, 2):
+        turned = jnp.concatenate([turned_ref[z], turned_ref[z + 1]], axis=1)
+        mine = jnp.concatenate([blocks_ref[2 * (z + i) + core, :TILE] for i in range(2)], axis=0)
+        w_in = w_in + jnp.dot(turned, mine, preferred_element_type=F32)
     for k in range(NX):
         out_ref[k, TILE:] = w_in[k * TILE : (k + 1) * TILE].astype(BF16)
 
@@ -198,7 +195,7 @@
 
 def final_kernel(weights_ref, spread_ref, weight_in_ref, w_out_ref, w_in_ref, input_ref):
     for x in range(NX):
-        weights = weights_ref[x].astype(F32)
+        weights = weights_ref[2 * x].astype(F32)
         for z in range(NZ):
             row = z * CHUNK + x * PIECE
             at, left = z * PIECE, min(PIECE, 8 * TILE - row)
@@ -207,7 +204,7 @@
                 n = min(left, TILE - r)
                 w_out_ref[r : r + n, j * TILE : (j + 1) * TILE] = weights[at : at + n]
                 row, at, left = row + n, at + n, left - n
-        w_in_ref[x * TILE : (x + 1) * TILE] = weights[NZ * PIECE :]
+        w_in_ref[x * TILE : (x + 1) * TILE] = weights[NZ * PIECE :] + weights_ref[2 * x + 1, NZ * PIECE :].astype(F32)
     total = jnp.zeros((TILE, 512), F32)
     for k in range(NREP):
         total = total + lax.dot_general(spread_ref[k], weight_in_ref[k], BY_ROWS, preferred_element_type=F32)
@@ -228,7 +225,7 @@
 ):
     shape = jax.ShapeDtypeStruct
     block = shape((TILE, TILE), BF16)
-    x = (lax.axis_index("blk") // LINE).astype(jnp.int32).reshape(1)
+    me = lax.axis_index("blk").astype(jnp.int32).reshape(1)
     degree = degree.reshape(1, TILE)
 
     copied = [tile_source, degree, grad_out, weight_out, agg_hidden, agg_input, edge_tiles]
@@ -243,9 +240,9 @@
             6000000,
             [home(a.shape, a.dtype) for home, a in zip(homes, copied)] + [pltpu.SemaphoreType.DMA((7,))],
             limit=56,
-        )(x, tile_count, *copied)
+        )(me, tile_count, *copied)
     with jax.named_scope("gather_input"):
-        turned = lax.all_gather(turned, "blk", axis=0, tiled=False, axis_index_groups=LINE_GROUPS)
+        turned = lax.all_gather(turned, "blk", axis=0, tiled=False, axis_index_groups=Z_GROUPS)
     with jax.named_scope("gather_weight_in"):
         weights_in = lax.all_gather(weight_in, "rep", axis=0, tiled=False)
     with jax.named_scope("exchange_tiles"):
@@ -263,7 +260,7 @@
             2 * 512 * 3072 * 128,
             4000000,
             limit=50,
-        )(x, *tiles, blocks, weights)
+        )(me, *tiles, blocks, weights)
     with jax.named_scope("sum_out_x"):
         parts = lax.all_to_all(parts, "blk", 0, 0, tiled=True, axis_index_groups=X_GROUPS)
     with jax.named_scope("hidden"):
@@ -277,12 +274,11 @@
         parts, w_out = call(
             pre_parts_kernel,
             [shape((NX, 2 * TILE, TILE), BF16), shape((NZ * PIECE, TILE), BF16)],
-            [smem()] + [vmem()] * 5 + [hbm()],
+            [smem()] + [vmem()] * 6,
             4 * 512 * 3072 * 128,
             8000000,
-            [pltpu.VMEM((LINE, 4 * TILE, TILE), BF16), pltpu.SemaphoreType.DMA((6,))],
-            limit=48,
-        )(x, *tiles, blocks, turned)
+            limit=44,
+        )(me, *tiles, blocks, turned)
     with jax.named_scope("sum_pre_x"):
         parts = lax.all_to_all(parts, "blk", 0, 0, tiled=True, axis_index_groups=X_GROUPS)
     with jax.named_scope("spread"):
@@ -296,7 +292,7 @@
     with jax.named_scope("gather_spread"):
         spread = lax.all_to_all(spread, "rep", 0, 0, tiled=True)
     with jax.named_scope("gather_weights"):
-        weights = lax.all_gather(weights, "blk", axis=0, tiled=False, axis_index_groups=X_GROUPS)
+        weights = lax.all_gather(weights, "blk", axis=0, tiled=False, axis_index_groups=SIDE_GROUPS)
     with jax.named_scope("final"):
         return tuple(
             call(

time: 155 us -> 154 us (level)
  the two profiles are of different devices: /device:TPU:8 before, /device:TPU:1 now
where the time goes in v7:
time: 154 us; the launch traced here: 153 us
  blocking collectives  92.4 us (60%)
  starting transfers between devices  33.5 us (22%)
  between operations  14.8 us (10%)
  Pallas kernels  9.97 us (6%)
  local copies, waits for them, and re-layouts  2.65 us (2%)
    all_gather x1, blocking collectives, local(): lax.all_gather(scaled, 'blk', axis=0, tiled=True, axis_index_groups=LINE_...  31.1 us
    all_gather x1, blocking collectives, local(): lax.all_gather(scaled, 'blk', axis=0, tiled=False, axis_index_groups=LINE...  28.7 us
    all_to_all x2, blocking collectives, local(): lax.all_to_all(parts, 'blk', 0, 0, tiled=True, axis_index_groups=X_GROUPS)  17.6 us
    all_to_all x1, starting transfers between devices, local(): lax.all_to_all(weights, 'blk', 0, 0, tiled=True, axis_index_groups=Z_GROUPS)  15.5 us
    all_gather x1, blocking collectives, local(): lax.all_gather(weights, 'blk', axis=0, tiled=False, axis_index_groups=SID...  14.9 us
    ppermute x3, starting transfers between devices, local(): lax.ppermute(tiles[k], 'blk', along_x(k))  11.1 us
    all_to_all x1, starting transfers between devices, local(): spread = lax.all_to_all(spread, 'rep', 0, 0, tiled=True)  6.8 us
    pallas_call x1, Pallas kernels, local(): call(start_kernel, [shape((TILE, WIDE), BF16)] * NX + [block, shape((NZ *...  4.21 us
  transfers between devices with their start and end apart: 7, of which 0 were waited for; matrix products, arithmetic and copies ran while one was open for 0% of the time, Pallas kernels for 3%

profile of v7, /device:TPU:1, one launch (start us, length us, event | category | flops | bytes accessed | tf_op | source)
XLA Modules:
  0.0 153.4 jit_solution(832748497875096858)
XLA Ops:
  7.2 0.0 all-gather.7.cloned.1.call-start
  7.9 4.2 %start.1 = (bf16[128,3072]{1,0:T(8,128)(2,1)}, bf16[128,3072]{1,0:T(8,128)(2,1)}, bf16[128,3072]{1,0:T(8,128)(2,1)}, bf16[128,3072]{1,0:T(8,128)(2,1)}, bf16[128...) custom-call(s32[1]{0:T(128)} %bitcast.1.me_ref, s32[1]{0:T(128)S(6)} %copy.13.count_ref, ...), custom_call_target="tpu_custom_call" | custom-call | flops 67108864 | bytes 6000000 | tf_op jit(solution)/shard_map/start/pallas_call | solution.py:234
  12.1 0.0 copy-start
  12.1 0.0 all-gather.7.cloned.1.call-update
  12.1 15.5 %all-to-all-start = ((bf16[12,96,128]{2,1,0:T(8,128)(2,1)}), bf16[12,96,128]{2,1,0:T(8,128)(2,1)S(1)}, u32[]{:S(2)}, u32[]{:S(2)}) async-start(bf16[12,96,128]{2,1,0:T(8,128)(2,1)} %bitcast.14), calls=%async_computation | async-start | bytes 589824 | tf_op jit(solution)/shard_map/sum_weights_z/all_to_all | solution.py:252
  27.7 0.0 all-gather.9.cloned.1.call-start
  27.7 3.3 %collective-permute-start = (bf16[128,3072]{1,0:T(8,128)(2,1)}, bf16[128,3072]{1,0:T(8,128)(2,1)S(1)}, u32[]{:S(2)}, u32[]{:S(2)}) collective-permute-start(bf16[128,3072]{1,0:T(8,128)(2,1)} %get-tuple-element.17), channel_id=1, source_target_pairs={{0,192},{8,200},{16,208},{24,216},{32,224},{40,232},{48,240},{56,2... | collective-permute-start | bytes 2359304 | tf_op jit(solution)/shard_map/exchange_tiles/ppermute | solution.py:249
  31.1 4.8 %collective-permute-start.1 = (bf16[128,3072]{1,0:T(8,128)(2,1)}, bf16[128,3072]{1,0:T(8,128)(2,1)S(1)}, u32[]{:S(2)}, u32[]{:S(2)}) collective-permute-start(bf16[128,3072]{1,0:T(8,128)(2,1)} %get-tuple-element.18), channel_id=1, source_target_pairs={{0,384},{8,392},{16,400},{24,408},{32,416},{40,424},{48,432},{56,4... | collective-permute-start | bytes 2359304 | tf_op jit(solution)/shard_map/exchange_tiles/ppermute | solution.py:249
  35.9 3.0 %collective-permute-start.2 = (bf16[128,3072]{1,0:T(8,128)(2,1)}, bf16[128,3072]{1,0:T(8,128)(2,1)S(1)}, u32[]{:S(2)}, u32[]{:S(2)}) collective-permute-start(bf16[128,3072]{1,0:T(8,128)(2,1)} %get-tuple-element.19), channel_id=1, source_target_pairs={{0,576},{8,584},{16,592},{24,600},{32,608},{40,616},{48,624},{56,6... | collective-permute-start | bytes 2359304 | tf_op jit(solution)/shard_map/exchange_tiles/ppermute | solution.py:249
  38.8 0.0 all-gather.9.cloned.1.call-update
  38.9 31.1 %all_gather.27.blocks_ref = bf16[3072,128]{1,0:T(8,128)(2,1)} all-gather(bf16[128,128]{1,0:T(8,128)(2,1)} %get-tuple-element.20), channel_id=1, replica_groups={{0,8,16,24,32,40,48,56,64,72,80,88,96,104,112,120,128,136,144,152,160,1..., dimensions={0}, use_global_device_ids=true | all-gather | bytes 819200 | tf_op jit(solution)/shard_map/gather_out/all_gather | solution.py:254
  70.0 0.0 collective-permute-done.t1_ref
  70.0 0.0 collective-permute-done.1.t2_ref
  70.0 0.0 collective-permute-done.2.t3_ref
  70.0 0.0 all-to-all-done.weight_ref
  70.0 0.0 copy-done
  70.0 0.0 copy-start.3
  70.0 0.0 copy-start.4
  70.1 2.1 %out_parts.1 = bf16[4,160,128]{2,1,0:T(8,128)(2,1)S(1)} custom-call(s32[1]{0:T(128)} %bitcast.1.me_ref, bf16[128,3072]{1,0:T(8,128)(2,1)S(1)} %copy-done, bf16[128,3072]{1,0:T(8,128)(2,1)S(1)} %collective-permute-done.t1_ref, bf16[128,3072]{1,0:T(8,128)(2,1)S(1)} %collective-permute-done.1.t2_ref, bf16[128,3072]{1,0:T(8,128)(2,1)S(1)} %collective-permute-done.2.t3_ref, ...), custom_call_target="tpu_custom_call" | custom-call | flops 402653184 | bytes 4000000 | tf_op jit(solution)/shard_map/out_parts/pallas_call | solution.py:256
  72.2 8.8 %all_to_all.20.got_ref = bf16[4,160,128]{2,1,0:T(8,128)(2,1)S(1)} all-to-all(bf16[4,160,128]{2,1,0:T(8,128)(2,1)S(1)} %out_parts.1), channel_id=1, replica_groups={{0,192,384,576},{8,200,392,584},{16,208,400,592},{24,216,408,600},{32,2..., dimensions={0} | all-to-all | bytes 327680 | tf_op jit(solution)/shard_map/sum_out_x/all_to_all | solution.py:265
  81.0 0.0 copy-done.3
  81.0 0.0 copy-done.4
  81.0 0.1 hidden.1
  81.2 0.0 all-gather.7.cloned.1.call-done
  81.2 28.7 %all-gather.1 = bf16[3840,128]{1,0:T(8,128)(2,1)S(1)} all-gather(bf16[160,128]{1,0:T(8,128)(2,1)S(1)} %hidden.1), channel_id=3, replica_groups={{0,8,16,24,32,40,48,56,64,72,80,88,96,104,112,120,128,136,144,152,160,1..., dimensions={0}, use_global_device_ids=true | all-gather | bytes 1024000 | tf_op jit(solution)/shard_map/gather_pre/all_gather | solution.py:272
  109.9 0.0 copy-start.1
  109.9 1.4 copy-done.1
  111.3 1.4 pre_parts.1
  112.7 8.8 %all_to_all.21.got_ref = bf16[4,256,128]{2,1,0:T(8,128)(2,1)S(1)} all-to-all(bf16[4,256,128]{2,1,0:T(8,128)(2,1)S(1)} %get-tuple-element.25), channel_id=1, replica_groups={{0,192,384,576},{8,200,392,584},{16,208,400,592},{24,216,408,600},{32,2..., dimensions={0} | all-to-all | bytes 524288 | tf_op jit(solution)/shard_map/sum_pre_x/all_to_all | solution.py:283
  121.5 0.8 spread.1
  122.3 6.8 %all-to-all-start.3 = ((bf16[8,128,128]{2,1,0:T(8,128)(2,1)}), bf16[8,128,128]{2,1,0:T(8,128)(2,1)S(1)}, u32[]{:S(2)}, u32[]{:S(2)}) async-start(bf16[8,128,128]{2,1,0:T(8,128)(2,1)} %get-tuple-element.28), calls=%async_computation.3 | async-start | bytes 524288 | tf_op jit(solution)/shard_map/gather_spread/all_to_all | solution.py:293
  129.1 14.9 %all-gather.2 = bf16[3328,128]{1,0:T(8,128)(2,1)S(1)} all-gather(bf16[416,128]{1,0:T(8,128)(2,1)S(1)} %get-tuple-element.27), channel_id=4, replica_groups={{0,8,192,200,384,392,576,584},{16,24,208,216,400,408,592,600},{32,40,22..., dimensions={0}, use_global_device_ids=true | all-gather | bytes 958464 | tf_op jit(solution)/shard_map/gather_weights/all_gather | solution.py:295
  144.1 0.0 all-gather.9.cloned.1.call-done
  144.1 0.0 all-to-all-done.3.spread_ref
  144.1 0.0 copy-start.2
  144.1 1.2 copy-done.2
  145.3 1.3 final.1
Async XLA Ops:
  7.2 74.0 %all-gather.7.cloned.1.call-start = ((), (), s32[]{:S(2)}) async-start(), calls=%async_computation.4 | async-start | bytes 1703936 | tf_op jit(solution)/shard_map/gather_input/all_gather | solution.py:245
  12.1 57.9 %copy-start = (bf16[128,3072]{1,0:T(8,128)(2,1)S(1)}, bf16[128,3072]{1,0:T(8,128)(2,1)}, u32[]{:S(2)}) copy-start(bf16[128,3072]{1,0:T(8,128)(2,1)} %get-tuple-element.16.t0_ref) | copy-start | bytes 2359300
  12.1 57.9 %all-to-all-start = ((bf16[12,96,128]{2,1,0:T(8,128)(2,1)}), bf16[12,96,128]{2,1,0:T(8,128)(2,1)S(1)}, u32[]{:S(2)}, u32[]{:S(2)}) async-start(bf16[12,96,128]{2,1,0:T(8,128)(2,1)} %bitcast.14), calls=%async_computation | async-start | bytes 589824 | tf_op jit(solution)/shard_map/sum_weights_z/all_to_all | solution.py:252
  27.7 116.4 %all-gather.9.cloned.1.call-start = ((), (), s32[]{:S(2)}) async-start(), calls=%async_computation.5 | async-start | bytes 1179648 | tf_op jit(solution)/shard_map/gather_weight_in/all_gather | solution.py:247
  27.7 42.3 %collective-permute-start = (bf16[128,3072]{1,0:T(8,128)(2,1)}, bf16[128,3072]{1,0:T(8,128)(2,1)S(1)}, u32[]{:S(2)}, u32[]{:S(2)}) collective-permute-start(bf16[128,3072]{1,0:T(8,128)(2,1)} %get-tuple-element.17), channel_id=1, source_target_pairs={{0,192},{8,200},{16,208},{24,216},{32,224},{40,232},{48,240},{56,2... | collective-permute-start | bytes 2359304 | tf_op jit(solution)/shard_map/exchange_tiles/ppermute | solution.py:249
  31.1 38.9 %collective-permute-start.1 = (bf16[128,3072]{1,0:T(8,128)(2,1)}, bf16[128,3072]{1,0:T(8,128)(2,1)S(1)}, u32[]{:S(2)}, u32[]{:S(2)}) collective-permute-start(bf16[128,3072]{1,0:T(8,128)(2,1)} %get-tuple-element.18), channel_id=1, source_target_pairs={{0,384},{8,392},{16,400},{24,408},{32,416},{40,424},{48,432},{56,4... | collective-permute-start | bytes 2359304 | tf_op jit(solution)/shard_map/exchange_tiles/ppermute | solution.py:249
  35.9 34.1 %collective-permute-start.2 = (bf16[128,3072]{1,0:T(8,128)(2,1)}, bf16[128,3072]{1,0:T(8,128)(2,1)S(1)}, u32[]{:S(2)}, u32[]{:S(2)}) collective-permute-start(bf16[128,3072]{1,0:T(8,128)(2,1)} %get-tuple-element.19), channel_id=1, source_target_pairs={{0,576},{8,584},{16,592},{24,600},{32,608},{40,616},{48,624},{56,6... | collective-permute-start | bytes 2359304 | tf_op jit(solution)/shard_map/exchange_tiles/ppermute | solution.py:249
  70.0 11.0 %copy-start.3 = (bf16[128,128]{1,0:T(8,128)(2,1)S(1)}, bf16[128,128]{1,0:T(8,128)(2,1)}, u32[]{:S(2)}) copy-start(bf16[128,128]{1,0:T(8,128)(2,1)} %pre_hidden_ref.1) | copy-start | bytes 98308
  70.0 11.0 %copy-start.4 = (s32[128]{0:T(128)S(1)}, s32[128]{0:T(128)}, u32[]{:S(2)}) copy-start(s32[128]{0:T(128)} %param.19) | copy-start | bytes 1540
  109.9 1.4 copy-start.1
  122.3 21.7 %all-to-all-start.3 = ((bf16[8,128,128]{2,1,0:T(8,128)(2,1)}), bf16[8,128,128]{2,1,0:T(8,128)(2,1)S(1)}, u32[]{:S(2)}, u32[]{:S(2)}) async-start(bf16[8,128,128]{2,1,0:T(8,128)(2,1)} %get-tuple-element.28), calls=%async_computation.3 | async-start | bytes 524288 | tf_op jit(solution)/shard_map/gather_spread/all_to_all | solution.py:293
  144.1 1.2 copy-start.2
Sparse Core Ops, SparseCore 0:
  12.2 63.6 all-gather.6
  78.3 42.6 all-gather.8

commit v8 on v7

--- a/solution.py
+++ b/solution.py
@@ -140,7 +140,7 @@
     return [jnp.dot(tiles_ref[...], blocks, preferred_element_type=F32).astype(BF16) for tiles_ref in tiles_refs]
 
 
-def out_parts_kernel(me_ref, t0_ref, t1_ref, t2_ref, t3_ref, blocks_ref, weight_ref, out_ref):
+def out_parts_kernel(me_ref, t0_ref, t2_ref, t3_ref, t1_ref, blocks_ref, weight_ref, out_ref):
     parts = multiply((t0_ref, t1_ref, t2_ref, t3_ref), blocks_ref[...])
     total = weight_ref[0].astype(F32)
     for j in range(1, NZ):
@@ -164,7 +164,7 @@
     out_ref[TILE:] = total[TILE:].astype(BF16)
 
 
-def pre_parts_kernel(me_ref, t0_ref, t1_ref, t2_ref, t3_ref, blocks_ref, turned_ref, out_ref, weight_ref):
+def pre_parts_kernel(me_ref, t0_ref, t2_ref, t3_ref, t1_ref, blocks_ref, turned_ref, out_ref, weight_ref):
     blocks = blocks_ref[:, :TILE].reshape(WIDE, TILE)
     parts = multiply((t0_ref, t1_ref, t2_ref, t3_ref), blocks)
     for k in range(NX):
@@ -246,7 +246,8 @@
     with jax.named_scope("gather_weight_in"):
         weights_in = lax.all_gather(weight_in, "rep", axis=0, tiled=False)
     with jax.named_scope("exchange_tiles"):
-        tiles = [tiles[0]] + [lax.ppermute(tiles[k], "blk", along_x(k)) for k in range(1, NX)]
+        far, left, right = (lax.ppermute(tiles[k], "blk", along_x(k)) for k in (2, 3, 1))
+        tiles = [tiles[0], far, left, right]
     with jax.named_scope("sum_weights_z"):
         weights = weights.reshape(NZ, CHUNK, TILE)
         weights = lax.all_to_all(weights, "blk", 0, 0, tiled=True, axis_index_groups=Z_GROUPS)

time: 154 us -> 152 us (0.987)
    ppermute x3, starting transfers between devices: 11.1 us -> 9.19 us  [local(): lax.ppermute(tiles[k], 'blk', along_x(k))]
where the time goes in v8:
time: 152 us; the launch traced here: 151 us
  blocking collectives  91.1 us (60%)
  starting transfers between devices  32.8 us (22%)
  between operations  14.8 us (10%)
  Pallas kernels  10.1 us (7%)
  local copies, waits for them, and re-layouts  2.65 us (2%)
    all_gather x1, blocking collectives, local(): lax.all_gather(scaled, 'blk', axis=0, tiled=True, axis_index_groups=LINE_...  31.8 us
    all_gather x1, blocking collectives, local(): lax.all_gather(scaled, 'blk', axis=0, tiled=False, axis_index_groups=LINE...  27.8 us
    all_to_all x1, starting transfers between devices, local(): lax.all_to_all(weights, 'blk', 0, 0, tiled=True, axis_index_groups=Z_GROUPS)  17 us
    all_to_all x2, blocking collectives, local(): lax.all_to_all(parts, 'blk', 0, 0, tiled=True, axis_index_groups=X_GROUPS)  16.6 us
    all_gather x1, blocking collectives, local(): lax.all_gather(weights, 'blk', axis=0, tiled=False, axis_index_groups=SID...  14.9 us
    ppermute x3, starting transfers between devices, local(): lax.ppermute(tiles[k], 'blk', along_x(k))  9.19 us
    all_to_all x1, starting transfers between devices, local(): spread = lax.all_to_all(spread, 'rep', 0, 0, tiled=True)  6.48 us
    pallas_call x1, Pallas kernels, local(): call(start_kernel, [shape((TILE, WIDE), BF16)] * NX + [block, shape((NZ *...  4.32 us
  transfers between devices with their start and end apart: 7, of which 0 were waited for; matrix products, arithmetic and copies ran while one was open for 0% of the time, Pallas kernels for 3%

profile of v8, /device:TPU:1, one launch (start us, length us, event | category | flops | bytes accessed | tf_op | source)
XLA Modules:
  0.0 151.5 jit_solution(10652743424650871213)
XLA Ops:
  7.2 0.0 all-gather.7.cloned.1.call-start
  7.9 4.3 %start.1 = (bf16[128,3072]{1,0:T(8,128)(2,1)}, bf16[128,3072]{1,0:T(8,128)(2,1)}, bf16[128,3072]{1,0:T(8,128)(2,1)}, bf16[128,3072]{1,0:T(8,128)(2,1)}, bf16[128...) custom-call(s32[1]{0:T(128)} %bitcast.1.me_ref, s32[1]{0:T(128)S(6)} %copy.13.count_ref, ...), custom_call_target="tpu_custom_call" | custom-call | flops 67108864 | bytes 6000000 | tf_op jit(solution)/shard_map/start/pallas_call | solution.py:234
  12.2 0.0 copy-start
  12.2 0.0 all-gather.7.cloned.1.call-update
  12.2 17.0 %all-to-all-start = ((bf16[12,96,128]{2,1,0:T(8,128)(2,1)}), bf16[12,96,128]{2,1,0:T(8,128)(2,1)S(1)}, u32[]{:S(2)}, u32[]{:S(2)}) async-start(bf16[12,96,128]{2,1,0:T(8,128)(2,1)} %bitcast.14), calls=%async_computation | async-start | bytes 589824 | tf_op jit(solution)/shard_map/sum_weights_z/all_to_all | solution.py:253
  29.3 0.0 all-gather.9.cloned.1.call-start
  29.3 3.9 %collective-permute-start = (bf16[128,3072]{1,0:T(8,128)(2,1)}, bf16[128,3072]{1,0:T(8,128)(2,1)S(1)}, u32[]{:S(2)}, u32[]{:S(2)}) collective-permute-start(bf16[128,3072]{1,0:T(8,128)(2,1)} %get-tuple-element.17), channel_id=1, source_target_pairs={{0,384},{8,392},{16,400},{24,408},{32,416},{40,424},{48,432},{56,4... | collective-permute-start | bytes 2359304 | tf_op jit(solution)/shard_map/exchange_tiles/ppermute | solution.py:249
  33.2 2.9 %collective-permute-start.1 = (bf16[128,3072]{1,0:T(8,128)(2,1)}, bf16[128,3072]{1,0:T(8,128)(2,1)S(1)}, u32[]{:S(2)}, u32[]{:S(2)}) collective-permute-start(bf16[128,3072]{1,0:T(8,128)(2,1)} %get-tuple-element.18), channel_id=1, source_target_pairs={{0,576},{8,584},{16,592},{24,600},{32,608},{40,616},{48,624},{56,6... | collective-permute-start | bytes 2359304 | tf_op jit(solution)/shard_map/exchange_tiles/ppermute | solution.py:249
  36.1 2.4 %collective-permute-start.2 = (bf16[128,3072]{1,0:T(8,128)(2,1)}, bf16[128,3072]{1,0:T(8,128)(2,1)S(1)}, u32[]{:S(2)}, u32[]{:S(2)}) collective-permute-start(bf16[128,3072]{1,0:T(8,128)(2,1)} %get-tuple-element.19), channel_id=1, source_target_pairs={{0,192},{8,200},{16,208},{24,216},{32,224},{40,232},{48,240},{56,2... | collective-permute-start | bytes 2359304 | tf_op jit(solution)/shard_map/exchange_tiles/ppermute | solution.py:249
  38.5 0.0 all-gather.9.cloned.1.call-update
  38.5 31.8 %all_gather.27.blocks_ref = bf16[3072,128]{1,0:T(8,128)(2,1)} all-gather(bf16[128,128]{1,0:T(8,128)(2,1)} %get-tuple-element.20), channel_id=1, replica_groups={{0,8,16,24,32,40,48,56,64,72,80,88,96,104,112,120,128,136,144,152,160,1..., dimensions={0}, use_global_device_ids=true | all-gather | bytes 819200 | tf_op jit(solution)/shard_map/gather_out/all_gather | solution.py:255
  70.4 0.0 collective-permute-done.t2_ref
  70.4 0.0 collective-permute-done.1.t3_ref
  70.4 0.0 collective-permute-done.2.t1_ref
  70.4 0.0 all-to-all-done.weight_ref
  70.4 0.0 copy-done
  70.4 0.0 copy-start.3
  70.4 0.0 copy-start.4
  70.4 2.1 %out_parts.1 = bf16[4,160,128]{2,1,0:T(8,128)(2,1)S(1)} custom-call(s32[1]{0:T(128)} %bitcast.1.me_ref, bf16[128,3072]{1,0:T(8,128)(2,1)S(1)} %copy-done, bf16[128,3072]{1,0:T(8,128)(2,1)S(1)} %collective-permute-done.t2_ref, bf16[128,3072]{1,0:T(8,128)(2,1)S(1)} %collective-permute-done.1.t3_ref, bf16[128,3072]{1,0:T(8,128)(2,1)S(1)} %collective-permute-done.2.t1_ref, ...), custom_call_target="tpu_custom_call" | custom-call | flops 402653184 | bytes 4000000 | tf_op jit(solution)/shard_map/out_parts/pallas_call | solution.py:257
  72.6 7.4 %all_to_all.20.got_ref = bf16[4,160,128]{2,1,0:T(8,128)(2,1)S(1)} all-to-all(bf16[4,160,128]{2,1,0:T(8,128)(2,1)S(1)} %out_parts.1), channel_id=1, replica_groups={{0,192,384,576},{8,200,392,584},{16,208,400,592},{24,216,408,600},{32,2..., dimensions={0} | all-to-all | bytes 327680 | tf_op jit(solution)/shard_map/sum_out_x/all_to_all | solution.py:266
  80.0 0.0 copy-done.3
  80.0 0.0 copy-done.4
  80.0 0.1 hidden.1
  80.1 0.0 all-gather.7.cloned.1.call-done
  80.2 27.8 %all-gather.1 = bf16[3840,128]{1,0:T(8,128)(2,1)S(1)} all-gather(bf16[160,128]{1,0:T(8,128)(2,1)S(1)} %hidden.1), channel_id=3, replica_groups={{0,8,16,24,32,40,48,56,64,72,80,88,96,104,112,120,128,136,144,152,160,1..., dimensions={0}, use_global_device_ids=true | all-gather | bytes 1024000 | tf_op jit(solution)/shard_map/gather_pre/all_gather | solution.py:273
  108.0 0.0 copy-start.1
  108.0 1.4 copy-done.1
  109.4 1.4 pre_parts.1
  110.8 9.2 %all_to_all.21.got_ref = bf16[4,256,128]{2,1,0:T(8,128)(2,1)S(1)} all-to-all(bf16[4,256,128]{2,1,0:T(8,128)(2,1)S(1)} %get-tuple-element.25), channel_id=1, replica_groups={{0,192,384,576},{8,200,392,584},{16,208,400,592},{24,216,408,600},{32,2..., dimensions={0} | all-to-all | bytes 524288 | tf_op jit(solution)/shard_map/sum_pre_x/all_to_all | solution.py:284
  119.9 0.8 spread.1
  120.8 6.5 %all-to-all-start.3 = ((bf16[8,128,128]{2,1,0:T(8,128)(2,1)}), bf16[8,128,128]{2,1,0:T(8,128)(2,1)S(1)}, u32[]{:S(2)}, u32[]{:S(2)}) async-start(bf16[8,128,128]{2,1,0:T(8,128)(2,1)} %get-tuple-element.28), calls=%async_computation.3 | async-start | bytes 524288 | tf_op jit(solution)/shard_map/gather_spread/all_to_all | solution.py:294
  127.2 14.9 %all-gather.2 = bf16[3328,128]{1,0:T(8,128)(2,1)S(1)} all-gather(bf16[416,128]{1,0:T(8,128)(2,1)S(1)} %get-tuple-element.27), channel_id=4, replica_groups={{0,8,192,200,384,392,576,584},{16,24,208,216,400,408,592,600},{32,40,22..., dimensions={0}, use_global_device_ids=true | all-gather | bytes 958464 | tf_op jit(solution)/shard_map/gather_weights/all_gather | solution.py:296
  142.1 0.0 all-gather.9.cloned.1.call-done
  142.1 0.0 all-to-all-done.3.spread_ref
  142.1 0.0 copy-start.2
  142.1 1.2 copy-done.2
  143.3 1.3 final.1
Async XLA Ops:
  7.2 73.0 %all-gather.7.cloned.1.call-start = ((), (), s32[]{:S(2)}) async-start(), calls=%async_computation.4 | async-start | bytes 1703936 | tf_op jit(solution)/shard_map/gather_input/all_gather | solution.py:245
  12.2 58.2 %copy-start = (bf16[128,3072]{1,0:T(8,128)(2,1)S(1)}, bf16[128,3072]{1,0:T(8,128)(2,1)}, u32[]{:S(2)}) copy-start(bf16[128,3072]{1,0:T(8,128)(2,1)} %get-tuple-element.16.t0_ref) | copy-start | bytes 2359300
  12.2 58.2 %all-to-all-start = ((bf16[12,96,128]{2,1,0:T(8,128)(2,1)}), bf16[12,96,128]{2,1,0:T(8,128)(2,1)S(1)}, u32[]{:S(2)}, u32[]{:S(2)}) async-start(bf16[12,96,128]{2,1,0:T(8,128)(2,1)} %bitcast.14), calls=%async_computation | async-start | bytes 589824 | tf_op jit(solution)/shard_map/sum_weights_z/all_to_all | solution.py:253
  29.3 112.9 %all-gather.9.cloned.1.call-start = ((), (), s32[]{:S(2)}) async-start(), calls=%async_computation.5 | async-start | bytes 1179648 | tf_op jit(solution)/shard_map/gather_weight_in/all_gather | solution.py:247
  29.3 41.1 %collective-permute-start = (bf16[128,3072]{1,0:T(8,128)(2,1)}, bf16[128,3072]{1,0:T(8,128)(2,1)S(1)}, u32[]{:S(2)}, u32[]{:S(2)}) collective-permute-start(bf16[128,3072]{1,0:T(8,128)(2,1)} %get-tuple-element.17), channel_id=1, source_target_pairs={{0,384},{8,392},{16,400},{24,408},{32,416},{40,424},{48,432},{56,4... | collective-permute-start | bytes 2359304 | tf_op jit(solution)/shard_map/exchange_tiles/ppermute | solution.py:249
  33.2 37.2 %collective-permute-start.1 = (bf16[128,3072]{1,0:T(8,128)(2,1)}, bf16[128,3072]{1,0:T(8,128)(2,1)S(1)}, u32[]{:S(2)}, u32[]{:S(2)}) collective-permute-start(bf16[128,3072]{1,0:T(8,128)(2,1)} %get-tuple-element.18), channel_id=1, source_target_pairs={{0,576},{8,584},{16,592},{24,600},{32,608},{40,616},{48,624},{56,6... | collective-permute-start | bytes 2359304 | tf_op jit(solution)/shard_map/exchange_tiles/ppermute | solution.py:249
  36.1 34.3 %collective-permute-start.2 = (bf16[128,3072]{1,0:T(8,128)(2,1)}, bf16[128,3072]{1,0:T(8,128)(2,1)S(1)}, u32[]{:S(2)}, u32[]{:S(2)}) collective-permute-start(bf16[128,3072]{1,0:T(8,128)(2,1)} %get-tuple-element.19), channel_id=1, source_target_pairs={{0,192},{8,200},{16,208},{24,216},{32,224},{40,232},{48,240},{56,2... | collective-permute-start | bytes 2359304 | tf_op jit(solution)/shard_map/exchange_tiles/ppermute | solution.py:249
  70.4 9.6 %copy-start.3 = (bf16[128,128]{1,0:T(8,128)(2,1)S(1)}, bf16[128,128]{1,0:T(8,128)(2,1)}, u32[]{:S(2)}) copy-start(bf16[128,128]{1,0:T(8,128)(2,1)} %pre_hidden_ref.1) | copy-start | bytes 98308
  70.4 9.6 %copy-start.4 = (s32[128]{0:T(128)S(1)}, s32[128]{0:T(128)}, u32[]{:S(2)}) copy-start(s32[128]{0:T(128)} %param.19) | copy-start | bytes 1540
  108.0 1.4 copy-start.1
  120.8 21.3 %all-to-all-start.3 = ((bf16[8,128,128]{2,1,0:T(8,128)(2,1)}), bf16[8,128,128]{2,1,0:T(8,128)(2,1)S(1)}, u32[]{:S(2)}, u32[]{:S(2)}) async-start(bf16[8,128,128]{2,1,0:T(8,128)(2,1)} %get-tuple-element.28), calls=%async_computation.3 | async-start | bytes 524288 | tf_op jit(solution)/shard_map/gather_spread/all_to_all | solution.py:294
  142.1 1.2 copy-start.2
Sparse Core Ops, SparseCore 0:
  12.4 62.9 all-gather.6
  77.7 42.9 all-gather.8

commit v9 on v8

--- a/solution.py
+++ b/solution.py
@@ -164,7 +164,14 @@
     out_ref[TILE:] = total[TILE:].astype(BF16)
 
 
-def pre_parts_kernel(me_ref, t0_ref, t2_ref, t3_ref, t1_ref, blocks_ref, turned_ref, out_ref, weight_ref):
+def pre_parts_kernel(
+    me_ref, t0_ref, t2_ref, t3_ref, t1_ref, blocks_ref, turned_hbm, out_ref, weight_ref, turned_ref, sems
+):
+    copies = []
+    for i in range(NZ // 2):
+        part = pl.ds(2 * i, 2)
+        copies.append(pltpu.make_async_copy(turned_hbm.at[part], turned_ref.at[part], sems.at[i]))
+        copies[-1].start()
     blocks = blocks_ref[:, :TILE].reshape(WIDE, TILE)
     parts = multiply((t0_ref, t1_ref, t2_ref, t3_ref), blocks)
     for k in range(NX):
@@ -177,6 +184,7 @@
     core = me_ref[0] & 1
     w_in = jnp.zeros((4 * TILE, TILE), F32)
     for z in range(0, NZ, 2):
+        copies[z // 2].wait()
         turned = jnp.concatenate([turned_ref[z], turned_ref[z + 1]], axis=1)
         mine = jnp.concatenate([blocks_ref[2 * (z + i) + core, :TILE] for i in range(2)], axis=0)
         w_in = w_in + jnp.dot(turned, mine, preferred_element_type=F32)
@@ -268,17 +276,17 @@
         scaled = call(hidden_kernel, shape((TILE + ROOM, TILE), BF16), [vmem()] * 3, 1000000, 600000)(
             degree, parts, pre_hidden
         )
-    scaled, turned = lax.optimization_barrier((scaled, turned))
     with jax.named_scope("gather_pre"):
         blocks = lax.all_gather(scaled, "blk", axis=0, tiled=False, axis_index_groups=LINE_GROUPS)
     with jax.named_scope("pre_parts"):
         parts, w_out = call(
             pre_parts_kernel,
             [shape((NX, 2 * TILE, TILE), BF16), shape((NZ * PIECE, TILE), BF16)],
-            [smem()] + [vmem()] * 6,
+            [smem()] + [vmem()] * 5 + [hbm()],
             4 * 512 * 3072 * 128,
             8000000,
-            limit=44,
+            scratch=[pltpu.VMEM((NZ, 4 * TILE, TILE), BF16), pltpu.SemaphoreType.DMA((NZ // 2,))],
+            limit=50,
         )(me, *tiles, blocks, turned)
     with jax.named_scope("sum_pre_x"):
         parts = lax.all_to_all(parts, "blk", 0, 0, tiled=True, axis_index_groups=X_GROUPS)

time: 152 us -> 156 us (1.026)
  Pallas kernels: 10.1 us -> 13.7 us
  blocking collectives: 91.1 us -> 92.8 us
    pallas_call x1, Pallas kernels: 1.38 us -> 4.35 us  [local(): call(pre_parts_kernel, [shape((NX, 2 * TILE, TILE), BF16), shape((NZ * PI...]
    all_to_all x1, starting transfers between devices: 17 us -> 14.9 us  [local(): lax.all_to_all(weights, 'blk', 0, 0, tiled=True, axis_index_groups=Z_GROUPS)]
  transfers between devices with their start and end apart: 7 -> 7, of which waited for: 0 -> 0; matrix products, arithmetic and copies ran while one was open for 0% -> 0% of each run, Pallas kernels for 3% -> 5%
where the time goes in v9:
time: 156 us; the launch traced here: 155 us
  blocking collectives  92.8 us (59%)
  starting transfers between devices  32.4 us (21%)
  between operations  14.8 us (9%)
  Pallas kernels  13.7 us (9%)
    all_gather x1, blocking collectives, local(): lax.all_gather(scaled, 'blk', axis=0, tiled=True, axis_index_groups=LINE_...  31 us
    all_gather x1, blocking collectives, local(): lax.all_gather(scaled, 'blk', axis=0, tiled=False, axis_index_groups=LINE...  29.1 us
    all_to_all x2, blocking collectives, local(): lax.all_to_all(parts, 'blk', 0, 0, tiled=True, axis_index_groups=X_GROUPS)  17.8 us
    all_gather x1, blocking collectives, local(): lax.all_gather(weights, 'blk', axis=0, tiled=False, axis_index_groups=SID...  14.9 us
    all_to_all x1, starting transfers between devices, local(): lax.all_to_all(weights, 'blk', 0, 0, tiled=True, axis_index_groups=Z_GROUPS)  14.9 us
    ppermute x3, starting transfers between devices, local(): lax.ppermute(tiles[k], 'blk', along_x(k))  10.6 us
    all_to_all x1, starting transfers between devices, local(): spread = lax.all_to_all(spread, 'rep', 0, 0, tiled=True)  6.81 us
    pallas_call x1, Pallas kernels, local(): call(start_kernel, [shape((TILE, WIDE), BF16)] * NX + [block, shape((NZ *...  5.01 us
  transfers between devices with their start and end apart: 7, of which 0 were waited for; matrix products, arithmetic and copies ran while one was open for 0% of the time, Pallas kernels for 5%

profile of v9, /device:TPU:1, one launch (start us, length us, event | category | flops | bytes accessed | tf_op | source)
XLA Modules:
  0.0 155.0 jit_solution(15997487182307478075)
XLA Ops:
  7.2 0.0 all-gather.7.cloned.1.call-start
  7.9 5.0 %start.1 = (bf16[128,3072]{1,0:T(8,128)(2,1)}, bf16[128,3072]{1,0:T(8,128)(2,1)}, bf16[128,3072]{1,0:T(8,128)(2,1)}, bf16[128,3072]{1,0:T(8,128)(2,1)}, bf16[128...) custom-call(s32[1]{0:T(128)} %bitcast.1.me_ref, s32[1]{0:T(128)S(6)} %copy.13.count_ref, ...), custom_call_target="tpu_custom_call" | custom-call | flops 67108864 | bytes 6000000 | tf_op jit(solution)/shard_map/start/pallas_call | solution.py:242
  12.9 0.0 copy-start
  12.9 0.0 all-gather.7.cloned.1.call-update
  12.9 14.9 %all-to-all-start = ((bf16[12,96,128]{2,1,0:T(8,128)(2,1)}), bf16[12,96,128]{2,1,0:T(8,128)(2,1)S(1)}, u32[]{:S(2)}, u32[]{:S(2)}) async-start(bf16[12,96,128]{2,1,0:T(8,128)(2,1)} %bitcast.14), calls=%async_computation | async-start | bytes 589824 | tf_op jit(solution)/shard_map/sum_weights_z/all_to_all | solution.py:261
  27.9 0.0 all-gather.9.cloned.1.call-start
  27.9 5.3 %collective-permute-start = (bf16[128,3072]{1,0:T(8,128)(2,1)}, bf16[128,3072]{1,0:T(8,128)(2,1)S(1)}, u32[]{:S(2)}, u32[]{:S(2)}) collective-permute-start(bf16[128,3072]{1,0:T(8,128)(2,1)} %get-tuple-element.15), channel_id=1, source_target_pairs={{0,384},{8,392},{16,400},{24,408},{32,416},{40,424},{48,432},{56,4... | collective-permute-start | bytes 2359304 | tf_op jit(solution)/shard_map/exchange_tiles/ppermute | solution.py:257
  33.2 2.1 %collective-permute-start.1 = (bf16[128,3072]{1,0:T(8,128)(2,1)}, bf16[128,3072]{1,0:T(8,128)(2,1)S(1)}, u32[]{:S(2)}, u32[]{:S(2)}) collective-permute-start(bf16[128,3072]{1,0:T(8,128)(2,1)} %get-tuple-element.16), channel_id=1, source_target_pairs={{0,576},{8,584},{16,592},{24,600},{32,608},{40,616},{48,624},{56,6... | collective-permute-start | bytes 2359304 | tf_op jit(solution)/shard_map/exchange_tiles/ppermute | solution.py:257
  35.3 3.1 %collective-permute-start.2 = (bf16[128,3072]{1,0:T(8,128)(2,1)}, bf16[128,3072]{1,0:T(8,128)(2,1)S(1)}, u32[]{:S(2)}, u32[]{:S(2)}) collective-permute-start(bf16[128,3072]{1,0:T(8,128)(2,1)} %get-tuple-element.17), channel_id=1, source_target_pairs={{0,192},{8,200},{16,208},{24,216},{32,224},{40,232},{48,240},{56,2... | collective-permute-start | bytes 2359304 | tf_op jit(solution)/shard_map/exchange_tiles/ppermute | solution.py:257
  38.5 0.0 all-gather.9.cloned.1.call-update
  38.5 31.0 %all_gather.27.blocks_ref = bf16[3072,128]{1,0:T(8,128)(2,1)} all-gather(bf16[128,128]{1,0:T(8,128)(2,1)} %get-tuple-element.18), channel_id=1, replica_groups={{0,8,16,24,32,40,48,56,64,72,80,88,96,104,112,120,128,136,144,152,160,1..., dimensions={0}, use_global_device_ids=true | all-gather | bytes 819200 | tf_op jit(solution)/shard_map/gather_out/all_gather | solution.py:263
  69.5 0.0 collective-permute-done.t2_ref
  69.5 0.0 collective-permute-done.1.t3_ref
  69.5 0.0 collective-permute-done.2.t1_ref
  69.6 0.0 all-to-all-done.weight_ref
  69.6 0.0 copy-done
  69.6 0.0 copy-start.2
  69.6 0.0 copy-start.3
  69.6 2.1 %out_parts.1 = bf16[4,160,128]{2,1,0:T(8,128)(2,1)S(1)} custom-call(s32[1]{0:T(128)} %bitcast.1.me_ref, bf16[128,3072]{1,0:T(8,128)(2,1)S(1)} %copy-done, bf16[128,3072]{1,0:T(8,128)(2,1)S(1)} %collective-permute-done.t2_ref, bf16[128,3072]{1,0:T(8,128)(2,1)S(1)} %collective-permute-done.1.t3_ref, bf16[128,3072]{1,0:T(8,128)(2,1)S(1)} %collective-permute-done.2.t1_ref, ...), custom_call_target="tpu_custom_call" | custom-call | flops 402653184 | bytes 4000000 | tf_op jit(solution)/shard_map/out_parts/pallas_call | solution.py:265
  71.7 9.0 %all_to_all.20.got_ref = bf16[4,160,128]{2,1,0:T(8,128)(2,1)S(1)} all-to-all(bf16[4,160,128]{2,1,0:T(8,128)(2,1)S(1)} %out_parts.1), channel_id=1, replica_groups={{0,192,384,576},{8,200,392,584},{16,208,400,592},{24,216,408,600},{32,2..., dimensions={0} | all-to-all | bytes 327680 | tf_op jit(solution)/shard_map/sum_out_x/all_to_all | solution.py:274
  80.7 0.0 copy-done.2
  80.7 0.0 copy-done.3
  80.7 0.1 hidden.1
  80.9 29.1 %all-gather = bf16[3840,128]{1,0:T(8,128)(2,1)} all-gather(bf16[160,128]{1,0:T(8,128)(2,1)S(1)} %hidden.1), channel_id=2, replica_groups={{0,8,16,24,32,40,48,56,64,72,80,88,96,104,112,120,128,136,144,152,160,1..., dimensions={0}, use_global_device_ids=true | all-gather | bytes 1024000 | tf_op jit(solution)/shard_map/gather_pre/all_gather | solution.py:280
  109.9 0.0 all-gather.7.cloned.1.call-done
  110.0 4.3 %pre_parts.1 = (bf16[4,256,128]{2,1,0:T(8,128)(2,1)S(1)}, bf16[288,128]{1,0:T(8,128)(2,1)S(1)}) custom-call(s32[1]{0:T(128)} %bitcast.1.me_ref, bf16[128,3072]{1,0:T(8,128)(2,1)S(1)} %copy-done, bf16[128,3072]{1,0:T(8,128)(2,1)S(1)} %collective-permute-done.t2_ref, bf16[128,3072]{1,0:T(8,128)(2,1)S(1)} %collective-permute-done.1.t3_ref, ...), custom_call_target="tpu_custom_call" | custom-call | flops 805306368 | bytes 8000000 | tf_op jit(solution)/shard_map/pre_parts/pallas_call | solution.py:282
  114.3 8.8 %all_to_all.21.got_ref = bf16[4,256,128]{2,1,0:T(8,128)(2,1)S(1)} all-to-all(bf16[4,256,128]{2,1,0:T(8,128)(2,1)S(1)} %get-tuple-element.21), channel_id=1, replica_groups={{0,192,384,576},{8,200,392,584},{16,208,400,592},{24,216,408,600},{32,2..., dimensions={0} | all-to-all | bytes 524288 | tf_op jit(solution)/shard_map/sum_pre_x/all_to_all | solution.py:292
  123.1 0.8 spread.1
  123.9 6.8 %all-to-all-start.3 = ((bf16[8,128,128]{2,1,0:T(8,128)(2,1)}), bf16[8,128,128]{2,1,0:T(8,128)(2,1)S(1)}, u32[]{:S(2)}, u32[]{:S(2)}) async-start(bf16[8,128,128]{2,1,0:T(8,128)(2,1)} %get-tuple-element.24), calls=%async_computation.3 | async-start | bytes 524288 | tf_op jit(solution)/shard_map/gather_spread/all_to_all | solution.py:302
  130.7 14.9 %all-gather.2 = bf16[3328,128]{1,0:T(8,128)(2,1)S(1)} all-gather(bf16[416,128]{1,0:T(8,128)(2,1)S(1)} %get-tuple-element.23), channel_id=4, replica_groups={{0,8,192,200,384,392,576,584},{16,24,208,216,400,408,592,600},{32,40,22..., dimensions={0}, use_global_device_ids=true | all-gather | bytes 958464 | tf_op jit(solution)/shard_map/gather_weights/all_gather | solution.py:304
  145.7 0.0 all-gather.9.cloned.1.call-done
  145.7 0.0 all-to-all-done.3.spread_ref
  145.7 0.0 copy-start.1
  145.7 1.2 copy-done.1
  146.9 1.3 final.1
Async XLA Ops:
  7.2 102.8 %all-gather.7.cloned.1.call-start = ((), (), s32[]{:S(2)}) async-start(), calls=%async_computation.4 | async-start | bytes 1703936 | tf_op jit(solution)/shard_map/gather_input/all_gather | solution.py:253
  12.9 56.7 %copy-start = (bf16[128,3072]{1,0:T(8,128)(2,1)S(1)}, bf16[128,3072]{1,0:T(8,128)(2,1)}, u32[]{:S(2)}) copy-start(bf16[128,3072]{1,0:T(8,128)(2,1)} %get-tuple-element.14.t0_ref) | copy-start | bytes 2359300
  12.9 56.6 %all-to-all-start = ((bf16[12,96,128]{2,1,0:T(8,128)(2,1)}), bf16[12,96,128]{2,1,0:T(8,128)(2,1)S(1)}, u32[]{:S(2)}, u32[]{:S(2)}) async-start(bf16[12,96,128]{2,1,0:T(8,128)(2,1)} %bitcast.14), calls=%async_computation | async-start | bytes 589824 | tf_op jit(solution)/shard_map/sum_weights_z/all_to_all | solution.py:261
  27.9 117.8 %all-gather.9.cloned.1.call-start = ((), (), s32[]{:S(2)}) async-start(), calls=%async_computation.5 | async-start | bytes 1179648 | tf_op jit(solution)/shard_map/gather_weight_in/all_gather | solution.py:255
  27.9 41.6 %collective-permute-start = (bf16[128,3072]{1,0:T(8,128)(2,1)}, bf16[128,3072]{1,0:T(8,128)(2,1)S(1)}, u32[]{:S(2)}, u32[]{:S(2)}) collective-permute-start(bf16[128,3072]{1,0:T(8,128)(2,1)} %get-tuple-element.15), channel_id=1, source_target_pairs={{0,384},{8,392},{16,400},{24,408},{32,416},{40,424},{48,432},{56,4... | collective-permute-start | bytes 2359304 | tf_op jit(solution)/shard_map/exchange_tiles/ppermute | solution.py:257
  33.2 36.3 %collective-permute-start.1 = (bf16[128,3072]{1,0:T(8,128)(2,1)}, bf16[128,3072]{1,0:T(8,128)(2,1)S(1)}, u32[]{:S(2)}, u32[]{:S(2)}) collective-permute-start(bf16[128,3072]{1,0:T(8,128)(2,1)} %get-tuple-element.16), channel_id=1, source_target_pairs={{0,576},{8,584},{16,592},{24,600},{32,608},{40,616},{48,624},{56,6... | collective-permute-start | bytes 2359304 | tf_op jit(solution)/shard_map/exchange_tiles/ppermute | solution.py:257
  35.3 34.2 %collective-permute-start.2 = (bf16[128,3072]{1,0:T(8,128)(2,1)}, bf16[128,3072]{1,0:T(8,128)(2,1)S(1)}, u32[]{:S(2)}, u32[]{:S(2)}) collective-permute-start(bf16[128,3072]{1,0:T(8,128)(2,1)} %get-tuple-element.17), channel_id=1, source_target_pairs={{0,192},{8,200},{16,208},{24,216},{32,224},{40,232},{48,240},{56,2... | collective-permute-start | bytes 2359304 | tf_op jit(solution)/shard_map/exchange_tiles/ppermute | solution.py:257
  69.6 11.2 %copy-start.2 = (bf16[128,128]{1,0:T(8,128)(2,1)S(1)}, bf16[128,128]{1,0:T(8,128)(2,1)}, u32[]{:S(2)}) copy-start(bf16[128,128]{1,0:T(8,128)(2,1)} %pre_hidden_ref.1) | copy-start | bytes 98308
  69.6 11.1 %copy-start.3 = (s32[128]{0:T(128)S(1)}, s32[128]{0:T(128)}, u32[]{:S(2)}) copy-start(s32[128]{0:T(128)} %param.19) | copy-start | bytes 1540
  123.9 21.7 %all-to-all-start.3 = ((bf16[8,128,128]{2,1,0:T(8,128)(2,1)}), bf16[8,128,128]{2,1,0:T(8,128)(2,1)S(1)}, u32[]{:S(2)}, u32[]{:S(2)}) async-start(bf16[8,128,128]{2,1,0:T(8,128)(2,1)} %get-tuple-element.24), calls=%async_computation.3 | async-start | bytes 524288 | tf_op jit(solution)/shard_map/gather_spread/all_to_all | solution.py:302
  145.7 1.2 copy-start.1
Sparse Core Ops, SparseCore 0:
  13.0 61.6 all-gather.6
  77.1 42.7 all-gather.8
